TPU v7x, 32 devices: a whole 2x2x4 slice. The times are simulated.
32 devices in a mesh: cells: 8 (over z, x), chrom: 4 (over y, core).
Axes of the slice: x: 2, y: 2, z: 4, core: 2. Of those that a mesh axis runs over, the one named last changes fastest.
Arguments:
- tokens: bfloat16 [24, 1024, 1280], P('cells', 'chrom'), may hold values from -6 to 6
- cotangent: bfloat16 [24, 1024, 1280], P('cells', 'chrom'), may hold values from -6 to 6
- block_lengths: int32 [24, 8], P('cells'), may hold values from 1 to 128, 768 in all within a row
- group_ids: int32 [24], P('cells'), may hold values from 0 to 3
- group_weights: float32 [4], replicated, may hold values from 0.5 to 2
- first_gain: float32 [1280], replicated, may hold values from 0.5 to 1.5
- first_shift: float32 [1280], replicated, may hold values from -3 to 3
- query_weight: bfloat16 [1280, 1280], replicated, may hold values from -0.15625 to 0.15625
- key_weight: bfloat16 [1280, 1280], replicated, may hold values from -0.15625 to 0.15625
- value_weight: bfloat16 [1280, 1280], replicated, may hold values from -0.15625 to 0.15625
- output_weight: bfloat16 [1280, 1280], replicated, may hold values from -2.5 to 2.5
- second_gain: float32 [1280], replicated, may hold values from 0.5 to 1.5
- second_shift: float32 [1280], replicated, may hold values from -3 to 3
- up_weight: bfloat16 [1280, 5120], replicated, may hold values from -0.15625 to 0.15625
- down_weight: bfloat16 [5120, 1280], replicated, may hold values from -0.078125 to 0.078125
Outputs:
- layer_out: bfloat16 [24, 1024, 1280], P('cells', 'chrom')
- tokens_grad: float32 [24, 1024, 1280], P('cells', 'chrom')
- first_gain_grad: float32 [1280], P(('cells', 'chrom'))
- first_shift_grad: float32 [1280], P(('cells', 'chrom'))
- query_grad: float32 [1280, 1280], P(('cells', 'chrom'))
- key_grad: float32 [1280, 1280], P(('cells', 'chrom'))
- value_grad: float32 [1280, 1280], P(('cells', 'chrom'))
- output_grad: float32 [1280, 1280], P(('cells', 'chrom'))
- second_gain_grad: float32 [1280], P(('cells', 'chrom'))
- second_shift_grad: float32 [1280], P(('cells', 'chrom'))
- up_grad: float32 [1280, 5120], P(('cells', 'chrom'))
- down_grad: float32 [5120, 1280], P(('cells', 'chrom'))
- cls_mean: float32 [1280], replicated
- cls_var: float32 [1280], replicated
Inputs may be any that keep to these rules, and one draw needn't show every extreme that they name: `block_lengths`: each row sums to 768 and its largest entry is 128.
All inputs are finite; a program needn't handle non-finite values.
Results may differ from a plain program's by a relative error of at most 0.025.
Values may be sent and summed in bfloat16 or wider, within the bound.
A program may use at most 384 MiB of HBM per device.

v0:
```python
import jax
import jax.numpy as jnp
from jax import lax
from jax.sharding import PartitionSpec as P

HEAD_DIM = 64


EPS = 1e-05
ROOT_HALF = 0.7071067811865476
DENSITY_SCALE = 0.3989422804014327


def norm_rows(values, gain, shift):
    center = values - jnp.mean(values, axis=-1, keepdims=True)
    inverse = lax.rsqrt(jnp.mean(center * center, axis=-1, keepdims=True) + EPS)
    normed = center * inverse
    return (normed * gain + shift, normed, inverse)


def norm_back(grad_out, normed, inverse, gain):
    scaled = grad_out * gain
    grad_in = inverse * (
        scaled
        - jnp.mean(scaled, axis=-1, keepdims=True)
        - normed * jnp.mean(scaled * normed, axis=-1, keepdims=True)
    )
    return (grad_in, jnp.sum(grad_out * normed, axis=0), jnp.sum(grad_out, axis=0))


def gelu_slope(upper):
    cumulative = 0.5 * (1.0 + lax.erf(upper * ROOT_HALF))
    density = jnp.exp(-0.5 * upper * upper) * DENSITY_SCALE
    return cumulative + upper * density


def contract(left, right):
    return jnp.einsum("rd,re->de", left, right, preferred_element_type=jnp.float32)


def back_through(grad, weight):
    return jnp.einsum("re,de->rd", grad, weight, preferred_element_type=jnp.float32)


def masked_scores(query, keys, valid, scale):
    scores = jnp.einsum("cqhe,ckhe->chqk", query, keys, preferred_element_type=jnp.float32) * scale
    return jnp.where(valid[:, None, None, :], scores, -1e30)


def attend(query, keys, values, valid, scale):
    scores = masked_scores(query, keys, valid, scale)
    top = jnp.max(scores, axis=-1, keepdims=True)
    expo = jnp.exp(scores - top)
    total = jnp.sum(expo, axis=-1, keepdims=True)
    probs = (expo / total).astype(jnp.bfloat16)
    mixed = jnp.einsum("chqk,ckhe->cqhe", probs, values, preferred_element_type=jnp.float32)
    return (mixed.astype(jnp.bfloat16), top + jnp.log(total))


def attend_back(query, keys, values, valid, logsum, mixed_grad, scale):
    scores = masked_scores(query, keys, valid, scale)
    probs = jnp.exp(scores - logsum)
    prob_grad = jnp.einsum(
        "cqhe,ckhe->chqk", mixed_grad, values, preferred_element_type=jnp.float32
    )
    inner = jnp.sum(probs * prob_grad, axis=-1, keepdims=True)
    score_grad = (probs * (prob_grad - inner)).astype(jnp.bfloat16)
    query_part = (
        jnp.einsum("chqk,ckhe->cqhe", score_grad, keys, preferred_element_type=jnp.float32) * scale
    )
    return (query_part.astype(jnp.bfloat16), probs.astype(jnp.bfloat16), score_grad, inner)


def per_device(
    tokens,
    cotangent,
    block_lengths,
    group_ids,
    group_weights,
    first_gain,
    first_shift,
    query_weight,
    key_weight,
    value_weight,
    output_weight,
    second_gain,
    second_shift,
    up_weight,
    down_weight,
):
    cells_here, seq_here, width = tokens.shape
    heads = width // HEAD_DIM
    rows = cells_here * seq_here
    seq_full = seq_here * lax.axis_size("chrom")
    nblocks = block_lengths.shape[1]
    block = seq_full // nblocks
    scale = HEAD_DIM ** (-0.5)
    valid = (jnp.arange(block)[None, None, :] < block_lengths[:, :, None]).reshape(
        cells_here, seq_full
    )
    start = lax.axis_index("chrom") * seq_here
    local_valid = lax.dynamic_slice_in_dim(valid, start, seq_here, 1)
    n_groups = group_weights.shape[0]
    cell_scale = jnp.sum(
        jnp.where(group_ids[:, None] == jnp.arange(n_groups)[None, :], group_weights[None, :], 0.0),
        axis=1,
    )
    flat = tokens.reshape(rows, width).astype(jnp.float32)
    first_out, first_norm, first_inv = norm_rows(flat, first_gain, first_shift)
    first_low = first_out.astype(jnp.bfloat16)
    query_low = jnp.dot(first_low, query_weight, preferred_element_type=jnp.float32).astype(
        jnp.bfloat16
    )
    key_low = jnp.dot(first_low, key_weight, preferred_element_type=jnp.float32).astype(
        jnp.bfloat16
    )
    value_low = jnp.dot(first_low, value_weight, preferred_element_type=jnp.float32).astype(
        jnp.bfloat16
    )
    keys_all, values_all = (
        lax.all_gather(key_low.reshape(cells_here, seq_here, width), "chrom", axis=1, tiled=True),
        lax.all_gather(value_low.reshape(cells_here, seq_here, width), "chrom", axis=1, tiled=True),
    )
    query_heads = query_low.reshape(cells_here, seq_here, heads, HEAD_DIM)
    mixed, logsum = attend(
        query_heads,
        keys_all.reshape(cells_here, seq_full, heads, HEAD_DIM),
        values_all.reshape(cells_here, seq_full, heads, HEAD_DIM),
        valid,
        scale,
    )
    mixed_flat = mixed.reshape(rows, width)
    middle = flat + jnp.dot(mixed_flat, output_weight, preferred_element_type=jnp.float32)
    second_out, second_norm, second_inv = norm_rows(middle, second_gain, second_shift)
    second_low = second_out.astype(jnp.bfloat16)
    upper = jnp.dot(second_low, up_weight, preferred_element_type=jnp.float32)
    active = jax.nn.gelu(upper, approximate=False).astype(jnp.bfloat16)
    result = middle + jnp.dot(active, down_weight, preferred_element_type=jnp.float32)
    result_cells = result.reshape(cells_here, seq_here, width)
    layer_out = result_cells.astype(jnp.bfloat16)
    owner = lax.axis_index("chrom") == 0
    cls_rows = jnp.where(owner, result_cells[:, 0, :], 0.0)
    cls_total, cls_square = lax.psum(
        (jnp.sum(cls_rows, axis=0), jnp.sum(cls_rows * cls_rows, axis=0)), ("cells", "chrom")
    )
    count_cells = cells_here * lax.axis_size("cells")
    cls_mean = cls_total / count_cells
    cls_var = cls_square / count_cells - cls_mean * cls_mean
    result_back = (
        cotangent.astype(jnp.float32)
        * cell_scale[:, None, None]
        * local_valid.astype(jnp.float32)[:, :, None]
    ).reshape(rows, width)
    down_low = result_back.astype(jnp.bfloat16)
    down_grad = contract(active, down_low)
    upper_back = (back_through(down_low, down_weight) * gelu_slope(upper)).astype(jnp.bfloat16)
    up_grad = contract(second_low, upper_back)
    second_back = back_through(upper_back, up_weight)
    middle_ln, second_gain_grad, second_shift_grad = norm_back(
        second_back, second_norm, second_inv, second_gain
    )
    middle_back = result_back + middle_ln
    attend_low = middle_back.astype(jnp.bfloat16)
    output_grad = contract(mixed_flat, attend_low)
    mixed_back = back_through(attend_low, output_weight).astype(jnp.bfloat16)
    keys_again, values_again = (keys_all, values_all)
    mixed_heads = mixed_back.reshape(cells_here, seq_here, heads, HEAD_DIM)
    keys_heads = keys_again.reshape(cells_here, seq_full, heads, HEAD_DIM)
    query_part, probs_low, score_grad, inner = attend_back(
        query_heads,
        keys_heads,
        values_again.reshape(cells_here, seq_full, heads, HEAD_DIM),
        valid,
        logsum,
        mixed_heads,
        scale,
    )
    value_part = jnp.einsum(
        "chqk,cqhe->ckhe", probs_low, mixed_heads, preferred_element_type=jnp.float32
    )
    key_part = (
        jnp.einsum("chqk,cqhe->ckhe", score_grad, query_heads, preferred_element_type=jnp.float32)
        * scale
    )
    key_sum, value_sum = (
        lax.psum_scatter(
            key_part.reshape(cells_here, seq_full, width).astype(jnp.bfloat16),
            "chrom",
            scatter_dimension=1,
            tiled=True,
        ).astype(jnp.float32),
        lax.psum_scatter(
            value_part.reshape(cells_here, seq_full, width).astype(jnp.bfloat16),
            "chrom",
            scatter_dimension=1,
            tiled=True,
        ).astype(jnp.float32),
    )
    keys_back = key_sum.astype(jnp.bfloat16).reshape(rows, width)
    values_back = value_sum.astype(jnp.bfloat16).reshape(rows, width)
    query_back = query_part.reshape(rows, width)
    query_grad = contract(first_low, query_back)
    key_grad = contract(first_low, keys_back)
    value_grad = contract(first_low, values_back)
    first_back = (
        back_through(query_back, query_weight)
        + back_through(keys_back, key_weight)
        + back_through(values_back, value_weight)
    )
    first_ln, first_gain_grad, first_shift_grad = norm_back(
        first_back, first_norm, first_inv, first_gain
    )
    tokens_grad = (middle_back + first_ln).reshape(cells_here, seq_here, width)
    summed = (
        lax.psum_scatter(first_gain_grad, ("cells", "chrom"), scatter_dimension=0, tiled=True),
        lax.psum_scatter(first_shift_grad, ("cells", "chrom"), scatter_dimension=0, tiled=True),
        lax.psum_scatter(query_grad, ("cells", "chrom"), scatter_dimension=0, tiled=True),
        lax.psum_scatter(key_grad, ("cells", "chrom"), scatter_dimension=0, tiled=True),
        lax.psum_scatter(value_grad, ("cells", "chrom"), scatter_dimension=0, tiled=True),
        lax.psum_scatter(output_grad, ("cells", "chrom"), scatter_dimension=0, tiled=True),
        lax.psum_scatter(second_gain_grad, ("cells", "chrom"), scatter_dimension=0, tiled=True),
        lax.psum_scatter(second_shift_grad, ("cells", "chrom"), scatter_dimension=0, tiled=True),
        lax.psum_scatter(up_grad, ("cells", "chrom"), scatter_dimension=0, tiled=True),
        lax.psum_scatter(down_grad, ("cells", "chrom"), scatter_dimension=0, tiled=True),
    )
    (
        first_gain_out,
        first_shift_out,
        query_out,
        key_out,
        value_out,
        output_out,
        second_gain_out,
        second_shift_out,
        up_out,
        down_out,
    ) = summed
    return (
        layer_out,
        tokens_grad,
        first_gain_out,
        first_shift_out,
        query_out,
        key_out,
        value_out,
        output_out,
        second_gain_out,
        second_shift_out,
        up_out,
        down_out,
        cls_mean,
        cls_var,
    )


def solution(mesh):
    in_specs = (
        P("cells", "chrom", None),
        P("cells", "chrom", None),
        P("cells", None),
        P("cells"),
        P(),
        P(),
        P(),
        P(),
        P(),
        P(),
        P(),
        P(),
        P(),
        P(),
        P(),
    )
    out_specs = (
        P("cells", "chrom", None),
        P("cells", "chrom", None),
        P(("cells", "chrom")),
        P(("cells", "chrom")),
        P(("cells", "chrom"), None),
        P(("cells", "chrom"), None),
        P(("cells", "chrom"), None),
        P(("cells", "chrom"), None),
        P(("cells", "chrom")),
        P(("cells", "chrom")),
        P(("cells", "chrom"), None),
        P(("cells", "chrom"), None),
        P(),
        P(),
    )
    return jax.shard_map(
        per_device, mesh=mesh, in_specs=in_specs, out_specs=out_specs, check_vma=False
    )
```

profile of v0, /device:TPU:1, one launch (start us, length us, event | category | flops | bytes accessed | tf_op | source)
XLA Modules:
  0.0 1680.5 jit_solution(6170283669334905070)
XLA Ops:
  14.1 3.9 convolution_convert_fusion.1
  18.1 5.5 convolution_convert_fusion.3
  23.7 6.5 convolution_convert_fusion.2
  30.2 6.8 reshape.250
  37.1 6.2 copy.70
  48.9 27.1 %all-gather.5.cloned.1.call-done = bf16[3,1024,1280]{2,1,0:T(8,128)(2,1)} async-done(((bf16[3,256,1280]{2,1,0:T(8,128)(2,1)}), bf16[3,1024,1280]{2,1,0:T(8,128)(2,1)}) %all-gather.5.cloned.1.call-update) | async-done | bytes 7864336 | tf_op jit(solution)/shard_map/all_gather | solution.py:121
  76.0 10.7 copy.69
  86.8 26.6 %fusion.6 = (f32[3,20,256]{2,1,0:T(8,128)S(1)}, f32[3,20,256,1024]{3,2,1,0:T(8,128)}) fusion(pred[3,1024]{1,0:T(4,128)(4,1)S(1)} %bitcast_compare_fusion, bf16[3,256,20,64]{1,3,2,0:T(8,128)(2,1)} %copy.70, bf16[3,1024,20,64]{1,3,2,0:T(8,128)(2,1)} %bitcast.111), kind=kOutput, calls=%fused_computation.11 | convolution fusion | flops 2060436480 | bytes 72809472 | tf_op jit(solution)/shard_map/cqhe,ckhe->chqk/dot_general | solution.py:46
  113.4 20.4 %fusion = f32[3,20,256]{2,1,0:T(8,128)S(1)} fusion(f32[3,20,256]{2,1,0:T(8,128)S(1)} %get-tuple-element.32, f32[3,20,256,1024]{3,2,1,0:T(8,128)} %get-tuple-element.33, pred[3,1024]{1,0:T(4,128)(4,1)S(1)} %bitcast_compare_fusion), kind=kLoop, calls=%fused_computation.6 | loop fusion | flops 62899200 | bytes 63040512 | tf_op jit(solution)/shard_map/reduce_sum | solution.py:54
  134.5 10.7 copy.67
  145.1 26.8 %convert_bitcast_fusion = bf16[3,256,20,64]{1,3,2,0:T(8,128)(2,1)} fusion(bf16[3,1024,20,64]{1,3,2,0:T(8,128)(2,1)} %bitcast.114, f32[3,20,256]{2,1,0:T(8,128)S(1)} %fusion, f32[3,20,256]{2,1,0:T(8,128)S(1)} %get-tuple-element.32, f32[3,20,256,1024]{3,2,1,0:T(8,128)} %get-tuple-element.33, pred[3,1024]{1,0:T(4,128)(4,1)S(1)} %bitcast_compare_fusion), kind=kOutput, calls=%fused_computation.82 | convolution fusion | flops 2092892160 | bytes 72870912 | tf_op jit(solution)/shard_map/chqk,ckhe->cqhe/dot_general | solution.py:56
  172.0 3.4 copy.71
  176.0 3.1 fusion.55
  179.7 3.1 copy-done.40
  182.8 47.8 %fusion.9 = (bf16[768,5120]{1,0:T(8,128)(2,1)}, f32[768,5120]{1,0:T(8,128)}) fusion(bf16[1280,5120]{1,0:T(8,128)(2,1)S(1)} %copy-done.40, f32[768,1280]{1,0:T(8,128)S(1)} %get-tuple-element.35, f32[1280]{0:T(1024)S(1)} %copy-done.23, f32[1280]{0:T(1024)S(1)} %copy-done.21, f32[768]{0:T(1024)S(1)} %add_rsqrt_fusion, f32[768]{0:T(1024)S(1)} %broadcast_multiply_fusion.5), kind=kOutput, calls=%fused_computation.16 | convolution fusion | flops 10326835200 | bytes 40648704 | tf_op jit(solution)/shard_map/dot_general | solution.py:136
  230.6 18.8 %fusion.15 = bf16[768,5120]{1,0:T(8,128)(2,1)} fusion(f32[768,5120]{1,0:T(8,128)} %get-tuple-element.37, bf16[768,1280]{1,0:T(8,128)(2,1)S(1)} %copy-done.9, bf16[5120,1280]{1,0:T(8,128)(2,1)} %param.29), kind=kOutput, calls=%fused_computation.22 | convolution fusion | flops 10105651200 | bytes 38666240 | tf_op jit(solution)/shard_map/re,de->rd/dot_general | solution.py:42
  249.4 19.3 %multiply_reduce_fusion.1 = (f32[1280]{0:T(1024)}, f32[768]{0:T(1024)S(1)}, f32[768]{0:T(1024)S(1)}, f32[1280]{0:T(1024)}, f32[768,1280]{1,0:T(8,128)}) fusion(f32[768,1280]{1,0:T(8,128)} %copy-done.3, f32[768]{0:T(1024)S(1)} %add_rsqrt_fusion, f32[768]{0:T(1024)S(1)} %broadcast_multiply_fusion.5, f32[1280]{0:T(1024)S(1)} %copy-done.21, ...), kind=kOutput, calls=%fused_computation.67 | convolution fusion | flops 10075172864 | bytes 28863488 | tf_op jit(solution)/shard_map/re,de->rd/dot_general | solution.py:42
  268.8 5.3 bitcast_add_fusion
  275.9 3.9 convolution_convert_fusion
  279.9 6.6 reshape.251
  286.5 6.2 copy.73
  292.7 28.3 %fusion.23 = bf16[3,20,64,1024]{3,2,1,0:T(8,128)(2,1)} fusion(bf16[3,256,20,64]{1,3,2,0:T(8,128)(2,1)} %copy.73, f32[3,20,256]{2,1,0:T(8,128)S(1)} %copy-done.16, f32[3,20,256,1024]{3,2,1,0:T(8,128)} %get-tuple-element.33, pred[3,1024]{1,0:T(4,128)(4,1)S(1)} %copy-done.15), kind=kOutput, calls=%fused_computation.41 | convolution fusion | flops 2080112640 | bytes 72809472 | tf_op jit(solution)/shard_map/chqk,cqhe->ckhe/dot_general | solution.py:178
  320.9 10.7 copy.78
  331.7 49.1 %multiply_reduce_fusion = (f32[3,20,256]{2,1,0:T(8,128)S(1)}, f32[3,20,256,1024]{3,2,1,0:T(8,128)}) fusion(f32[3,20,256]{2,1,0:T(8,128)S(1)} %copy-done.16, f32[3,20,256,1024]{3,2,1,0:T(8,128)} %get-tuple-element.33, pred[3,1024]{1,0:T(4,128)(4,1)S(1)} %copy-done.15, bf16[3,256,20,64]{1,3,2,0:T(8,128)(2,1)} %copy.73, bf16[3,1024,20,64]{1,3,2,0:T(8,128)(2,1)} %bitcast.115), kind=kOutput, calls=%fused_computation.1 | convolution fusion | flops 2091893760 | bytes 135785472 | tf_op jit(solution)/shard_map/cqhe,ckhe->chqk/dot_general | solution.py:63
  380.8 50.2 %multiply_convert_fusion = bf16[3,20,256,1024]{3,2,1,0:T(8,128)(2,1)} fusion(f32[3,20,256,1024]{3,2,1,0:T(8,128)} %get-tuple-element.40, f32[3,20,256]{2,1,0:T(8,128)S(1)} %get-tuple-element.39, f32[3,20,256]{2,1,0:T(8,128)S(1)} %copy-done.16, f32[3,20,256,1024]{3,2,1,0:T(8,128)} %get-tuple-element.33, pred[3,1024]{1,0:T(4,128)(4,1)S(1)} %copy-done.15), kind=kLoop, calls=%fused_computation | loop fusion | flops 94371840 | bytes 157412352 | tf_op jit(solution)/shard_map/convert_element_type | solution.py:67
  431.0 16.7 multiply_convert_fusion.1
  447.7 10.5 copy.76
  458.7 8.7 fusion.45
  468.1 3.9 fusion.31
  472.0 17.5 %fusion.44 = bf16[3,256,20,64]{1,3,2,0:T(8,128)(2,1)S(1)} fusion(bf16[3,1024,20,64]{1,3,2,0:T(8,128)(2,1)} %bitcast.112, bf16[3,20,256,1024]{3,2,1,0:T(8,128)(2,1)} %multiply_convert_fusion), kind=kOutput, calls=%fused_computation.81 | convolution fusion | flops 2015232000 | bytes 41287680 | tf_op jit(solution)/shard_map/chqk,ckhe->cqhe/dot_general | solution.py:69
  493.1 4.7 fusion.58
  497.9 7.7 convolution_bitcast_fusion
  505.8 20.6 %reduce-scatter.9.cloned.1.call-done = bf16[3,256,1280]{2,1,0:T(8,128)(2,1)} async-done(((bf16[3,1024,1280]{2,1,0:T(8,128)(2,1)}), bf16[3,256,1280]{2,1,0:T(8,128)(2,1)}) %reduce-scatter.9.cloned.1.call-update) | async-done | bytes 1966096 | tf_op jit(solution)/shard_map/reduce_scatter | solution.py:186
  526.4 7.6 convolution_bitcast_fusion.1
  534.8 19.2 %fusion.53 = f32[1280,5120]{1,0:T(8,128)} fusion(bf16[768,5120]{1,0:T(8,128)(2,1)} %fusion.15, f32[768,1280]{1,0:T(8,128)} %copy-done.3, f32[1280]{0:T(1024)S(1)} %copy-done.24, f32[1280]{0:T(1024)S(1)} %copy-done.22, f32[768]{0:T(1024)S(1)} %copy-done.20, f32[768]{0:T(1024)S(1)} %copy-done.18), kind=kOutput, calls=%fused_computation.110 | convolution fusion | flops 10071244800 | bytes 38027264 | tf_op jit(solution)/shard_map/rd,re->de/dot_general | solution.py:38
  554.3 18.2 %fusion.59 = f32[5120,1280]{1,0:T(8,128)} fusion(bf16[768,5120]{1,0:T(8,128)(2,1)} %get-tuple-element.36, bf16[768,1280]{1,0:T(8,128)(2,1)} %bitcast_convert_fusion), kind=kOutput, calls=%fused_computation.116 | convolution fusion | flops 10066329600 | bytes 36044800 | tf_op jit(solution)/shard_map/rd,re->de/dot_general | solution.py:38
  572.4 16.4 convolution_add_fusion
  592.1 2.8 fusion.56
  594.9 2.7 fusion.57
  597.7 5.6 fusion.43
  603.4 43.1 %all-reduce.4 = (f32[1280]{0:T(1024)S(1)}, f32[1280]{0:T(1024)S(1)}, f32[1280]{0:T(1024)S(1)}, f32[1280]{0:T(1024)S(1)}, f32[1280]{0:T(1024)S(1)}, /*index=5*/f32[1280]{0:T(1024)S(1)}) all-reduce(f32[1280]{0:T(1024)S(1)} %get-tuple-element.16, ...), channel_id=4, replica_groups=mesh['cells'=8,'chrom'=4] {'cells','chrom'}, use_global_device_ids=true, to_apply=%region_15.16.clone | all-reduce | flops 7680 | bytes 61440
  649.4 7.1 fusion.42
  656.6 12.9 reduce-scatter.19.cloned.1.call-done
  669.5 144.8 %reduce-scatter.13.cloned.1.call-done = f32[40,1280]{1,0:T(8,128)} async-done(((f32[1280,1280]{1,0:T(8,128)}), f32[40,1280]{1,0:T(8,128)}) %reduce-scatter.13.cloned.1.call-update) | async-done | bytes 204816 | tf_op jit(solution)/shard_map/reduce_scatter | solution.py:217
  814.3 144.5 %reduce-scatter.17.cloned.1.call-done = f32[40,1280]{1,0:T(8,128)} async-done(((f32[1280,1280]{1,0:T(8,128)}), f32[40,1280]{1,0:T(8,128)}) %reduce-scatter.17.cloned.1.call-update) | async-done | bytes 204816 | tf_op jit(solution)/shard_map/reduce_scatter | solution.py:219
  958.9 144.5 %reduce-scatter.15.cloned.1.call-done = f32[40,1280]{1,0:T(8,128)} async-done(((f32[1280,1280]{1,0:T(8,128)}), f32[40,1280]{1,0:T(8,128)}) %reduce-scatter.15.cloned.1.call-update) | async-done | bytes 204816 | tf_op jit(solution)/shard_map/reduce_scatter | solution.py:218
  1103.4 286.0 %reduce-scatter.21.cloned.1.call-done = f32[40,5120]{1,0:T(8,128)} async-done(((f32[1280,5120]{1,0:T(8,128)}), f32[40,5120]{1,0:T(8,128)}) %reduce-scatter.21.cloned.1.call-update) | async-done | bytes 819216 | tf_op jit(solution)/shard_map/reduce_scatter | solution.py:223
  1389.4 284.0 %reduce-scatter.23.cloned.1.call-done = f32[160,1280]{1,0:T(8,128)} async-done(((f32[5120,1280]{1,0:T(8,128)}), f32[160,1280]{1,0:T(8,128)}) %reduce-scatter.23.cloned.1.call-update) | async-done | bytes 819216 | tf_op jit(solution)/shard_map/reduce_scatter | solution.py:224
  (148 shorter events, 28.6 us)
Async XLA Ops:
  7.2 10.9 copy-start
  7.2 4.4 copy-start.25
  7.2 4.4 copy-start.35
  7.2 68.8 %all-gather.5.cloned.1.call-start = ((), (), s32[]{:S(2)}) async-start(), calls=%async_computation.9 | async-start | bytes 9830400 | tf_op jit(solution)/shard_map/all_gather | solution.py:121
  9.3 8.7 copy-start.27
  9.3 8.7 copy-start.29
  11.6 6.5 copy-start.33
  11.6 6.4 copy-start.31
  11.6 2.5 copy-start.42
  14.1 3.9 copy-start.13
  18.1 116.4 %all-gather.3.cloned.1.call-start = ((), (), s32[]{:S(2)}) async-start(), calls=%async_computation.8 | async-start | bytes 9830400 | tf_op jit(solution)/shard_map/all_gather | solution.py:122
  23.7 474.3 %reduce-scatter.11.cloned.1.call-start = ((), (), s32[]{:S(2)}) async-start(), calls=%async_computation.11 | async-start | bytes 9830400 | tf_op jit(solution)/shard_map/reduce_scatter | solution.py:192
  37.1 6.2 copy-start.39
  37.1 6.3 copy-start.46
  37.1 6.3 copy-start.47
  43.3 101.8 %copy-start.14 = (pred[3,1024]{1,0:T(4,128)(4,1)}, pred[3,1024]{1,0:T(4,128)(4,1)S(1)}, u32[]{:S(2)}) copy-start(pred[3,1024]{1,0:T(4,128)(4,1)S(1)} %bitcast_compare_fusion) | copy-start | bytes 9220
  45.6 1.9 copy-start.4
  172.0 4.0 copy-start.1
  172.0 4.0 copy-start.7
  175.9 3.2 copy-start.6
  176.0 6.8 copy-start.40
  179.1 51.5 %copy-start.3 = (f32[768,1280]{1,0:T(8,128)}, f32[768,1280]{1,0:T(8,128)S(1)}, u32[]{:S(2)}) copy-start(f32[768,1280]{1,0:T(8,128)S(1)} %get-tuple-element.35) | copy-start | bytes 11796484
  179.1 3.7 copy-start.21
  179.1 3.7 copy-start.23
  179.2 89.6 %copy-start.17 = (f32[768]{0:T(1024)}, f32[768]{0:T(1024)S(1)}, u32[]{:S(2)}) copy-start(f32[768]{0:T(1024)S(1)} %broadcast_multiply_fusion.5) | copy-start | bytes 9220
  182.8 86.0 %copy-start.19 = (f32[768]{0:T(1024)}, f32[768]{0:T(1024)S(1)}, u32[]{:S(2)}) copy-start(f32[768]{0:T(1024)S(1)} %add_rsqrt_fusion) | copy-start | bytes 9220
  182.8 47.8 %copy-start.9 = (bf16[768,1280]{1,0:T(8,128)(2,1)S(1)}, bf16[768,1280]{1,0:T(8,128)(2,1)}, u32[]{:S(2)}) copy-start(bf16[768,1280]{1,0:T(8,128)(2,1)} %bitcast_convert_fusion) | copy-start | bytes 5898244
  268.8 7.2 copy-start.8
  286.5 6.2 copy-start.15
  286.5 6.2 copy-start.16
  331.6 194.8 %reduce-scatter.9.cloned.1.call-start = ((), (), s32[]{:S(2)}) async-start(), calls=%async_computation.10 | async-start | bytes 9830400 | tf_op jit(solution)/shard_map/reduce_scatter | solution.py:186
  458.2 211.3 %reduce-scatter.19.cloned.1.call-start = ((), (), s32[]{:S(2)}) async-start(), calls=%async_computation.15 | async-start | bytes 6758400 | tf_op jit(solution)/shard_map/reduce_scatter | solution.py:220
  467.4 346.9 %reduce-scatter.13.cloned.1.call-start = ((), (), s32[]{:S(2)}) async-start(), calls=%async_computation.12 | async-start | bytes 6758400 | tf_op jit(solution)/shard_map/reduce_scatter | solution.py:217
  489.5 3.6 copy-start.12
  497.9 461.0 %reduce-scatter.17.cloned.1.call-start = ((), (), s32[]{:S(2)}) async-start(), calls=%async_computation.14 | async-start | bytes 6758400 | tf_op jit(solution)/shard_map/reduce_scatter | solution.py:219
  505.6 597.8 %reduce-scatter.15.cloned.1.call-start = ((), (), s32[]{:S(2)}) async-start(), calls=%async_computation.13 | async-start | bytes 6758400 | tf_op jit(solution)/shard_map/reduce_scatter | solution.py:218
  534.1 855.4 %reduce-scatter.21.cloned.1.call-start = ((), (), s32[]{:S(2)}) async-start(), calls=%async_computation.16 | async-start | bytes 27033600 | tf_op jit(solution)/shard_map/reduce_scatter | solution.py:223
  554.0 1119.4 %reduce-scatter.23.cloned.1.call-start = ((), (), s32[]{:S(2)}) async-start(), calls=%async_computation.17 | async-start | bytes 27033600 | tf_op jit(solution)/shard_map/reduce_scatter | solution.py:224
  588.8 2.3 copy-start.11
  588.8 3.3 copy-start.41
  592.1 2.8 copy-start.43
  592.1 2.8 copy-start.45
  594.9 2.8 copy-start.2
  594.9 2.8 copy-start.30
  594.9 2.8 copy-start.32
  594.9 2.8 copy-start.44
  597.7 5.7 copy-start.37
  597.7 5.6 copy-start.38
  (10 other events, 9.0 us)
Sparse Core Ops, SparseCore 0:
  18.2 57.8 all-gather.4
  78.2 55.3 all-gather.2
  331.8 68.7 reduce-scatter.10
  458.3 68.0 reduce-scatter.8
  529.1 140.3 reduce-scatter.18
  672.2 142.0 reduce-scatter.12
  817.2 141.6 reduce-scatter.16
  961.7 141.6 reduce-scatter.14
  1106.3 283.0 reduce-scatter.20
  1392.1 281.2 reduce-scatter.22
where the time goes:
time: 1690 us; the launch traced here: 1680 us
  waiting for transfers between devices  1060 us (63%)
  matrix products  367 us (22%)
  other arithmetic  101 us (6%)
  local copies, waits for them, and re-layouts  88.4 us (5%)
  blocking collectives  43.1 us (3%)
    reduce_scatter x1, waiting for transfers between devices, per_device(): lax.psum_scatter(up_grad, ('cells', 'chrom'), scatter_dimension=0, tiled=...  286 us
    reduce_scatter x1, waiting for transfers between devices, per_device(): lax.psum_scatter(down_grad, ('cells', 'chrom'), scatter_dimension=0, tile...  284 us
    reduce_scatter x1, waiting for transfers between devices, per_device(): lax.psum_scatter(query_grad, ('cells', 'chrom'), scatter_dimension=0, til...  145 us
    reduce_scatter x1, waiting for transfers between devices, per_device(): lax.psum_scatter(value_grad, ('cells', 'chrom'), scatter_dimension=0, til...  145 us
    reduce_scatter x1, waiting for transfers between devices, per_device(): lax.psum_scatter(key_grad, ('cells', 'chrom'), scatter_dimension=0, tiled...  145 us
    dot_general x6, matrix products, contract(): jnp.einsum('rd,re->de', left, right, preferred_element_type=jnp.float32)  66 us
    dot_general x6, matrix products, back_through(): jnp.einsum('re,de->rd', grad, weight, preferred_element_type=jnp.float32)  53.2 us
    convert_element_type x1, other arithmetic, attend_back(): score_grad = (probs * (prob_grad - inner)).astype(jnp.bfloat16)  50.2 us
  transfers between devices with their start and end apart: 10, of which 8 were waited for; matrix products, arithmetic and copies ran while one was open for 20% of the time, Pallas kernels for 0%

commit v1 on v0

v1 whole, which is shorter than its diff:
```python
import functools
import math

import jax
import jax.numpy as jnp
from jax import lax
from jax.experimental import pallas as pl
from jax.experimental.pallas import tpu as pltpu
from jax.sharding import PartitionSpec as P

HEAD_DIM = 64
FILLED = 768
EPS = 1e-05
ROOT_HALF = 0.7071067811865476
DENSITY_SCALE = 0.3989422804014327
LOG2E = 1.4426950408889634
BF = jnp.bfloat16
F32 = jnp.float32
NT = (((1,), (1,)), ((), ()))
TN = (((0,), (0,)), ((), ()))
VMEM_MAX = 60 * 2**20


def whole(shape):
    return pl.BlockSpec(shape, lambda *_: (0,) * len(shape), pipeline_mode=pl.Buffered(1))


def smem():
    return pl.BlockSpec(memory_space=pltpu.SMEM)


def cost(flops, moved, exps=0):
    return pl.CostEstimate(flops=int(flops), bytes_accessed=int(moved), transcendentals=int(exps))


def shift_rows(shape, dim, shift, length):
    slot = lax.broadcasted_iota(jnp.int32, shape, dim)
    row = lax.broadcasted_iota(jnp.int32, shape, 1 - dim)
    return jnp.where((row == slot + shift) & (slot < length), 1.0, 0.0).astype(BF)


def pack(packed, values, lens, part, block, at):
    per = values.shape[0] // block
    for b in range(per):
        here = lens[part * per + b]
        rows = values[b * block : (b + 1) * block, :]
        shift = at % 8
        base = pl.multiple_of(at - shift, 8) if part + b else 0
        move = shift_rows((block + 8, block), 1, shift, here)
        moved = jnp.dot(move, rows, preferred_element_type=F32)
        if part + b:
            packed[pl.ds(base, 8), :] += moved[:8, :]
            packed[pl.ds(pl.multiple_of(base + 8, 8), block), :] = moved[8:, :]
        else:
            packed[: block + 8, :] = moved
        at = at + here
    return at


def unpack(packed, out, lens, part, block, at):
    per = out.shape[0] // block
    for b in range(per):
        here = lens[part * per + b]
        shift = at % 8
        base = pl.multiple_of(at - shift, 8) if part + b else 0
        rows = packed[pl.ds(base, block + 8), :].astype(BF)
        move = shift_rows((block, block + 8), 0, shift, here)
        out[b * block : (b + 1) * block, :] = jnp.dot(
            move, rows, preferred_element_type=F32
        ).astype(BF)
        at = at + here
    return at


def attend_kernel(block, heads, lens, *refs):
    parts = 4
    firsts, weight = refs[:parts], refs[parts]
    mixed = refs[parts + 1 : 2 * parts + 1]
    qkv_c = refs[2 * parts + 1]
    query, packed = refs[2 * parts + 2 :]
    rows = firsts[0].shape[0]
    wide = heads * HEAD_DIM
    at = 0
    for r in range(parts):
        qkv = jnp.dot(firsts[r][...], weight[...], preferred_element_type=F32)
        query[r * rows : (r + 1) * rows, :] = qkv[:, :wide].astype(BF)
        at = pack(packed, qkv.astype(BF), lens, r, block, at)
    qkv_c[...] = packed[:FILLED, :].astype(BF)
    scale = LOG2E / math.sqrt(HEAD_DIM)
    ones = jnp.ones((FILLED, HEAD_DIM), BF)
    for r in range(parts):
        for h in range(heads):
            lo = h * HEAD_DIM
            q = query[r * rows : (r + 1) * rows, lo : lo + HEAD_DIM]
            k = qkv_c[:, wide + lo : wide + lo + HEAD_DIM]
            v = qkv_c[:, 2 * wide + lo : 2 * wide + lo + HEAD_DIM]
            s = lax.dot_general(q, k, NT, preferred_element_type=F32)
            top = jnp.max(s, axis=1, keepdims=True) * scale
            e = jnp.exp2(s * scale - top).astype(BF)
            o = jnp.dot(e, jnp.concatenate([v, ones], axis=1), preferred_element_type=F32)
            o = o[:, :HEAD_DIM] / o[:, HEAD_DIM:]
            mixed[r][:, lo : lo + HEAD_DIM] = o.astype(BF)


def attend(firsts, lens, weight, block):
    rows, width = firsts[0].shape
    wide3 = weight.shape[1]
    wide = wide3 // 3
    heads = wide // HEAD_DIM
    out = pl.pallas_call(
        functools.partial(attend_kernel, block, heads),
        in_specs=[smem()] + [whole((rows, width))] * 4 + [whole(weight.shape)],
        out_specs=[whole((rows, wide))] * 4 + [whole((FILLED, wide3))],
        out_shape=[jax.ShapeDtypeStruct((rows, wide), BF)] * 4
        + [jax.ShapeDtypeStruct((FILLED, wide3), BF)],
        scratch_shapes=[pltpu.VMEM((4 * rows, wide), BF), pltpu.VMEM((FILLED + block, wide3), F32)],
        compiler_params=pltpu.CompilerParams(vmem_limit_bytes=VMEM_MAX),
        cost_estimate=cost(2 * 4 * rows * width * wide3 + 4 * 4 * rows * FILLED * 256 * heads, 8e6),
        grid=(1,),
        name="attend",
    )(lens, *firsts, weight)
    return out[:4], out[4]


def attend_back_kernel(block, heads, lens, *refs):
    parts = 4
    grads, qkv_c = refs[:parts], refs[parts]
    outs = refs[parts + 1 : 2 * parts + 1]
    packed, back = refs[2 * parts + 1 :]
    wide = heads * HEAD_DIM
    at = 0
    for r in range(parts):
        at = pack(packed, grads[r][...], lens, r, block, at)
    scale = LOG2E / math.sqrt(HEAD_DIM)
    inv_root = 1.0 / math.sqrt(HEAD_DIM)
    chunk = 256
    back[FILLED:, :] = jnp.zeros((block, 3 * wide), F32)
    grad_t = packed[:FILLED, :].T
    query_t = qkv_c[:, :wide].astype(F32).T.astype(BF)
    key_t = qkv_c[:, wide : 2 * wide].astype(F32).T.astype(BF)
    for h in range(heads):
        lo = h * HEAD_DIM
        k = qkv_c[:, wide + lo : wide + lo + HEAD_DIM]
        v = qkv_c[:, 2 * wide + lo : 2 * wide + lo + HEAD_DIM]
        kt = key_t[lo : lo + HEAD_DIM, :]
        dv = jnp.zeros((FILLED, HEAD_DIM), F32)
        dk = jnp.zeros((FILLED, HEAD_DIM), F32)
        for c in range(0, FILLED, chunk):
            qt = query_t[lo : lo + HEAD_DIM, c : c + chunk]
            s = jnp.dot(k, qt, preferred_element_type=F32)
            top = jnp.max(s, axis=0, keepdims=True) * scale
            e = jnp.exp2(s * scale - top)
            inv = 1.0 / jnp.sum(e, axis=0, keepdims=True)
            gt = (grad_t[lo : lo + HEAD_DIM, c : c + chunk] * inv).astype(BF)
            dp = jnp.dot(v, gt, preferred_element_type=F32)
            inner = jnp.sum(e * dp, axis=0, keepdims=True) * inv
            ds = (e * (dp - inner)).astype(BF)
            dv = dv + lax.dot_general(e.astype(BF), gt, NT, preferred_element_type=F32)
            dk = dk + lax.dot_general(ds, qt, NT, preferred_element_type=F32)
            dqt = jnp.dot(kt, ds, preferred_element_type=F32)
            back[c : c + chunk, lo : lo + HEAD_DIM] = dqt.T * inv_root
        back[:FILLED, wide + lo : wide + lo + HEAD_DIM] = dk * inv_root
        back[:FILLED, 2 * wide + lo : 2 * wide + lo + HEAD_DIM] = dv
    at = 0
    for r in range(parts):
        at = unpack(back, outs[r], lens, r, block, at)


def attend_back(grads, lens, qkv_c, block):
    rows, wide = grads[0].shape
    heads = wide // HEAD_DIM
    return pl.pallas_call(
        functools.partial(attend_back_kernel, block, heads),
        in_specs=[smem()] + [whole((rows, wide))] * 4 + [whole(qkv_c.shape)],
        out_specs=[whole((rows, 3 * wide))] * 4,
        out_shape=[jax.ShapeDtypeStruct((rows, 3 * wide), BF)] * 4,
        scratch_shapes=[
            pltpu.VMEM((FILLED + block, wide), F32),
            pltpu.VMEM((FILLED + block, 3 * wide), F32),
        ],
        compiler_params=pltpu.CompilerParams(vmem_limit_bytes=VMEM_MAX),
        cost_estimate=cost(2 * 5 * FILLED * FILLED * 256 * heads, 6e6),
        grid=(1,),
        name="attend_back",
    )(lens, *grads, qkv_c)


FF_TILE = 512
FF_ROWS = 256
FF_GRAD = 256


def feed_kernel(half, second_a, second_b, low_a, low_b, up, down, *refs):
    result, send_result, back, send_back, down_grad, up_grad = refs[:6]
    second_t, active, upper_back, acc_result, acc_back = refs[6:]
    rows, width = second_a.shape
    tile = up.shape[1]
    step = pl.program_id(0)

    @pl.when(step == 0)
    def _():
        result[...] = jnp.zeros_like(result)
        back[...] = jnp.zeros_like(back)
        acc_result[...] = jnp.zeros_like(acc_result)
        acc_back[...] = jnp.zeros_like(acc_back)
        for part, ref in enumerate((second_a, second_b)):
            for lo in range(0, rows, FF_ROWS):
                at = part * rows + lo
                second_t[:, at : at + FF_ROWS] = ref[lo : lo + FF_ROWS, :].astype(F32).T.astype(BF)

    for part, (second, low, to_result, to_back) in enumerate(
        ((second_a, low_a, result, back), (second_b, low_b, acc_result, acc_back))
    ):

        def chunk(i, carry):
            here = pl.ds(pl.multiple_of(i * FF_ROWS, FF_ROWS), FF_ROWS)
            there = pl.ds(pl.multiple_of(part * rows + i * FF_ROWS, FF_ROWS), FF_ROWS)
            upper = jnp.dot(second[here, :], up[...], preferred_element_type=F32)
            grad = lax.dot_general(low[here, :], down[...], NT, preferred_element_type=F32)
            below = 0.5 * (1.0 + lax.erf(upper * ROOT_HALF))
            density = jnp.exp(-0.5 * upper * upper) * DENSITY_SCALE
            act = (upper * below).astype(BF)
            ub = (grad * (below + upper * density)).astype(BF)
            active[there, :] = act
            upper_back[there, :] = ub
            to_result[here, :] += jnp.dot(act, down[...], preferred_element_type=F32)
            to_back[here, :] += lax.dot_general(ub, up[...], NT, preferred_element_type=F32)
            return carry

        lax.fori_loop(0, rows // FF_ROWS, chunk, 0)

    def one_down(i, carry):
        here = pl.ds(pl.multiple_of(i * FF_GRAD, FF_GRAD), FF_GRAD)
        act = active[:, here].astype(F32).T.astype(BF)
        down_grad[here, :] = (
            jnp.dot(act[:, :rows], low_a[...], preferred_element_type=F32)
            + jnp.dot(act[:, rows:], low_b[...], preferred_element_type=F32)
        ).astype(BF)
        return carry

    lax.fori_loop(0, tile // FF_GRAD, one_down, 0)

    def one_up(i, carry):
        here = pl.ds(pl.multiple_of(i * FF_GRAD, FF_GRAD), FF_GRAD)
        up_grad[here, :] = jnp.dot(
            second_t[here, :], upper_back[...], preferred_element_type=F32
        ).astype(BF)
        return carry

    lax.fori_loop(0, width // FF_GRAD, one_up, 0)

    @pl.when(step == pl.num_programs(0) - 1)
    def _():
        send_result[...] = acc_result[...].astype(BF)
        send_back[...] = acc_back[...].astype(BF)


def feed_forward(half, second_a, second_b, low_a, low_b, up, down):
    rows, width = second_a.shape
    units = up.shape[1] // 2
    tiles = units // FF_TILE
    two = 2 * rows
    return pl.pallas_call(
        feed_kernel,
        grid_spec=pltpu.PrefetchScalarGridSpec(
            num_scalar_prefetch=1,
            grid=(tiles,),
            in_specs=[whole((rows, width))] * 4
            + [
                pl.BlockSpec((width, FF_TILE), lambda j, half: (0, half[0] * tiles + j)),
                pl.BlockSpec((FF_TILE, width), lambda j, half: (half[0] * tiles + j, 0)),
            ],
            out_specs=[whole((rows, width))] * 4
            + [
                pl.BlockSpec((FF_TILE, width), lambda j, half: (j, 0)),
                pl.BlockSpec((width, FF_TILE), lambda j, half: (0, j)),
            ],
            scratch_shapes=[
                pltpu.VMEM((width, two), BF),
                pltpu.VMEM((two, FF_TILE), BF),
                pltpu.VMEM((two, FF_TILE), BF),
                pltpu.VMEM((rows, width), F32),
                pltpu.VMEM((rows, width), F32),
            ],
        ),
        out_shape=[
            jax.ShapeDtypeStruct((rows, width), F32),
            jax.ShapeDtypeStruct((rows, width), BF),
            jax.ShapeDtypeStruct((rows, width), F32),
            jax.ShapeDtypeStruct((rows, width), BF),
            jax.ShapeDtypeStruct((units, width), BF),
            jax.ShapeDtypeStruct((width, units), BF),
        ],
        compiler_params=pltpu.CompilerParams(vmem_limit_bytes=VMEM_MAX),
        cost_estimate=cost(2 * 6 * two * width * units, 6e7),
        name="feed_forward",
    )(half, second_a, second_b, low_a, low_b, up, down)


def swap(x, axis, mask):
    size = lax.axis_size(axis)
    return lax.ppermute(x, axis, [(i, i ^ mask) for i in range(size)])


def halve(x, dim, axis, bit):
    mine = (lax.axis_index(axis) >> bit) & 1
    send = lax.dynamic_index_in_dim(x, 1 - mine, dim, keepdims=False)
    keep = lax.dynamic_index_in_dim(x, mine, dim, keepdims=False)
    got = swap(send, axis, 1 << bit)
    return keep.astype(F32) + got.astype(F32)


def log2(n):
    return n.bit_length() - 1


def scatter_rows(x, order, names):
    names = list(names)
    for i, name in enumerate(order):
        x = halve(x.astype(BF), names.index(name), name[0], name[1])
        names.remove(name)
    return x


def sum_all(x):
    for bit in range(log2(lax.axis_size("chrom"))):
        x = x + swap(x, "chrom", 1 << bit)
    for bit in range(log2(lax.axis_size("cells"))):
        x = x + swap(x, "cells", 1 << bit)
    return x


def scatter_columns_split(x, order):
    cell_bits = log2(lax.axis_size("cells"))
    core = lax.axis_index("chrom") & 1
    width = x.shape[1]
    names = [("cells", b) for b in reversed(range(cell_bits))] + [("chrom", 1)]
    x = x.reshape((2,) * (cell_bits + 1) + (-1, width))
    x = scatter_rows(x, order, names)
    x = x.reshape(2, -1, width)
    keep = lax.dynamic_index_in_dim(x, core, 0, keepdims=False)
    got = swap(lax.dynamic_index_in_dim(x, 1 - core, 0, keepdims=False).astype(BF), "chrom", 1).astype(F32)
    left = jnp.where(core == 0, keep, got)
    right = jnp.where(core == 0, got, keep)
    return jnp.concatenate([left, right], axis=1)


def scatter_rows_split(x, order):
    cells = lax.axis_size("cells")
    cell_bits = log2(cells)
    chrom = lax.axis_size("chrom")
    core = lax.axis_index("chrom") & 1
    high = (lax.axis_index("cells") >> (cell_bits - 1)) & 1
    width = x.shape[1]
    names = [("cells", b) for b in reversed(range(cell_bits - 1))] + [("chrom", 1)]
    x = x.reshape((2,) * cell_bits + (-1, width))
    x = scatter_rows(x, order, names)
    top = cells // 2
    pairs = []
    for cell in range(cells):
        for place in range(chrom):
            if (cell // top) != (place & 1):
                pairs.append((cell * chrom + place, (cell ^ top) * chrom + place))
    got = lax.ppermute(x.astype(BF), ("cells", "chrom"), pairs)
    x = (x + got.astype(F32)).reshape(2, -1, width)
    keep = lax.dynamic_index_in_dim(x, core, 0, keepdims=False)
    send = lax.dynamic_index_in_dim(x, 1 - core, 0, keepdims=False).astype(BF)
    back = []
    for cell in range(cells):
        for place in range(chrom):
            if (cell // top) == (place & 1):
                back.append((cell * chrom + place, cell * chrom + (place ^ 1)))
    got = lax.ppermute(send, ("cells", "chrom"), back)
    return jnp.where(core == high, keep, got.astype(F32))


def norm_rows(values, gain, shift):
    center = values - jnp.mean(values, axis=-1, keepdims=True)
    inverse = lax.rsqrt(jnp.mean(center * center, axis=-1, keepdims=True) + EPS)
    normed = center * inverse
    return (normed * gain + shift, normed, inverse)


def norm_back(grad_out, normed, inverse, gain):
    scaled = grad_out * gain
    grad_in = inverse * (
        scaled
        - jnp.mean(scaled, axis=-1, keepdims=True)
        - normed * jnp.mean(scaled * normed, axis=-1, keepdims=True)
    )
    return (grad_in, jnp.sum(grad_out * normed, axis=0), jnp.sum(grad_out, axis=0))


def contract(left, right):
    return lax.dot_general(left, right, TN, preferred_element_type=F32)


def back_through(grad, weight):
    return lax.dot_general(grad, weight, NT, preferred_element_type=F32)


def per_device(
    tokens,
    cotangent,
    block_lengths,
    group_ids,
    group_weights,
    first_gain,
    first_shift,
    query_weight,
    key_weight,
    value_weight,
    output_weight,
    second_gain,
    second_shift,
    up_weight,
    down_weight,
):
    cells_here, seq_here, width = tokens.shape
    rows = cells_here * seq_here
    parts = lax.axis_size("chrom")
    cell_bits = log2(lax.axis_size("cells"))
    seq_full = seq_here * parts
    nblocks = block_lengths.shape[1]
    block = seq_full // nblocks
    per = nblocks // parts
    wide = width // parts
    place = lax.axis_index("chrom")
    core = place & 1
    near = [place ^ r for r in range(parts)]

    valid = (jnp.arange(block)[None, None, :] < block_lengths[:, :, None]).reshape(
        cells_here, seq_full
    )
    local_valid = lax.dynamic_slice_in_dim(valid, place * seq_here, seq_here, 1)
    lens = jnp.concatenate(
        [lax.dynamic_slice_in_dim(block_lengths, n * per, per, 1) for n in near], axis=1
    )
    n_groups = group_weights.shape[0]
    cell_scale = jnp.sum(
        jnp.where(group_ids[:, None] == jnp.arange(n_groups)[None, :], group_weights[None, :], 0.0),
        axis=1,
    )

    def my_heads(weight):
        return lax.dynamic_slice_in_dim(weight, place * wide, wide, 1)

    qkv_weight = jnp.concatenate(
        [my_heads(query_weight), my_heads(key_weight), my_heads(value_weight)], axis=1
    )
    output_near = jnp.concatenate(
        [lax.dynamic_slice_in_dim(output_weight, n * wide, wide, 0) for n in near], axis=0
    )

    flat = tokens.reshape(rows, width).astype(F32)
    first_out, first_norm, first_inv = norm_rows(flat, first_gain, first_shift)
    first_low = first_out.astype(BF).reshape(cells_here, seq_here, width)
    first_all, mixed_near, kept = [], [], []
    for c in range(cells_here):
        mine = first_low[c]
        over = swap(mine, "chrom", 2)
        first_all.append([mine, swap(mine, "chrom", 1), over, swap(over, "chrom", 1)])
    for c in range(cells_here):
        mixed, qkv_c = attend(first_all[c], lens[c], qkv_weight, block)
        kept.append(qkv_c)
        mixed_near.append(
            jnp.concatenate([mixed[0]] + [swap(mixed[r], "chrom", r) for r in range(1, parts)], axis=1)
        )
    mixed_flat = jnp.concatenate(mixed_near, axis=0)

    middle = flat + jnp.dot(mixed_flat, output_near, preferred_element_type=F32)
    second_out, second_norm, second_inv = norm_rows(middle, second_gain, second_shift)
    second_low = second_out.astype(BF)
    result_back = (
        cotangent.astype(F32)
        * cell_scale[:, None, None]
        * local_valid.astype(F32)[:, :, None]
    ).reshape(rows, width)
    down_low = result_back.astype(BF)
    down_low_near = swap(down_low, "chrom", 1)
    second_low_near = swap(second_low, "chrom", 1)

    result_part, result_send, back_part, back_send, down_grad, up_grad = feed_forward(
        core[None].astype(jnp.int32),
        second_low,
        second_low_near,
        down_low,
        down_low_near,
        up_weight,
        down_weight,
    )
    second_back = back_part + swap(back_send, "chrom", 1).astype(F32)
    result = middle + result_part + swap(result_send, "chrom", 1).astype(F32)
    result_cells = result.reshape(cells_here, seq_here, width)
    layer_out = result_cells.astype(BF)
    low_bits = [("cells", b) for b in range(cell_bits - 1)]
    down_out = scatter_rows_split(down_grad, low_bits + [("chrom", 1)])
    up_out = scatter_columns_split(up_grad, [("chrom", 1)] + low_bits[::-1] + [("cells", cell_bits - 1)])

    cls_rows = jnp.where(place == 0, result_cells[:, 0, :], 0.0)
    cls_total = jnp.sum(cls_rows, axis=0)
    cls_square = jnp.sum(cls_rows * cls_rows, axis=0)

    middle_ln, second_gain_grad, second_shift_grad = norm_back(
        second_back, second_norm, second_inv, second_gain
    )
    middle_back = result_back + middle_ln
    attend_low = middle_back.astype(BF)
    mixed_back = back_through(attend_low, output_near).astype(BF)
    output_grad = contract(mixed_flat, attend_low).reshape(parts, wide, width)
    output_grad = jnp.concatenate(
        [lax.dynamic_index_in_dim(output_grad, place ^ j, 0, keepdims=False) for j in range(parts)],
        axis=0,
    )
    half_width = width // 2
    output_half = lax.dynamic_slice_in_dim(output_grad, core * half_width, half_width, 1) + swap(
        lax.dynamic_slice_in_dim(output_grad, (1 - core) * half_width, half_width, 1).astype(BF),
        "chrom",
        1,
    ).astype(F32)
    output_out = scatter_columns_split(
        output_half.astype(BF), low_bits + [("cells", cell_bits - 1), ("chrom", 1)]
    )
    early = sum_all(jnp.stack([cls_total, cls_square, second_gain_grad, second_shift_grad]))

    mixed_back = mixed_back.reshape(cells_here, seq_here, width)
    heads_back = []
    for c in range(cells_here):
        pieces = [mixed_back[c, :, r * wide : (r + 1) * wide] for r in range(parts)]
        heads_back.append(
            [pieces[0]] + [swap(pieces[r], "chrom", r) for r in range(1, parts)]
        )
    qkv_grad = None
    first_back = []
    for c in range(cells_here):
        qkv_back = attend_back(heads_back[c], lens[c], kept[c], block)
        pieces = [back_through(g, qkv_weight) for g in qkv_back]
        sent = swap(jnp.stack([pieces[1].astype(BF), pieces[3].astype(BF)]), "chrom", 1).astype(F32)
        over = swap((pieces[2] + sent[1]).astype(BF), "chrom", 2)
        first_back.append(pieces[0] + sent[0] + over.astype(F32))
        part = contract(
            jnp.concatenate(first_all[c], axis=0), jnp.concatenate(qkv_back, axis=0)
        )
        qkv_grad = part if qkv_grad is None else qkv_grad + part
    first_back = jnp.concatenate(first_back, axis=0)

    names = [("cells", b) for b in reversed(range(cell_bits))]
    qkv_sum = scatter_rows(
        qkv_grad.reshape((2,) * cell_bits + (-1, 3 * wide)),
        [("cells", b) for b in range(cell_bits)],
        names,
    ).reshape(parts, -1, 3 * wide)
    pieces = [lax.dynamic_index_in_dim(qkv_sum, near[0], 0, keepdims=False)]
    for r in range(1, parts):
        piece = lax.dynamic_index_in_dim(qkv_sum, near[r], 0, keepdims=False).astype(BF)
        pieces.append(swap(piece, "chrom", r).astype(F32))
    pieces = jnp.stack(pieces)
    pieces = [lax.dynamic_index_in_dim(pieces, place ^ j, 0, keepdims=False) for j in range(parts)]
    query_out, key_out, value_out = [
        jnp.concatenate([p[:, i * wide : (i + 1) * wide] for p in pieces], axis=1) for i in range(3)
    ]

    first_ln, first_gain_grad, first_shift_grad = norm_back(
        first_back, first_norm, first_inv, first_gain
    )
    tokens_grad = (middle_back + first_ln).reshape(cells_here, seq_here, width)
    late = sum_all(jnp.stack([first_gain_grad, first_shift_grad]))

    count_cells = cells_here * lax.axis_size("cells")
    cls_mean = early[0] / count_cells
    cls_var = early[1] / count_cells - cls_mean * cls_mean
    share = width // (parts * lax.axis_size("cells"))
    start = (lax.axis_index("cells") * parts + place) * share

    def mine(vector):
        return lax.dynamic_slice_in_dim(vector, start, share, 0)

    return (
        layer_out,
        tokens_grad,
        mine(late[0]),
        mine(late[1]),
        query_out,
        key_out,
        value_out,
        output_out,
        mine(early[2]),
        mine(early[3]),
        up_out,
        down_out,
        cls_mean,
        cls_var,
    )


def solution(mesh):
    rows = P("cells", "chrom", None)
    both = ("cells", "chrom")
    in_specs = (rows, rows, P("cells", None), P("cells")) + (P(),) * 11
    out_specs = (
        (rows, rows)
        + (P(both), P(both))
        + (P(both, None),) * 4
        + (P(both), P(both))
        + (P(both, None), P(both, None))
        + (P(), P())
    )
    return jax.shard_map(
        per_device, mesh=mesh, in_specs=in_specs, out_specs=out_specs, check_vma=False
    )
```

time: 1690 us -> 657 us (0.39)
  waiting for transfers between devices: 1060 us -> 224 us
  matrix products: 367 us -> 47.7 us
  Pallas kernels: 0 us -> 199 us
  starting transfers between devices: 1.2 us -> 71.2 us
  other arithmetic: 101 us -> 52.4 us
  blocking collectives: 43.1 us -> 0 us
  local copies, waits for them, and re-layouts: 88.4 us -> 51.1 us
    reduce_scatter x8 -> x0, waiting for transfers between devices: 1040 us -> none  [the longest x1 286 us: per_device(): lax.psum_scatter(up_grad, ('cells', 'chrom'), scatter_dimension=0, tiled=...]
    dot_general x24 -> x18, matrix products: 367 us -> 47.7 us  [the longest x4 26.1 us: contract(): return lax.dot_general(left, right, TN, preferred_element_type=F32)]
    ppermute x0 -> x69, waiting for transfers between devices: none -> 224 us  [the longest x67 207 us: swap(): return lax.ppermute(x, axis, [(i, i ^ mask) for i in range(size)])]
    pallas_call x0 -> x7, Pallas kernels: none -> 199 us  [the longest x1 84.9 us: feed_forward(): pl.pallas_call(feed_kernel, grid_spec=pltpu.PrefetchScalarGridSpec(num_sc...]
    ppermute x0 -> x69, starting transfers between devices: none -> 71.2 us  [the longest x67 68.5 us: swap(): return lax.ppermute(x, axis, [(i, i ^ mask) for i in range(size)])]
    unnamed x1 -> x0, blocking collectives: 43.1 us -> none
    convert_element_type x6 -> x20, other arithmetic: 59.5 us -> 24.3 us  [the longest x10 12.9 us: scatter_rows(): x = halve(x.astype(BF), names.index(name), name[0], name[1])]
    all_gather x2 -> x0, waiting for transfers between devices: 27.1 us -> none  [the longest x1 27.1 us: per_device(): lax.all_gather(key_low.reshape(cells_here, seq_here, width), 'chrom', axi...]
  transfers between devices with their start and end apart: 10 -> 69, of which waited for: 8 -> 29; matrix products, arithmetic and copies ran while one was open for 20% -> 21% of each run, Pallas kernels for 0% -> 18%
where the time goes in v1:
time: 657 us; the launch traced here: 647 us
  waiting for transfers between devices  224 us (34%)
  Pallas kernels  199 us (30%)
  starting transfers between devices  71.2 us (11%)
  other arithmetic  52.4 us (8%)
  local copies, waits for them, and re-layouts  51.1 us (8%)
  matrix products  47.7 us (7%)
    ppermute x67, waiting for transfers between devices, swap(): return lax.ppermute(x, axis, [(i, i ^ mask) for i in range(size)])  207 us
    pallas_call x1, Pallas kernels, feed_forward(): pl.pallas_call(feed_kernel, grid_spec=pltpu.PrefetchScalarGridSpec(num_sc...  84.9 us
    ppermute x67, starting transfers between devices, swap(): return lax.ppermute(x, axis, [(i, i ^ mask) for i in range(size)])  68.5 us
    pallas_call x3, Pallas kernels, attend_back(): pl.pallas_call(functools.partial(attend_back_kernel, block, heads), in_sp...  61.8 us
    pallas_call x3, Pallas kernels, attend(): pl.pallas_call(functools.partial(attend_kernel, block, heads), in_specs=[...  52 us
    dot_general x4, matrix products, contract(): return lax.dot_general(left, right, TN, preferred_element_type=F32)  26.1 us
    dot_general x13, matrix products, back_through(): return lax.dot_general(grad, weight, NT, preferred_element_type=F32)  16.5 us
    squeeze x14, local copies, waits for them, and re-layouts, halve(): send = lax.dynamic_index_in_dim(x, 1 - mine, dim, keepdims=False)  14.1 us
  transfers between devices with their start and end apart: 69, of which 29 were waited for; matrix products, arithmetic and copies ran while one was open for 21% of the time, Pallas kernels for 18%

profile of v1, /device:TPU:1, one launch (start us, length us, event | category | flops | bytes accessed | tf_op | source)
XLA Modules:
  0.0 647.3 jit_solution(3820833318847855216)
XLA Ops:
  4.3 2.3 fusion.13
  18.6 2.8 constant_dynamic-slice_fusion.10
  21.8 3.1 collective-permute-done.1.refs_2_
  27.0 2.6 pad_maximum_fusion.3.refs_4_
  29.6 9.3 %collective-permute-done.7.refs_2_ = bf16[256,1280]{1,0:T(8,128)(2,1)} collective-permute-done((bf16[256,1280]{1,0:T(8,128)(2,1)}, bf16[256,1280]{1,0:T(8,128)(2,1)}, u32[]{:S(2)}, u32[]{:S(2)}) %collective-permute-start.7) | collective-permute-done | bytes 655392 | tf_op jit(solution)/shard_map/ppermute | solution.py:302
  41.5 11.5 %collective-permute-done.13.refs_2_ = bf16[256,1280]{1,0:T(8,128)(2,1)} collective-permute-done((bf16[256,1280]{1,0:T(8,128)(2,1)}, bf16[256,1280]{1,0:T(8,128)(2,1)}, u32[]{:S(2)}, u32[]{:S(2)}) %collective-permute-start.13) | collective-permute-done | bytes 655392 | tf_op jit(solution)/shard_map/ppermute | solution.py:302
  55.0 17.3 %attend.3 = (bf16[256,320]{1,0:T(8,128)(2,1)}, bf16[256,320]{1,0:T(8,128)(2,1)}, bf16[256,320]{1,0:T(8,128)(2,1)}, bf16[256,320]{1,0:T(8,128)(2,1)}, bf16[768,960]{1,0:T(8,128)(2,1)}) custom-call(s32[8]{0:T(128)} %get-tuple-element.144.lens, bf16[256,1280]{1,0:T(8,128)(2,1)} %get-tuple-element.114.refs_0_, bf16[256,1280]{1,0:T(8,128)(2,1)} %collective-permute-done.refs_1_, ...), custom_call_target="tpu_custom_call" | custom-call | flops 6543114240 | bytes 8000000 | tf_op jit(solution)/shard_map/attend/pallas_call | solution.py:110
  74.7 17.1 %attend.4 = (bf16[256,320]{1,0:T(8,128)(2,1)}, bf16[256,320]{1,0:T(8,128)(2,1)}, bf16[256,320]{1,0:T(8,128)(2,1)}, bf16[256,320]{1,0:T(8,128)(2,1)}, bf16[768,960]{1,0:T(8,128)(2,1)}) custom-call(s32[8]{0:T(128)} %get-tuple-element.146.lens, bf16[256,1280]{1,0:T(8,128)(2,1)} %get-tuple-element.116.refs_0_, bf16[256,1280]{1,0:T(8,128)(2,1)} %collective-permute-done.6.refs_1_, ...), custom_call_target="tpu_custom_call" | custom-call | flops 6543114240 | bytes 8000000 | tf_op jit(solution)/shard_map/attend/pallas_call | solution.py:110
  94.3 17.5 %attend.5 = (bf16[256,320]{1,0:T(8,128)(2,1)}, bf16[256,320]{1,0:T(8,128)(2,1)}, bf16[256,320]{1,0:T(8,128)(2,1)}, bf16[256,320]{1,0:T(8,128)(2,1)}, bf16[768,960]{1,0:T(8,128)(2,1)}) custom-call(s32[8]{0:T(128)} %get-tuple-element.145.lens, bf16[256,1280]{1,0:T(8,128)(2,1)} %get-tuple-element.115.refs_0_, bf16[256,1280]{1,0:T(8,128)(2,1)} %copy-done.62, ...), custom_call_target="tpu_custom_call" | custom-call | flops 6543114240 | bytes 8000000 | tf_op jit(solution)/shard_map/attend/pallas_call | solution.py:110
  121.2 2.4 collective-permute-done.17
  125.7 5.1 fusion.118
  132.9 3.9 collective-permute-done.18.second_b
  136.8 84.9 %feed_forward.1 = (f32[768,1280]{1,0:T(8,128)}, bf16[768,1280]{1,0:T(8,128)(2,1)}, f32[768,1280]{1,0:T(8,128)}, bf16[768,1280]{1,0:T(8,128)(2,1)}, bf16[2560,128...) custom-call(s32[1]{0:T(128)} %bitcast.4.half, bf16[768,1280]{1,0:T(8,128)(2,1)} %copy-done.27, ...), custom_call_target="tpu_custom_call" | custom-call | flops 60397977600 | bytes 60000000 | tf_op jit(solution)/shard_map/feed_forward/pallas_call | solution.py:263
  222.2 4.0 dynamic-slice_bitcast_fusion
  227.4 4.0 dynamic-slice_bitcast_fusion.1
  232.0 2.4 multiply_reduce_fusion
  235.3 3.5 bitcast_add_fusion
  239.7 4.3 convolution_convert_fusion
  244.1 2.8 fusion.83
  252.0 52.2 %collective-permute-done.55 = f32[4,1280]{1,0:T(4,128)S(1)} collective-permute-done((f32[4,1280]{1,0:T(4,128)S(1)}, f32[4,1280]{1,0:T(4,128)S(1)}, u32[]{:S(2)}, u32[]{:S(2)}) %collective-permute-start.55) | collective-permute-done | bytes 20512 | tf_op jit(solution)/shard_map/ppermute | solution.py:302
  309.9 2.4 collective-permute-start.58
  313.6 5.6 collective-permute-start.29
  326.4 20.6 %attend_back.4 = (bf16[256,960]{1,0:T(8,128)(2,1)}, bf16[256,960]{1,0:T(8,128)(2,1)}, bf16[256,960]{1,0:T(8,128)(2,1)}, bf16[256,960]{1,0:T(8,128)(2,1)}) custom-call(s32[8]{0:T(128)} %get-tuple-element.146.lens, bf16[256,320]{1,0:T(8,128)(2,1)} %get-tuple-element.110.refs_0_, bf16[256,320]{1,0:T(8,128)(2,1)} %copy-done.68, bf16[256,320]{1,0:T(8,128)(2,1)} %copy-done.69, ...), custom_call_target="tpu_custom_call" | custom-call | flops 7549747200 | bytes 6000000 | tf_op jit(solution)/shard_map/attend_back/pallas_call | solution.py:172
  347.0 7.1 %fusion.30 = f32[1280,960]{0,1:T(8,128)} fusion(bf16[256,1280]{1,0:T(8,128)(2,1)S(1)} %copy-done.67, bf16[256,1280]{1,0:T(8,128)(2,1)} %collective-permute-done.7.refs_2_, bf16[256,1280]{1,0:T(8,128)(2,1)} %collective-permute-done.6.refs_1_, bf16[256,1280]{1,0:T(8,128)(2,1)} %get-tuple-element.116.refs_0_, bf16[256,960]{1,0:T(8,128)(2,1)} %get-tuple-element.71, ...), kind=kOutput, calls=%fused_computation.66 | convolution fusion | flops 2534932480 | bytes 9502720 | tf_op jit(solution)/shard_map/dot_general | solution.py:395
  356.3 20.4 %attend_back.3 = (bf16[256,960]{1,0:T(8,128)(2,1)}, bf16[256,960]{1,0:T(8,128)(2,1)}, bf16[256,960]{1,0:T(8,128)(2,1)}, bf16[256,960]{1,0:T(8,128)(2,1)}) custom-call(s32[8]{0:T(128)} %get-tuple-element.144.lens, bf16[256,320]{1,0:T(8,128)(2,1)} %get-tuple-element.113.refs_0_, bf16[256,320]{1,0:T(8,128)(2,1)} %copy-done.70, bf16[256,320]{1,0:T(8,128)(2,1)} %copy-done.71, ...), custom_call_target="tpu_custom_call" | custom-call | flops 7549747200 | bytes 6000000 | tf_op jit(solution)/shard_map/attend_back/pallas_call | solution.py:172
  376.7 7.2 %fusion.22 = f32[1280,960]{0,1:T(8,128)} fusion(bf16[256,1280]{1,0:T(8,128)(2,1)S(1)} %copy-done.61, bf16[256,1280]{1,0:T(8,128)(2,1)} %collective-permute-done.1.refs_2_, bf16[256,1280]{1,0:T(8,128)(2,1)} %collective-permute-done.refs_1_, bf16[256,1280]{1,0:T(8,128)(2,1)} %get-tuple-element.114.refs_0_, bf16[256,960]{1,0:T(8,128)(2,1)} %get-tuple-element.66, ...), kind=kOutput, calls=%fused_computation.58 | convolution fusion | flops 2534932480 | bytes 9502720 | tf_op jit(solution)/shard_map/dot_general | solution.py:395
  384.7 20.8 %attend_back.5 = (bf16[256,960]{1,0:T(8,128)(2,1)}, bf16[256,960]{1,0:T(8,128)(2,1)}, bf16[256,960]{1,0:T(8,128)(2,1)}, bf16[256,960]{1,0:T(8,128)(2,1)}) custom-call(s32[8]{0:T(128)} %get-tuple-element.145.lens, bf16[256,320]{1,0:T(8,128)(2,1)} %get-tuple-element.106.refs_0_, bf16[256,320]{1,0:T(8,128)(2,1)} %copy-done.72, bf16[256,320]{1,0:T(8,128)(2,1)} %copy-done.74, ...), custom_call_target="tpu_custom_call" | custom-call | flops 7549747200 | bytes 6000000 | tf_op jit(solution)/shard_map/attend_back/pallas_call | solution.py:172
  405.5 9.1 %add_convert_fusion = bf16[1280,960]{0,1:T(8,128)(2,1)} fusion(f32[1280,960]{0,1:T(8,128)} %fusion.22, f32[1280,960]{0,1:T(8,128)} %fusion.30, bf16[256,1280]{1,0:T(8,128)(2,1)S(1)} %copy-done.65, bf16[256,1280]{1,0:T(8,128)(2,1)} %collective-permute-done.13.refs_2_, bf16[256,1280]{1,0:T(8,128)(2,1)S(1)} %copy-done.63, ...), kind=kOutput, calls=%fused_computation.5 | convolution fusion | flops 2538618880 | bytes 16875520 | tf_op jit(solution)/shard_map/dot_general | solution.py:395
  414.6 4.6 copy.34
  429.7 3.0 fusion.1
  433.3 3.2 fusion
  439.4 13.2 %collective-permute-done.42 = bf16[2,2,160,960]{3,2,1,0:T(8,128)(2,1)S(1)} collective-permute-done((bf16[2,2,160,960]{3,2,1,0:T(8,128)(2,1)}, bf16[2,2,160,960]{3,2,1,0:T(8,128)(2,1)S(1)}, u32[]{:S(2)}, u32[]{:S(2)}) %collective-permute-start.42) | collective-permute-done | bytes 1228832 | tf_op jit(solution)/shard_map/ppermute | solution.py:302
  467.3 6.9 %collective-permute-done.26 = bf16[256,1280]{1,0:T(8,128)(2,1)S(1)} collective-permute-done((bf16[256,1280]{1,0:T(8,128)(2,1)S(1)}, bf16[256,1280]{1,0:T(8,128)(2,1)S(1)}, u32[]{:S(2)}, u32[]{:S(2)}) %collective-permute-start.26) | collective-permute-done | bytes 655392 | tf_op jit(solution)/shard_map/ppermute | solution.py:302
  476.4 11.8 %collective-permute-done.31 = bf16[256,1280]{1,0:T(8,128)(2,1)S(1)} collective-permute-done((bf16[256,1280]{1,0:T(8,128)(2,1)S(1)}, bf16[256,1280]{1,0:T(8,128)(2,1)S(1)}, u32[]{:S(2)}, u32[]{:S(2)}) %collective-permute-start.31) | collective-permute-done | bytes 655392 | tf_op jit(solution)/shard_map/ppermute | solution.py:302
  489.5 12.8 %collective-permute-done.36 = bf16[256,1280]{1,0:T(8,128)(2,1)S(1)} collective-permute-done((bf16[256,1280]{1,0:T(8,128)(2,1)S(1)}, bf16[256,1280]{1,0:T(8,128)(2,1)S(1)}, u32[]{:S(2)}, u32[]{:S(2)}) %collective-permute-start.36) | collective-permute-done | bytes 655392 | tf_op jit(solution)/shard_map/ppermute | solution.py:302
  506.9 3.0 collective-permute-start.37
  509.9 28.0 %collective-permute-done.43 = bf16[2,160,960]{2,1,0:T(8,128)(2,1)S(1)} collective-permute-done((bf16[2,160,960]{2,1,0:T(8,128)(2,1)S(1)}, bf16[2,160,960]{2,1,0:T(8,128)(2,1)S(1)}, u32[]{:S(2)}, u32[]{:S(2)}) %collective-permute-start.43) | collective-permute-done | bytes 614432 | tf_op jit(solution)/shard_map/ppermute | solution.py:302
  550.2 4.8 fusion.16
  555.0 2.8 collective-permute-done.41
  562.9 2.5 collective-permute-done.47
  574.7 6.2 collective-permute-done.50
  585.2 7.3 %collective-permute-done.51 = bf16[2,80,640]{2,1,0:T(8,128)(2,1)S(1)} collective-permute-done((bf16[2,80,640]{2,1,0:T(8,128)(2,1)S(1)}, bf16[2,80,640]{2,1,0:T(8,128)(2,1)S(1)}, u32[]{:S(2)}, u32[]{:S(2)}) %collective-permute-start.51) | collective-permute-done | bytes 204832 | tf_op jit(solution)/shard_map/ppermute | solution.py:302
  596.4 2.3 collective-permute-start.53
  599.7 3.4 collective-permute-done.61
  604.8 14.0 %collective-permute-done.66 = bf16[320,1280]{1,0:T(8,128)(2,1)S(1)} collective-permute-done((bf16[320,1280]{1,0:T(8,128)(2,1)S(1)}, bf16[320,1280]{1,0:T(8,128)(2,1)S(1)}, u32[]{:S(2)}, u32[]{:S(2)}) %collective-permute-start.66) | collective-permute-done | bytes 819232 | tf_op jit(solution)/shard_map/ppermute | solution.py:302
  620.3 3.6 collective-permute-done.62
  626.4 3.2 collective-permute-done.67
  632.3 13.6 %collective-permute-done.68 = bf16[160,1280]{1,0:T(8,128)(2,1)S(1)} collective-permute-done((bf16[160,1280]{1,0:T(8,128)(2,1)S(1)}, bf16[160,1280]{1,0:T(8,128)(2,1)S(1)}, u32[]{:S(2)}, u32[]{:S(2)}) %collective-permute-start.68) | collective-permute-done | bytes 409632 | tf_op jit(solution)/shard_map/ppermute | solution.py:373
  (429 shorter events, 148.2 us)
Async XLA Ops:
  8.0 16.9 %collective-permute-start.1 = (bf16[256,1280]{1,0:T(8,128)(2,1)}, bf16[256,1280]{1,0:T(8,128)(2,1)}, u32[]{:S(2)}, u32[]{:S(2)}) collective-permute-start(bf16[256,1280]{1,0:T(8,128)(2,1)} %get-tuple-element.114.refs_0_), channel_id=1, source_target_pairs={{0,2},{1,3},{2,0},{3,1},{4,6},{5,7},{6,4},{7,5},{8,10},{9,11},{10,... | collective-permute-start | bytes 1966088 | tf_op jit(solution)/shard_map/ppermute | solution.py:302
  10.1 31.4 %collective-permute-start = (bf16[256,1280]{1,0:T(8,128)(2,1)}, bf16[256,1280]{1,0:T(8,128)(2,1)}, u32[]{:S(2)}, u32[]{:S(2)}) collective-permute-start(bf16[256,1280]{1,0:T(8,128)(2,1)} %get-tuple-element.114.refs_0_), channel_id=1, source_target_pairs={{0,1},{1,0},{2,3},{3,2},{4,5},{5,4},{6,7},{7,6},{8,9},{9,8},{10,11... | collective-permute-start | bytes 1966088 | tf_op jit(solution)/shard_map/ppermute | solution.py:302
  11.0 27.9 %collective-permute-start.7 = (bf16[256,1280]{1,0:T(8,128)(2,1)}, bf16[256,1280]{1,0:T(8,128)(2,1)}, u32[]{:S(2)}, u32[]{:S(2)}) collective-permute-start(bf16[256,1280]{1,0:T(8,128)(2,1)} %get-tuple-element.116.refs_0_), channel_id=1, source_target_pairs={{0,2},{1,3},{2,0},{3,1},{4,6},{5,7},{6,4},{7,5},{8,10},{9,11},{10,... | collective-permute-start | bytes 1966088 | tf_op jit(solution)/shard_map/ppermute | solution.py:302
  11.0 61.3 %collective-permute-start.6 = (bf16[256,1280]{1,0:T(8,128)(2,1)}, bf16[256,1280]{1,0:T(8,128)(2,1)}, u32[]{:S(2)}, u32[]{:S(2)}) collective-permute-start(bf16[256,1280]{1,0:T(8,128)(2,1)} %get-tuple-element.116.refs_0_), channel_id=1, source_target_pairs={{0,1},{1,0},{2,3},{3,2},{4,5},{5,4},{6,7},{7,6},{8,9},{9,8},{10,11... | collective-permute-start | bytes 1966088 | tf_op jit(solution)/shard_map/ppermute | solution.py:302
  11.2 41.7 %collective-permute-start.13 = (bf16[256,1280]{1,0:T(8,128)(2,1)}, bf16[256,1280]{1,0:T(8,128)(2,1)}, u32[]{:S(2)}, u32[]{:S(2)}) collective-permute-start(bf16[256,1280]{1,0:T(8,128)(2,1)} %get-tuple-element.115.refs_0_), channel_id=1, source_target_pairs={{0,2},{1,3},{2,0},{3,1},{4,6},{5,7},{6,4},{7,5},{8,10},{9,11},{10,... | collective-permute-start | bytes 1966088 | tf_op jit(solution)/shard_map/ppermute | solution.py:302
  24.9 29.3 %collective-permute-start.2 = (bf16[256,1280]{1,0:T(8,128)(2,1)}, bf16[256,1280]{1,0:T(8,128)(2,1)S(1)}, u32[]{:S(2)}, u32[]{:S(2)}) collective-permute-start(bf16[256,1280]{1,0:T(8,128)(2,1)} %collective-permute-done.1.refs_2_), channel_id=1, source_target_pairs={{0,1},{1,0},{2,3},{3,2},{4,5},{5,4},{6,7},{7,6},{8,9},{9,8},{10,11... | collective-permute-start | bytes 1966088 | tf_op jit(solution)/shard_map/ppermute | solution.py:302
  38.9 35.0 %collective-permute-start.8 = (bf16[256,1280]{1,0:T(8,128)(2,1)}, bf16[256,1280]{1,0:T(8,128)(2,1)S(1)}, u32[]{:S(2)}, u32[]{:S(2)}) collective-permute-start(bf16[256,1280]{1,0:T(8,128)(2,1)} %collective-permute-done.7.refs_2_), channel_id=1, source_target_pairs={{0,1},{1,0},{2,3},{3,2},{4,5},{5,4},{6,7},{7,6},{8,9},{9,8},{10,11... | collective-permute-start | bytes 1966088 | tf_op jit(solution)/shard_map/ppermute | solution.py:302
  41.5 50.4 %collective-permute-start.12 = (bf16[256,1280]{1,0:T(8,128)(2,1)}, bf16[256,1280]{1,0:T(8,128)(2,1)S(1)}, u32[]{:S(2)}, u32[]{:S(2)}) collective-permute-start(bf16[256,1280]{1,0:T(8,128)(2,1)} %get-tuple-element.115.refs_0_), channel_id=1, source_target_pairs={{0,1},{1,0},{2,3},{3,2},{4,5},{5,4},{6,7},{7,6},{8,9},{9,8},{10,11... | collective-permute-start | bytes 1966088 | tf_op jit(solution)/shard_map/ppermute | solution.py:302
  53.0 40.2 %collective-permute-start.14 = (bf16[256,1280]{1,0:T(8,128)(2,1)}, bf16[256,1280]{1,0:T(8,128)(2,1)S(1)}, u32[]{:S(2)}, u32[]{:S(2)}) collective-permute-start(bf16[256,1280]{1,0:T(8,128)(2,1)} %collective-permute-done.13.refs_2_), channel_id=1, source_target_pairs={{0,1},{1,0},{2,3},{3,2},{4,5},{5,4},{6,7},{7,6},{8,9},{9,8},{10,11... | collective-permute-start | bytes 1966088 | tf_op jit(solution)/shard_map/ppermute | solution.py:302
  72.3 39.5 %collective-permute-start.3 = (bf16[256,320]{1,0:T(8,128)(2,1)}, bf16[256,320]{1,0:T(8,128)(2,1)S(1)}, u32[]{:S(2)}, u32[]{:S(2)}) collective-permute-start(bf16[256,320]{1,0:T(8,128)(2,1)} %get-tuple-element.48), channel_id=1, source_target_pairs={{0,1},{1,0},{2,3},{3,2},{4,5},{5,4},{6,7},{7,6},{8,9},{9,8},{10,11... | collective-permute-start | bytes 491528 | tf_op jit(solution)/shard_map/ppermute | solution.py:302
  72.3 39.6 %collective-permute-start.4 = (bf16[256,320]{1,0:T(8,128)(2,1)}, bf16[256,320]{1,0:T(8,128)(2,1)S(1)}, u32[]{:S(2)}, u32[]{:S(2)}) collective-permute-start(bf16[256,320]{1,0:T(8,128)(2,1)} %get-tuple-element.49), channel_id=1, source_target_pairs={{0,2},{1,3},{2,0},{3,1},{4,6},{5,7},{6,4},{7,5},{8,10},{9,11},{10,... | collective-permute-start | bytes 491528 | tf_op jit(solution)/shard_map/ppermute | solution.py:302
  73.9 38.5 %collective-permute-start.5 = (bf16[256,320]{1,0:T(8,128)(2,1)}, bf16[256,320]{1,0:T(8,128)(2,1)S(1)}, u32[]{:S(2)}, u32[]{:S(2)}) collective-permute-start(bf16[256,320]{1,0:T(8,128)(2,1)} %get-tuple-element.50), channel_id=1, source_target_pairs={{0,3},{1,2},{2,1},{3,0},{4,7},{5,6},{6,5},{7,4},{8,11},{9,10},{10,... | collective-permute-start | bytes 491528 | tf_op jit(solution)/shard_map/ppermute | solution.py:302
  91.9 21.1 %collective-permute-start.10 = (bf16[256,320]{1,0:T(8,128)(2,1)}, bf16[256,320]{1,0:T(8,128)(2,1)S(1)}, u32[]{:S(2)}, u32[]{:S(2)}) collective-permute-start(bf16[256,320]{1,0:T(8,128)(2,1)} %get-tuple-element.53), channel_id=1, source_target_pairs={{0,2},{1,3},{2,0},{3,1},{4,6},{5,7},{6,4},{7,5},{8,10},{9,11},{10,... | collective-permute-start | bytes 491528 | tf_op jit(solution)/shard_map/ppermute | solution.py:302
  93.2 25.7 %collective-permute-start.11 = (bf16[256,320]{1,0:T(8,128)(2,1)}, bf16[256,320]{1,0:T(8,128)(2,1)}, u32[]{:S(2)}, u32[]{:S(2)}) collective-permute-start(bf16[256,320]{1,0:T(8,128)(2,1)} %get-tuple-element.54), channel_id=1, source_target_pairs={{0,3},{1,2},{2,1},{3,0},{4,7},{5,6},{6,5},{7,4},{8,11},{9,10},{10,... | collective-permute-start | bytes 491528 | tf_op jit(solution)/shard_map/ppermute | solution.py:302
  118.9 14.0 %collective-permute-start.19 = (bf16[768,1280]{1,0:T(8,128)(2,1)}, bf16[768,1280]{1,0:T(8,128)(2,1)}, u32[]{:S(2)}, u32[]{:S(2)}) collective-permute-start(bf16[768,1280]{1,0:T(8,128)(2,1)} %bitcast_convert_fusion.low_a), channel_id=1, source_target_pairs={{0,1},{1,0},{2,3},{3,2},{4,5},{5,4},{6,7},{7,6},{8,9},{9,8},{10,11... | collective-permute-start | bytes 5898248 | tf_op jit(solution)/shard_map/ppermute | solution.py:302
  221.9 12.6 %collective-permute-start.20 = (bf16[768,1280]{1,0:T(8,128)(2,1)}, bf16[768,1280]{1,0:T(8,128)(2,1)}, u32[]{:S(2)}, u32[]{:S(2)}) collective-permute-start(bf16[768,1280]{1,0:T(8,128)(2,1)} %get-tuple-element.60), channel_id=1, source_target_pairs={{0,1},{1,0},{2,3},{3,2},{4,5},{5,4},{6,7},{7,6},{8,9},{9,8},{10,11... | collective-permute-start | bytes 5898248 | tf_op jit(solution)/shard_map/ppermute | solution.py:302
  226.2 206.4 %collective-permute-start.64 = (bf16[2,2,320,1280]{3,2,1,0:T(8,128)(2,1)}, bf16[2,2,320,1280]{3,2,1,0:T(8,128)(2,1)}, u32[]{:S(2)}, u32[]{:S(2)}) collective-permute-start(bf16[2,2,320,1280]{3,2,1,0:T(8,128)(2,1)} %dynamic-slice_bitcast_fusion), channel_id=1, source_target_pairs={{0,4},{4,0},{8,12},{12,8},{16,20},{20,16},{24,28},{28,24},{1,5},{5... | collective-permute-start | bytes 9830408 | tf_op jit(solution)/shard_map/ppermute | solution.py:302
  231.4 198.1 %collective-permute-start.59 = (bf16[2,2,2,80,2560]{4,3,2,1,0:T(8,128)(2,1)}, bf16[2,2,2,80,2560]{4,3,2,1,0:T(8,128)(2,1)}, u32[]{:S(2)}, u32[]{:S(2)}) collective-permute-start(bf16[2,2,2,80,2560]{4,3,2,1,0:T(8,128)(2,1)} %dynamic-slice_bitcast_fusion.1), channel_id=1, source_target_pairs={{0,2},{1,3},{2,0},{3,1},{4,6},{5,7},{6,4},{7,5},{8,10},{9,11},{10,... | collective-permute-start | bytes 9830408 | tf_op jit(solution)/shard_map/ppermute | solution.py:302
  247.0 57.2 %collective-permute-start.55 = (f32[4,1280]{1,0:T(4,128)S(1)}, f32[4,1280]{1,0:T(4,128)S(1)}, u32[]{:S(2)}, u32[]{:S(2)}) collective-permute-start(f32[4,1280]{1,0:T(4,128)S(1)} %fusion.110), channel_id=1, source_target_pairs={{0,2},{1,3},{2,0},{3,1},{4,6},{5,7},{6,4},{7,5},{8,10},{9,11},{10,... | collective-permute-start | bytes 61448 | tf_op jit(solution)/shard_map/ppermute | solution.py:302
  250.8 70.3 %collective-permute-start.27 = (bf16[256,320]{1,0:T(8,128)(2,1)S(1)}, bf16[256,320]{1,0:T(8,128)(2,1)S(1)}, u32[]{:S(2)}, u32[]{:S(2)}) collective-permute-start(bf16[256,320]{1,0:T(8,128)(2,1)S(1)} %get-tuple-element.109), channel_id=1, source_target_pairs={{0,1},{1,0},{2,3},{3,2},{4,5},{5,4},{6,7},{7,6},{8,9},{9,8},{10,11... | collective-permute-start | bytes 491528 | tf_op jit(solution)/shard_map/ppermute | solution.py:302
  251.5 69.6 %collective-permute-start.28 = (bf16[256,320]{1,0:T(8,128)(2,1)S(1)}, bf16[256,320]{1,0:T(8,128)(2,1)S(1)}, u32[]{:S(2)}, u32[]{:S(2)}) collective-permute-start(bf16[256,320]{1,0:T(8,128)(2,1)S(1)} %get-tuple-element.108), channel_id=1, source_target_pairs={{0,2},{1,3},{2,0},{3,1},{4,6},{5,7},{6,4},{7,5},{8,10},{9,11},{10,... | collective-permute-start | bytes 491528 | tf_op jit(solution)/shard_map/ppermute | solution.py:302
  321.0 33.1 %collective-permute-start.22 = (bf16[256,320]{1,0:T(8,128)(2,1)}, bf16[256,320]{1,0:T(8,128)(2,1)S(1)}, u32[]{:S(2)}, u32[]{:S(2)}) collective-permute-start(bf16[256,320]{1,0:T(8,128)(2,1)} %get-tuple-element.112), channel_id=1, source_target_pairs={{0,1},{1,0},{2,3},{3,2},{4,5},{5,4},{6,7},{7,6},{8,9},{9,8},{10,11... | collective-permute-start | bytes 491528 | tf_op jit(solution)/shard_map/ppermute | solution.py:302
  321.1 33.2 %collective-permute-start.23 = (bf16[256,320]{1,0:T(8,128)(2,1)}, bf16[256,320]{1,0:T(8,128)(2,1)S(1)}, u32[]{:S(2)}, u32[]{:S(2)}) collective-permute-start(bf16[256,320]{1,0:T(8,128)(2,1)} %get-tuple-element.111), channel_id=1, source_target_pairs={{0,2},{1,3},{2,0},{3,1},{4,6},{5,7},{6,4},{7,5},{8,10},{9,11},{10,... | collective-permute-start | bytes 491528 | tf_op jit(solution)/shard_map/ppermute | solution.py:302
  324.1 30.8 %collective-permute-start.24 = (bf16[256,320]{1,0:T(8,128)(2,1)S(1)}, bf16[256,320]{1,0:T(8,128)(2,1)S(1)}, u32[]{:S(2)}, u32[]{:S(2)}) collective-permute-start(bf16[256,320]{1,0:T(8,128)(2,1)S(1)} %get-tuple-element.102), channel_id=1, source_target_pairs={{0,3},{1,2},{2,1},{3,0},{4,7},{5,6},{6,5},{7,4},{8,11},{9,10},{10,... | collective-permute-start | bytes 491528 | tf_op jit(solution)/shard_map/ppermute | solution.py:302
  354.1 29.7 %collective-permute-start.32 = (bf16[256,320]{1,0:T(8,128)(2,1)S(1)}, bf16[256,320]{1,0:T(8,128)(2,1)S(1)}, u32[]{:S(2)}, u32[]{:S(2)}) collective-permute-start(bf16[256,320]{1,0:T(8,128)(2,1)S(1)} %get-tuple-element.105), channel_id=1, source_target_pairs={{0,1},{1,0},{2,3},{3,2},{4,5},{5,4},{6,7},{7,6},{8,9},{9,8},{10,11... | collective-permute-start | bytes 491528 | tf_op jit(solution)/shard_map/ppermute | solution.py:302
  354.2 29.6 %collective-permute-start.33 = (bf16[256,320]{1,0:T(8,128)(2,1)S(1)}, bf16[256,320]{1,0:T(8,128)(2,1)S(1)}, u32[]{:S(2)}, u32[]{:S(2)}) collective-permute-start(bf16[256,320]{1,0:T(8,128)(2,1)S(1)} %get-tuple-element.104), channel_id=1, source_target_pairs={{0,2},{1,3},{2,0},{3,1},{4,6},{5,7},{6,4},{7,5},{8,10},{9,11},{10,... | collective-permute-start | bytes 491528 | tf_op jit(solution)/shard_map/ppermute | solution.py:302
  354.9 29.0 %collective-permute-start.34 = (bf16[256,320]{1,0:T(8,128)(2,1)S(1)}, bf16[256,320]{1,0:T(8,128)(2,1)S(1)}, u32[]{:S(2)}, u32[]{:S(2)}) collective-permute-start(bf16[256,320]{1,0:T(8,128)(2,1)S(1)} %get-tuple-element.103), channel_id=1, source_target_pairs={{0,3},{1,2},{2,1},{3,0},{4,7},{5,6},{6,5},{7,4},{8,11},{9,10},{10,... | collective-permute-start | bytes 491528 | tf_op jit(solution)/shard_map/ppermute | solution.py:302
  383.9 79.5 %collective-permute-start.48 = (bf16[1280,640]{1,0:T(8,128)(2,1)}, bf16[1280,640]{1,0:T(8,128)(2,1)}, u32[]{:S(2)}, u32[]{:S(2)}) collective-permute-start(bf16[1280,640]{1,0:T(8,128)(2,1)} %dynamic-slice_convert_fusion), channel_id=1, source_target_pairs={{0,1},{1,0},{2,3},{3,2},{4,5},{5,4},{6,7},{7,6},{8,9},{9,8},{10,11... | collective-permute-start | bytes 4915208 | tf_op jit(solution)/shard_map/ppermute | solution.py:302
  422.5 30.1 %collective-permute-start.42 = (bf16[2,2,160,960]{3,2,1,0:T(8,128)(2,1)}, bf16[2,2,160,960]{3,2,1,0:T(8,128)(2,1)S(1)}, u32[]{:S(2)}, u32[]{:S(2)}) collective-permute-start(bf16[2,2,160,960]{3,2,1,0:T(8,128)(2,1)} %dynamic-slice_bitcast_fusion.8), channel_id=1, source_target_pairs={{0,4},{4,0},{8,12},{12,8},{16,20},{20,16},{24,28},{28,24},{1,5},{5... | collective-permute-start | bytes 3686408 | tf_op jit(solution)/shard_map/ppermute | solution.py:302
  423.8 30.6 %collective-permute-start.25 = (bf16[2,256,1280]{2,1,0:T(8,128)(2,1)S(1)}, bf16[2,256,1280]{2,1,0:T(8,128)(2,1)}, u32[]{:S(2)}, u32[]{:S(2)}) collective-permute-start(bf16[2,256,1280]{2,1,0:T(8,128)(2,1)S(1)} %pad_maximum_fusion.5), channel_id=1, source_target_pairs={{0,1},{1,0},{2,3},{3,2},{4,5},{5,4},{6,7},{7,6},{8,9},{9,8},{10,11... | collective-permute-start | bytes 3932168 | tf_op jit(solution)/shard_map/ppermute | solution.py:302
  429.6 26.7 %collective-permute-start.30 = (bf16[2,256,1280]{2,1,0:T(8,128)(2,1)}, bf16[2,256,1280]{2,1,0:T(8,128)(2,1)}, u32[]{:S(2)}, u32[]{:S(2)}) collective-permute-start(bf16[2,256,1280]{2,1,0:T(8,128)(2,1)} %pad_maximum_fusion.6), channel_id=1, source_target_pairs={{0,1},{1,0},{2,3},{3,2},{4,5},{5,4},{6,7},{7,6},{8,9},{9,8},{10,11... | collective-permute-start | bytes 3932168 | tf_op jit(solution)/shard_map/ppermute | solution.py:302
  432.7 27.3 %collective-permute-start.35 = (bf16[2,256,1280]{2,1,0:T(8,128)(2,1)S(1)}, bf16[2,256,1280]{2,1,0:T(8,128)(2,1)S(1)}, u32[]{:S(2)}, u32[]{:S(2)}) collective-permute-start(bf16[2,256,1280]{2,1,0:T(8,128)(2,1)S(1)} %pad_maximum_fusion.7), channel_id=1, source_target_pairs={{0,1},{1,0},{2,3},{3,2},{4,5},{5,4},{6,7},{7,6},{8,9},{9,8},{10,11... | collective-permute-start | bytes 3932168 | tf_op jit(solution)/shard_map/ppermute | solution.py:302
  452.6 140.0 %collective-permute-start.65 = (bf16[2,320,1280]{2,1,0:T(8,128)(2,1)}, bf16[2,320,1280]{2,1,0:T(8,128)(2,1)}, u32[]{:S(2)}, u32[]{:S(2)}) collective-permute-start(bf16[2,320,1280]{2,1,0:T(8,128)(2,1)} %dynamic-slice_bitcast_fusion.2), channel_id=1, source_target_pairs={{0,8},{4,12},{8,0},{12,4},{16,24},{20,28},{24,16},{28,20},{1,9},{5... | collective-permute-start | bytes 4915208 | tf_op jit(solution)/shard_map/ppermute | solution.py:302
  454.4 128.0 %collective-permute-start.60 = (bf16[2,2,80,2560]{3,2,1,0:T(8,128)(2,1)}, bf16[2,2,80,2560]{3,2,1,0:T(8,128)(2,1)}, u32[]{:S(2)}, u32[]{:S(2)}) collective-permute-start(bf16[2,2,80,2560]{3,2,1,0:T(8,128)(2,1)} %dynamic-slice_bitcast_fusion.3), channel_id=1, source_target_pairs={{0,8},{4,12},{8,0},{12,4},{16,24},{20,28},{24,16},{28,20},{1,9},{5... | collective-permute-start | bytes 4915208 | tf_op jit(solution)/shard_map/ppermute | solution.py:302
  456.3 81.7 %collective-permute-start.43 = (bf16[2,160,960]{2,1,0:T(8,128)(2,1)S(1)}, bf16[2,160,960]{2,1,0:T(8,128)(2,1)S(1)}, u32[]{:S(2)}, u32[]{:S(2)}) collective-permute-start(bf16[2,160,960]{2,1,0:T(8,128)(2,1)S(1)} %dynamic-slice_bitcast_fusion.12), channel_id=1, source_target_pairs={{0,8},{4,12},{8,0},{12,4},{16,24},{20,28},{24,16},{28,20},{1,9},{5... | collective-permute-start | bytes 1843208 | tf_op jit(solution)/shard_map/ppermute | solution.py:302
  460.0 14.3 %collective-permute-start.26 = (bf16[256,1280]{1,0:T(8,128)(2,1)S(1)}, bf16[256,1280]{1,0:T(8,128)(2,1)S(1)}, u32[]{:S(2)}, u32[]{:S(2)}) collective-permute-start(bf16[256,1280]{1,0:T(8,128)(2,1)S(1)} %fusion.49), channel_id=1, source_target_pairs={{0,2},{1,3},{2,0},{3,1},{4,6},{5,7},{6,4},{7,5},{8,10},{9,11},{10,... | collective-permute-start | bytes 1966088 | tf_op jit(solution)/shard_map/ppermute | solution.py:302
  463.3 24.9 %collective-permute-start.31 = (bf16[256,1280]{1,0:T(8,128)(2,1)S(1)}, bf16[256,1280]{1,0:T(8,128)(2,1)S(1)}, u32[]{:S(2)}, u32[]{:S(2)}) collective-permute-start(bf16[256,1280]{1,0:T(8,128)(2,1)S(1)} %fusion.50), channel_id=1, source_target_pairs={{0,2},{1,3},{2,0},{3,1},{4,6},{5,7},{6,4},{7,5},{8,10},{9,11},{10,... | collective-permute-start | bytes 1966088 | tf_op jit(solution)/shard_map/ppermute | solution.py:302
  474.2 28.1 %collective-permute-start.36 = (bf16[256,1280]{1,0:T(8,128)(2,1)S(1)}, bf16[256,1280]{1,0:T(8,128)(2,1)S(1)}, u32[]{:S(2)}, u32[]{:S(2)}) collective-permute-start(bf16[256,1280]{1,0:T(8,128)(2,1)S(1)} %fusion.51), channel_id=1, source_target_pairs={{0,2},{1,3},{2,0},{3,1},{4,6},{5,7},{6,4},{7,5},{8,10},{9,11},{10,... | collective-permute-start | bytes 1966088 | tf_op jit(solution)/shard_map/ppermute | solution.py:302
  488.3 79.9 %collective-permute-start.49 = (bf16[2,2,2,80,640]{4,3,2,1,0:T(8,128)(2,1)}, bf16[2,2,2,80,640]{4,3,2,1,0:T(8,128)(2,1)}, u32[]{:S(2)}, u32[]{:S(2)}) collective-permute-start(bf16[2,2,2,80,640]{4,3,2,1,0:T(8,128)(2,1)} %dynamic-slice_bitcast_fusion.11), channel_id=1, source_target_pairs={{0,4},{4,0},{8,12},{12,8},{16,20},{20,16},{24,28},{28,24},{1,5},{5... | collective-permute-start | bytes 2457608 | tf_op jit(solution)/shard_map/ppermute | solution.py:302
  506.9 31.3 %collective-permute-start.37 = (f32[2,1280]{1,0:T(2,128)S(1)}, f32[2,1280]{1,0:T(2,128)S(1)}, u32[]{:S(2)}, u32[]{:S(2)}) collective-permute-start(f32[2,1280]{1,0:T(2,128)S(1)} %pad_maximum_fusion.16), channel_id=1, source_target_pairs={{0,1},{1,0},{2,3},{3,2},{4,5},{5,4},{6,7},{7,6},{8,9},{9,8},{10,11... | collective-permute-start | bytes 30728 | tf_op jit(solution)/shard_map/ppermute | solution.py:302
  540.5 18.6 %collective-permute-start.44 = (bf16[160,960]{1,0:T(8,128)(2,1)}, bf16[160,960]{1,0:T(8,128)(2,1)}, u32[]{:S(2)}, u32[]{:S(2)}) collective-permute-start(bf16[160,960]{1,0:T(8,128)(2,1)} %dynamic-slice_bitcast_fusion.15), channel_id=1, source_target_pairs={{0,16},{4,20},{8,24},{12,28},{16,0},{20,4},{24,8},{28,12},{1,17},{... | collective-permute-start | bytes 921608 | tf_op jit(solution)/shard_map/ppermute | solution.py:302
  569.5 11.3 %collective-permute-start.50 = (bf16[2,2,80,640]{3,2,1,0:T(8,128)(2,1)S(1)}, bf16[2,2,80,640]{3,2,1,0:T(8,128)(2,1)S(1)}, u32[]{:S(2)}, u32[]{:S(2)}) collective-permute-start(bf16[2,2,80,640]{3,2,1,0:T(8,128)(2,1)S(1)} %dynamic-slice_bitcast_fusion.14), channel_id=1, source_target_pairs={{0,8},{4,12},{8,0},{12,4},{16,24},{20,28},{24,16},{28,20},{1,9},{5... | collective-permute-start | bytes 1228808 | tf_op jit(solution)/shard_map/ppermute | solution.py:302
  581.0 11.4 %collective-permute-start.51 = (bf16[2,80,640]{2,1,0:T(8,128)(2,1)S(1)}, bf16[2,80,640]{2,1,0:T(8,128)(2,1)S(1)}, u32[]{:S(2)}, u32[]{:S(2)}) collective-permute-start(bf16[2,80,640]{2,1,0:T(8,128)(2,1)S(1)} %dynamic-slice_bitcast_fusion.16), channel_id=1, source_target_pairs={{0,16},{4,20},{8,24},{12,28},{16,0},{20,4},{24,8},{28,12},{1,17},{... | collective-permute-start | bytes 614408 | tf_op jit(solution)/shard_map/ppermute | solution.py:302
  584.8 18.3 %collective-permute-start.61 = (bf16[2,80,2560]{2,1,0:T(8,128)(2,1)S(1)}, bf16[2,80,2560]{2,1,0:T(8,128)(2,1)S(1)}, u32[]{:S(2)}, u32[]{:S(2)}) collective-permute-start(bf16[2,80,2560]{2,1,0:T(8,128)(2,1)S(1)} %dynamic-slice_bitcast_fusion.10), channel_id=1, source_target_pairs={{0,4},{4,0},{8,12},{12,8},{16,20},{20,16},{24,28},{28,24},{1,5},{5... | collective-permute-start | bytes 2457608 | tf_op jit(solution)/shard_map/ppermute | solution.py:302
  598.8 19.9 %collective-permute-start.66 = (bf16[320,1280]{1,0:T(8,128)(2,1)S(1)}, bf16[320,1280]{1,0:T(8,128)(2,1)S(1)}, u32[]{:S(2)}, u32[]{:S(2)}) collective-permute-start(bf16[320,1280]{1,0:T(8,128)(2,1)S(1)} %dynamic-slice_bitcast_fusion.9), channel_id=1, source_target_pairs={{0,2},{1,3},{2,0},{3,1},{4,6},{5,7},{6,4},{7,5},{8,10},{9,11},{10,... | collective-permute-start | bytes 2457608 | tf_op jit(solution)/shard_map/ppermute | solution.py:302
  603.4 20.5 %collective-permute-start.62 = (bf16[80,2560]{1,0:T(8,128)(2,1)S(1)}, bf16[80,2560]{1,0:T(8,128)(2,1)S(1)}, u32[]{:S(2)}, u32[]{:S(2)}) collective-permute-start(bf16[80,2560]{1,0:T(8,128)(2,1)S(1)} %dynamic-slice_bitcast_fusion.13), channel_id=1, source_target_pairs={{0,16},{4,20},{8,24},{12,28},{16,0},{20,4},{24,8},{28,12},{1,17},{... | collective-permute-start | bytes 1228808 | tf_op jit(solution)/shard_map/ppermute | solution.py:302
  619.0 10.6 %collective-permute-start.67 = (bf16[320,1280]{1,0:T(8,128)(2,1)S(1)}, bf16[320,1280]{1,0:T(8,128)(2,1)S(1)}, u32[]{:S(2)}, u32[]{:S(2)}) collective-permute-start(bf16[320,1280]{1,0:T(8,128)(2,1)S(1)} %fusion.81), channel_id=1, source_target_pairs={{1,17},{3,19},{5,21},{7,23},{9,25},{11,27},{13,29},{15,31},{16,0},... | collective-permute-start | bytes 2457608 | tf_op jit(solution)/shard_map/ppermute | solution.py:364
  629.9 16.0 %collective-permute-start.68 = (bf16[160,1280]{1,0:T(8,128)(2,1)S(1)}, bf16[160,1280]{1,0:T(8,128)(2,1)S(1)}, u32[]{:S(2)}, u32[]{:S(2)}) collective-permute-start(bf16[160,1280]{1,0:T(8,128)(2,1)S(1)} %fusion.87), channel_id=1, source_target_pairs={{0,1},{2,3},{4,5},{6,7},{8,9},{10,11},{12,13},{14,15},{17,16},{19,... | collective-permute-start | bytes 1228808 | tf_op jit(solution)/shard_map/ppermute | solution.py:373
  (111 other events, 807.9 us)

commit v2 on v1

--- a/solution.py
+++ b/solution.py
@@ -19,6 +19,7 @@
 NT = (((1,), (1,)), ((), ()))
 TN = (((0,), (0,)), ((), ()))
 VMEM_MAX = 60 * 2**20
+VMEM_TOP = 63 * 2**20
 
 
 def whole(shape):
@@ -297,6 +298,374 @@
     )(half, second_a, second_b, low_a, low_b, up, down)
 
 
+MESH = pl.DeviceIdType.MESH
+TILE = 512
+SPAN = 256
+CHUNK = 256
+DOWN_ITEMS = ((0, 512, "xyz"), (512, 1024, "yzx"), (1024, 1280, "zxy"))
+UP_ORDERS = ("xyz", "yzx", "xyz", "zxy", "zxy")
+UP_WHOLE = 3
+
+
+def add_pieces(total, view, got):
+    lead = len(total.shape) - 2
+    tail = view[lead:] + (slice(None),) * (len(total.shape) - max(len(view), lead))
+    free = [i for i in range(lead) if isinstance(view[i], slice)]
+    for n in range(2 ** len(free)):
+        pick = [(n >> i) & 1 for i in range(len(free))]
+        index = list(view[:lead])
+        for i, bit in zip(free, pick):
+            index[i] = bit
+        here = tuple(index) + tail
+        total[here] = (total[here].astype(F32) + got[tuple(pick)].astype(F32)).astype(BF)
+
+
+def feed_sum_kernel(
+    second_in, low_in, up, down,
+    back_out, result_out, down_out, up_out, up_rest,
+    second, low, second_t, active, slope, down_part, up_part,
+    wide_buf, tall_buf, flat_buf, thin_buf, stage,
+    ra1, ra2, ra3, rb1, rb2, rb3, rc1, rc2, rc3, ru1, ru2, ru3,
+    load_sem, weight_sem, out_sem, end_sem, swap_send, swap_recv, sum_send, sum_recv,
+    ready_second, ready_low,
+):
+    rows = low_in.shape[0]
+    width = low_in.shape[1]
+    two = 2 * rows
+    units = active.shape[1]
+    tiles = units // TILE
+    spans = width // SPAN
+    cell = lax.axis_index("cells")
+    place = lax.axis_index("chrom")
+    core = place % 2
+    mine = {"y": place // 2, "x": cell % 2, "z": (cell // 2) % 2}
+    sibling = (cell, place + 1 - 2 * core)
+    near = {
+        "y": (cell, place + 2 - 4 * mine["y"]),
+        "x": (cell + 1 - 2 * mine["x"], place),
+        "z": (cell + 2 - 4 * mine["z"], place),
+    }
+
+    barrier = pltpu.get_barrier_semaphore()
+    for other in (sibling, near["x"], near["y"], near["z"]):
+        pl.semaphore_signal(barrier, inc=1, device_id=other, device_id_type=MESH)
+    loads = [
+        pltpu.make_async_copy(second_in, second.at[:rows], load_sem.at[0]),
+        pltpu.make_async_copy(low_in, low.at[:rows], load_sem.at[1]),
+    ]
+    for copy in loads:
+        copy.start()
+    base = core * units
+
+    def weight_copy(kind, j, slot):
+        if kind == "wide":
+            src = up.at[:, pl.ds(pl.multiple_of(base + j * TILE, 128), TILE)]
+            return pltpu.make_async_copy(src, wide_buf.at[slot], weight_sem.at[slot])
+        if kind == "tall":
+            src = down.at[pl.ds(pl.multiple_of(base + j * TILE, 128), TILE), :]
+            return pltpu.make_async_copy(src, tall_buf.at[slot], weight_sem.at[2 + slot])
+        if kind == "flat":
+            src = up.at[j * SPAN : (j + 1) * SPAN, pl.ds(pl.multiple_of(base, 128), units)]
+            return pltpu.make_async_copy(src, flat_buf, weight_sem.at[4])
+        src = down.at[pl.ds(pl.multiple_of(base, 128), units), j * SPAN : (j + 1) * SPAN]
+        return pltpu.make_async_copy(src, thin_buf, weight_sem.at[5])
+
+    plan = (
+        [("wide", j) for j in range(tiles)]
+        + [("tall", j) for j in range(tiles)]
+        + [(kind, j) for j in range(spans) for kind in ("flat", "thin")]
+    )
+    copies = {}
+
+    def fetch(i):
+        if i < len(plan):
+            kind, j = plan[i]
+            copies[i] = weight_copy(kind, j, j % 2)
+            copies[i].start()
+
+    fetch(0)
+    pl.semaphore_wait(barrier, 4)
+
+    def remote(src, dst, send, recv, device):
+        copy = pltpu.make_async_remote_copy(
+            src_ref=src, dst_ref=dst, send_sem=send, recv_sem=recv,
+            device_id=device, device_id_type=MESH,
+        )
+        copy.start()
+        return copy
+
+    sent = []
+    swaps = [
+        remote(second_in, second.at[rows:], swap_send.at[0], swap_recv.at[0], sibling),
+        remote(low_in, low.at[rows:], swap_send.at[1], swap_recv.at[1], sibling),
+    ]
+    sent += swaps
+
+    flight = {}
+
+    def down_view(order, stage_no, lo, hi, other, fix_z=None):
+        index = {"z": slice(None), "x": slice(None), "y": slice(None)}
+        for s, axis in enumerate(order[: stage_no + 1]):
+            index[axis] = 1 - mine[axis] if (s == stage_no and other) else mine[axis]
+        if fix_z is not None:
+            index["z"] = fix_z
+        return (index["z"], index["x"], index["y"], slice(None), slice(lo, hi))
+
+    def up_view(order, stage_no, other):
+        index = {"z": slice(None), "x": slice(None), "y": slice(None)}
+        for s, axis in enumerate(order[: stage_no + 1]):
+            index[axis] = 1 - mine[axis] if (s == stage_no and other) else mine[axis]
+        return (slice(None), index["z"], index["x"], index["y"])
+
+    down_recv = ((ra1, ra2, ra3), (rb1, rb2, rb3), (rc1, rc2, rc3))
+    up_recv = (ru1, ru2, ru3)
+
+    def go_down(item, stage_no, fix_z=None):
+        lo, hi, order = DOWN_ITEMS[item]
+        src = down_part.at[down_view(order, stage_no, lo, hi, True, fix_z)]
+        dst = down_recv[item][stage_no]
+        sem = item * 4 + stage_no
+        if fix_z is not None:
+            dst = dst.at[fix_z]
+            sem = item * 4 + (3 if fix_z else 0)
+        copy = remote(src, dst, sum_send.at[sem], sum_recv.at[sem], near[order[stage_no]])
+        flight.setdefault(("d", item, stage_no), []).append(copy)
+        sent.append(copy)
+
+    def end_down(item, stage_no):
+        lo, hi, order = DOWN_ITEMS[item]
+        for copy in flight[("d", item, stage_no)]:
+            copy.wait_recv()
+        add_pieces(down_part, down_view(order, stage_no, lo, hi, False), down_recv[item][stage_no])
+        if stage_no < 2:
+            go_down(item, stage_no + 1)
+
+    def go_up(j, stage_no):
+        order = UP_ORDERS[j]
+        src = up_part.at[j].at[up_view(order, stage_no, True)]
+        sem = 12 + 3 * j + stage_no
+        copy = remote(
+            src, up_recv[stage_no].at[j], sum_send.at[sem], sum_recv.at[sem], near[order[stage_no]]
+        )
+        flight[("u", j, stage_no)] = [copy]
+        sent.append(copy)
+
+    def end_up(j, stage_no):
+        flight[("u", j, stage_no)][0].wait_recv()
+        view = (j,) + up_view(UP_ORDERS[j], stage_no, False)
+        add_pieces(up_part, view, up_recv[stage_no].at[j])
+        if stage_no < 2 and j < UP_WHOLE:
+            go_up(j, stage_no + 1)
+
+    def down_rows(row):
+        block = row // 320
+        return (block // 4, (block // 2) % 2, block % 2, row % 320)
+
+    def transpose_rows(at):
+        second_t[:, at : at + CHUNK] = second[at : at + CHUNK, :].T
+
+    def hidden(j, lo):
+        here, cols = slice(lo, lo + rows), slice(j * TILE, (j + 1) * TILE)
+        upper = jnp.dot(second[here, :], wide_buf[j % 2], preferred_element_type=F32)
+        below = 0.5 * (1.0 + lax.erf(upper * ROOT_HALF))
+        density = jnp.exp(-0.5 * upper * upper) * DENSITY_SCALE
+        active[here, cols] = (upper * below).astype(BF)
+        slope[here, cols] = (below + upper * density).astype(BF)
+
+    def down_grad(lo):
+        act = active[:, lo : lo + CHUNK].T
+        grad = jnp.dot(act, low[...], preferred_element_type=F32).astype(BF)
+        for s in range(0, CHUNK, 64):
+            z, x, y, row = down_rows(lo + s)
+            down_part[z, x, y, row : row + 64, :] = grad[s : s + 64, :]
+
+    loads[0].wait()
+    for j in range(tiles + 1):
+        if j < tiles:
+            fetch(j + 1)
+            copies[j].wait()
+        for part in range(2):
+            if j < tiles:
+                hidden(j, part * rows)
+            if j:
+                down_grad((j - 1) * TILE + part * CHUNK)
+            if j == 0 and part == 0:
+                loads[1].wait()
+                for copy in swaps:
+                    copy.wait_recv()
+        if j < tiles:
+            transpose_rows(j * CHUNK)
+        else:
+            transpose_rows(two - CHUNK)
+        if j == 3:
+            go_down(0, 0, 0)
+            go_down(1, 0, 0)
+    go_down(0, 0, 1)
+    go_down(1, 0, 1)
+    go_down(2, 0)
+    for copy in swaps:
+        copy.wait_send()
+        sent.remove(copy)
+    pl.semaphore_signal(ready_second, inc=1, device_id=sibling, device_id_type=MESH)
+
+    for j in range(tiles):
+        fetch(tiles + j + 1)
+        copies[tiles + j].wait()
+        cols = slice(j * TILE, (j + 1) * TILE)
+
+        def hidden_back(i, carry, j=j, cols=cols):
+            here = pl.ds(pl.multiple_of(i * CHUNK, CHUNK), CHUNK)
+            grad = lax.dot_general(low[here, :], tall_buf[j % 2], NT, preferred_element_type=F32)
+            slope[here, cols] = (grad * slope[here, cols].astype(F32)).astype(BF)
+            return carry
+
+        lax.fori_loop(0, two // CHUNK, hidden_back, 0)
+        for m in range(4):
+            grad = jnp.dot(
+                second_t[m * 320 : (m + 1) * 320, :], slope[:, cols], preferred_element_type=F32
+            ).astype(BF)
+            for s in range(4):
+                k = 4 * m + s
+                up_part[j, k // 8, (k // 4) % 2, (k // 2) % 2, k % 2] = grad[s * 80 : (s + 1) * 80]
+        go_up(j, 0)
+        if j == 3:
+            end_down(2, 0)
+        if j == 4:
+            end_down(0, 0)
+            end_down(1, 0)
+    pl.semaphore_signal(ready_low, inc=1, device_id=sibling, device_id_type=MESH)
+
+    events = {
+        0: [(end_down, 2, 1), (end_up, 0, 0)],
+        2: [(end_up, 1, 0), (end_down, 0, 1)],
+        4: [(end_down, 1, 1), (end_down, 2, 2)],
+        5: [(end_up, 2, 0), (end_up, 0, 1)],
+        6: [(end_up, 1, 1)],
+        8: [(end_up, 2, 1), (end_up, 3, 0)],
+        9: [
+            (end_down, 0, 2), (end_down, 1, 2), (end_up, 0, 2), (end_up, 1, 2), (end_up, 2, 2),
+            (end_up, 4, 0),
+        ],
+    }
+    pending = []
+    writes = {}
+
+    def finish(step, buf, out, n, copy):
+        copy.wait_recv()
+        cols = slice(n * SPAN, (n + 1) * SPAN)
+        stage[step % 2] = stage[step % 2] + buf[rows:, cols].astype(F32)
+        writes[step] = pltpu.make_async_copy(stage.at[step % 2], out.at[:, cols], out_sem.at[step % 2])
+        writes[step].start()
+
+    for step in range(2 * spans):
+        n = step // 2
+        backward = step % 2 == 0
+        buf, out = (second, back_out) if backward else (low, result_out)
+        fetch(2 * tiles + step + 1)
+        copies[2 * tiles + step].wait()
+        cols = slice(n * SPAN, (n + 1) * SPAN)
+
+        def product(lo, n=n, backward=backward):
+            if backward:
+                return lax.dot_general(
+                    slope[lo : lo + rows, :], flat_buf[...], NT, preferred_element_type=F32
+                )
+            return jnp.dot(active[lo : lo + rows, :], thin_buf[...], preferred_element_type=F32)
+
+        buf[:rows, cols] = product(rows).astype(BF)
+        own = product(0)
+        if n == 0:
+            pl.semaphore_wait(ready_second if backward else ready_low, 1)
+        copy = remote(
+            buf.at[:rows, cols], buf.at[rows:, cols],
+            swap_send.at[2 + step], swap_recv.at[2 + step], sibling,
+        )
+        sent.append(copy)
+        if step >= 2:
+            writes[step - 2].wait()
+        stage[step % 2] = own
+        if pending:
+            finish(*pending.pop())
+        pending.append((step, buf, out, n, copy))
+        for event, item, stage_no in events.get(step, ()):
+            event(item, stage_no)
+    finish(*pending.pop())
+    ends = [
+        pltpu.make_async_copy(
+            down_part.at[mine["z"], mine["x"], mine["y"]], down_out, end_sem.at[0]
+        ),
+        pltpu.make_async_copy(
+            up_part.at[:UP_WHOLE, :, mine["z"], mine["x"], mine["y"]], up_out, end_sem.at[1]
+        ),
+        pltpu.make_async_copy(up_part.at[UP_WHOLE:, :, mine["z"]], up_rest, end_sem.at[2]),
+    ]
+    for copy in ends:
+        copy.start()
+    writes[2 * spans - 2].wait()
+    writes[2 * spans - 1].wait()
+    for copy in ends:
+        copy.wait()
+    for copy in sent:
+        copy.wait_send()
+
+
+def feed_forward_sum(second, low, up, down):
+    rows, width = second.shape
+    units = up.shape[1] // 2
+    tiles = units // TILE
+    two = 2 * rows
+    anywhere = pl.BlockSpec(memory_space=pl.ANY)
+    recv = []
+    for lo, hi, _ in DOWN_ITEMS:
+        recv += [
+            pltpu.VMEM((2, 2, 320, hi - lo), BF),
+            pltpu.VMEM((2, 320, hi - lo), BF),
+            pltpu.VMEM((320, hi - lo), BF),
+        ]
+    recv += [
+        pltpu.VMEM((tiles, 2, 2, 2, 80, TILE), BF),
+        pltpu.VMEM((UP_WHOLE, 2, 2, 80, TILE), BF),
+        pltpu.VMEM((UP_WHOLE, 2, 80, TILE), BF),
+    ]
+    dma = pltpu.SemaphoreType.DMA
+    return pl.pallas_call(
+        feed_sum_kernel,
+        in_specs=[anywhere] * 4,
+        out_specs=[anywhere] * 5,
+        out_shape=[
+            jax.ShapeDtypeStruct((rows, width), F32),
+            jax.ShapeDtypeStruct((rows, width), F32),
+            jax.ShapeDtypeStruct((320, width), BF),
+            jax.ShapeDtypeStruct((UP_WHOLE, 2, 80, TILE), BF),
+            jax.ShapeDtypeStruct((tiles - UP_WHOLE, 2, 2, 2, 80, TILE), BF),
+        ],
+        scratch_shapes=[
+            pltpu.VMEM((two, width), BF),
+            pltpu.VMEM((two, width), BF),
+            pltpu.VMEM((width, two), BF),
+            pltpu.VMEM((two, units), BF),
+            pltpu.VMEM((two, units), BF),
+            pltpu.VMEM((2, 2, 2, 320, width), BF),
+            pltpu.VMEM((tiles, 2, 2, 2, 2, 80, TILE), BF),
+            pltpu.VMEM((2, width, TILE), BF),
+            pltpu.VMEM((2, TILE, width), BF),
+            pltpu.VMEM((SPAN, units), BF),
+            pltpu.VMEM((units, SPAN), BF),
+            pltpu.VMEM((2, rows, SPAN), F32),
+        ]
+        + recv
+        + [
+            dma((2,)), dma((6,)), dma((2,)), dma((3,)), dma((12,)), dma((12,)), dma((27,)), dma((27,)),
+            pltpu.SemaphoreType.REGULAR, pltpu.SemaphoreType.REGULAR,
+        ],
+        compiler_params=pltpu.CompilerParams(
+            vmem_limit_bytes=VMEM_TOP, collective_id=0, has_side_effects=True
+        ),
+        cost_estimate=cost(2 * 6 * two * width * units, 6e7),
+        name="feed_sum",
+    )(second, low, up, down)
+
+
 def swap(x, axis, mask):
     size = lax.axis_size(axis)
     return lax.ppermute(x, axis, [(i, i ^ mask) for i in range(size)])
@@ -332,12 +701,15 @@
 
 def scatter_columns_split(x, order):
     cell_bits = log2(lax.axis_size("cells"))
-    core = lax.axis_index("chrom") & 1
     width = x.shape[1]
     names = [("cells", b) for b in reversed(range(cell_bits))] + [("chrom", 1)]
     x = x.reshape((2,) * (cell_bits + 1) + (-1, width))
-    x = scatter_rows(x, order, names)
-    x = x.reshape(2, -1, width)
+    return place_columns(scatter_rows(x, order, names))
+
+
+def place_columns(x):
+    core = lax.axis_index("chrom") & 1
+    x = x.reshape(2, -1, x.shape[-1])
     keep = lax.dynamic_index_in_dim(x, core, 0, keepdims=False)
     got = swap(lax.dynamic_index_in_dim(x, 1 - core, 0, keepdims=False).astype(BF), "chrom", 1).astype(F32)
     left = jnp.where(core == 0, keep, got)
@@ -346,23 +718,27 @@
 
 
 def scatter_rows_split(x, order):
-    cells = lax.axis_size("cells")
-    cell_bits = log2(cells)
-    chrom = lax.axis_size("chrom")
-    core = lax.axis_index("chrom") & 1
-    high = (lax.axis_index("cells") >> (cell_bits - 1)) & 1
+    cell_bits = log2(lax.axis_size("cells"))
     width = x.shape[1]
     names = [("cells", b) for b in reversed(range(cell_bits - 1))] + [("chrom", 1)]
     x = x.reshape((2,) * cell_bits + (-1, width))
-    x = scatter_rows(x, order, names)
+    return place_rows(scatter_rows(x, order, names))
+
+
+def place_rows(x):
+    cells = lax.axis_size("cells")
+    chrom = lax.axis_size("chrom")
+    core = lax.axis_index("chrom") & 1
     top = cells // 2
+    high = lax.axis_index("cells") // top
+    width = x.shape[1]
     pairs = []
     for cell in range(cells):
         for place in range(chrom):
             if (cell // top) != (place & 1):
                 pairs.append((cell * chrom + place, (cell ^ top) * chrom + place))
     got = lax.ppermute(x.astype(BF), ("cells", "chrom"), pairs)
-    x = (x + got.astype(F32)).reshape(2, -1, width)
+    x = (x.astype(F32) + got.astype(F32)).reshape(2, -1, width)
     keep = lax.dynamic_index_in_dim(x, core, 0, keepdims=False)
     send = lax.dynamic_index_in_dim(x, 1 - core, 0, keepdims=False).astype(BF)
     back = []
@@ -372,6 +748,28 @@
                 back.append((cell * chrom + place, cell * chrom + (place ^ 1)))
     got = lax.ppermute(send, ("cells", "chrom"), back)
     return jnp.where(core == high, keep, got.astype(F32))
+
+
+def feed_forward_plain(second_low, down_low, up_weight, down_weight):
+    cell_bits = log2(lax.axis_size("cells"))
+    core = lax.axis_index("chrom") & 1
+    result_part, result_send, back_part, back_send, down_grad, up_grad = feed_forward(
+        core[None].astype(jnp.int32),
+        second_low,
+        swap(second_low, "chrom", 1),
+        down_low,
+        swap(down_low, "chrom", 1),
+        up_weight,
+        down_weight,
+    )
+    second_back = back_part + swap(back_send, "chrom", 1).astype(F32)
+    result_part = result_part + swap(result_send, "chrom", 1).astype(F32)
+    low_bits = [("cells", b) for b in range(cell_bits - 1)]
+    down_out = scatter_rows_split(down_grad, low_bits + [("chrom", 1)])
+    up_out = scatter_columns_split(
+        up_grad, [("chrom", 1)] + low_bits[::-1] + [("cells", cell_bits - 1)]
+    )
+    return second_back, result_part, down_out, up_out
 
 
 def norm_rows(values, gain, shift):
@@ -477,25 +875,24 @@
         * local_valid.astype(F32)[:, :, None]
     ).reshape(rows, width)
     down_low = result_back.astype(BF)
-    down_low_near = swap(down_low, "chrom", 1)
-    second_low_near = swap(second_low, "chrom", 1)
-
-    result_part, result_send, back_part, back_send, down_grad, up_grad = feed_forward(
-        core[None].astype(jnp.int32),
-        second_low,
-        second_low_near,
-        down_low,
-        down_low_near,
-        up_weight,
-        down_weight,
-    )
-    second_back = back_part + swap(back_send, "chrom", 1).astype(F32)
-    result = middle + result_part + swap(result_send, "chrom", 1).astype(F32)
+    low_bits = [("cells", b) for b in range(cell_bits - 1)]
+    if lax.axis_size("cells") == 8 and parts == 4:
+        second_back, result_part, down_grad, up_grad, up_rest = feed_forward_sum(
+            second_low, down_low, up_weight, down_weight
+        )
+        result = middle + result_part
+        down_out = place_rows(down_grad)
+        up_rest = halve(halve(up_rest, 2, "cells", 0).astype(BF), 2, "chrom", 1).astype(BF)
+        up_grad = jnp.concatenate([up_grad, up_rest], axis=0)
+        up_grad = up_grad.transpose(1, 2, 0, 3).reshape(2, 80, -1)
+        up_out = place_columns(halve(up_grad, 0, "cells", 2))
+    else:
+        second_back, result_part, down_out, up_out = feed_forward_plain(
+            second_low, down_low, up_weight, down_weight
+        )
+        result = middle + result_part
     result_cells = result.reshape(cells_here, seq_here, width)
     layer_out = result_cells.astype(BF)
-    low_bits = [("cells", b) for b in range(cell_bits - 1)]
-    down_out = scatter_rows_split(down_grad, low_bits + [("chrom", 1)])
-    up_out = scatter_columns_split(up_grad, [("chrom", 1)] + low_bits[::-1] + [("cells", cell_bits - 1)])
 
     cls_rows = jnp.where(place == 0, result_cells[:, 0, :], 0.0)
     cls_total = jnp.sum(cls_rows, axis=0)

time: 657 us -> 575 us (0.88)
  waiting for transfers between devices: 224 us -> 128 us
  Pallas kernels: 199 us -> 234 us
  other arithmetic: 52.4 us -> 44.1 us
  local copies, waits for them, and re-layouts: 51.1 us -> 43.2 us
    ppermute x67 -> x59, waiting for transfers between devices: 207 us -> 126 us  [swap(): return lax.ppermute(x, axis, [(i, i ^ mask) for i in range(size)])]
    pallas_call x1, Pallas kernels: 84.9 us -> 121 us  [feed_forward_sum(): pl.pallas_call(feed_sum_kernel, in_specs=[anywhere] * 4, out_specs=[anywh...]
    ppermute x2, waiting for transfers between devices: 16.8 us -> 2.06 us  [the longest x1 2.05 us: place_rows(): got = lax.ppermute(send, ('cells', 'chrom'), back)]
    convert_element_type x10 -> x5, other arithmetic: 12.9 us -> 2.34 us  [scatter_rows(): x = halve(x.astype(BF), names.index(name), name[0], name[1])]
    squeeze x14 -> x10, local copies, waits for them, and re-layouts: 14.1 us -> 4.51 us  [halve(): send = lax.dynamic_index_in_dim(x, 1 - mine, dim, keepdims=False)]
    dot_general x4, matrix products: 26.1 us -> 18.3 us  [contract(): return lax.dot_general(left, right, TN, preferred_element_type=F32)]
    ppermute x67 -> x59, starting transfers between devices: 68.5 us -> 60.9 us  [swap(): return lax.ppermute(x, axis, [(i, i ^ mask) for i in range(size)])]
  transfers between devices with their start and end apart: 69 -> 61, of which waited for: 29 -> 23; matrix products, arithmetic and copies ran while one was open for 21% -> 16% of each run, Pallas kernels for 18% -> 20%
where the time goes in v2:
time: 575 us; the launch traced here: 566 us
  Pallas kernels  234 us (41%)
  waiting for transfers between devices  128 us (22%)
  starting transfers between devices  67.7 us (12%)
  matrix products  45.9 us (8%)
  other arithmetic  44.1 us (8%)
  local copies, waits for them, and re-layouts  43.2 us (8%)
    ppermute x59, waiting for transfers between devices, swap(): return lax.ppermute(x, axis, [(i, i ^ mask) for i in range(size)])  126 us
    pallas_call x1, Pallas kernels, feed_forward_sum(): pl.pallas_call(feed_sum_kernel, in_specs=[anywhere] * 4, out_specs=[anywh...  121 us
    pallas_call x3, Pallas kernels, attend_back(): pl.pallas_call(functools.partial(attend_back_kernel, block, heads), in_sp...  61.5 us
    ppermute x59, starting transfers between devices, swap(): return lax.ppermute(x, axis, [(i, i ^ mask) for i in range(size)])  60.9 us
    pallas_call x3, Pallas kernels, attend(): pl.pallas_call(functools.partial(attend_kernel, block, heads), in_specs=[...  51.9 us
    dot_general x13, matrix products, back_through(): return lax.dot_general(grad, weight, NT, preferred_element_type=F32)  22.6 us
    dot_general x4, matrix products, contract(): return lax.dot_general(left, right, TN, preferred_element_type=F32)  18.3 us
  transfers between devices with their start and end apart: 61, of which 23 were waited for; matrix products, arithmetic and copies ran while one was open for 16% of the time, Pallas kernels for 20%

profile of v2, /device:TPU:1, one launch (start us, length us, event | category | flops | bytes accessed | tf_op | source)
XLA Modules:
  0.0 565.6 jit_solution(365699576931041989)
XLA Ops:
  0.7 2.0 convert_reduce_fusion
  6.5 2.1 collective-permute-start.1
  17.1 2.8 constant_dynamic-slice_fusion.10
  23.1 2.1 collective-permute-start.2
  25.2 2.5 pad_maximum_fusion.3.refs_4_
  27.7 9.4 %collective-permute-done.7.refs_2_ = bf16[256,1280]{1,0:T(8,128)(2,1)} collective-permute-done((bf16[256,1280]{1,0:T(8,128)(2,1)}, bf16[256,1280]{1,0:T(8,128)(2,1)}, u32[]{:S(2)}, u32[]{:S(2)}) %collective-permute-start.7) | collective-permute-done | bytes 655392 | tf_op jit(solution)/shard_map/ppermute | solution.py:671
  37.1 2.1 collective-permute-start.8
  39.7 11.4 %collective-permute-done.13.refs_2_ = bf16[256,1280]{1,0:T(8,128)(2,1)} collective-permute-done((bf16[256,1280]{1,0:T(8,128)(2,1)S(1)}, bf16[256,1280]{1,0:T(8,128)(2,1)}, u32[]{:S(2)}, u32[]{:S(2)}) %collective-permute-start.13) | collective-permute-done | bytes 655392 | tf_op jit(solution)/shard_map/ppermute | solution.py:671
  52.4 17.3 %attend.3 = (bf16[256,320]{1,0:T(8,128)(2,1)}, bf16[256,320]{1,0:T(8,128)(2,1)}, bf16[256,320]{1,0:T(8,128)(2,1)}, bf16[256,320]{1,0:T(8,128)(2,1)}, bf16[768,960]{1,0:T(8,128)(2,1)}) custom-call(s32[8]{0:T(128)} %get-tuple-element.142.lens, bf16[256,1280]{1,0:T(8,128)(2,1)} %copy-done.33, bf16[256,1280]{1,0:T(8,128)(2,1)} %collective-permute-done.refs_1_, ...), custom_call_target="tpu_custom_call" | custom-call | flops 6543114240 | bytes 8000000 | tf_op jit(solution)/shard_map/attend/pallas_call | solution.py:111
  71.9 17.2 %attend.4 = (bf16[256,320]{1,0:T(8,128)(2,1)}, bf16[256,320]{1,0:T(8,128)(2,1)}, bf16[256,320]{1,0:T(8,128)(2,1)}, bf16[256,320]{1,0:T(8,128)(2,1)}, bf16[768,960]{1,0:T(8,128)(2,1)}) custom-call(s32[8]{0:T(128)} %get-tuple-element.144.lens, bf16[256,1280]{1,0:T(8,128)(2,1)} %get-tuple-element.114.refs_0_, bf16[256,1280]{1,0:T(8,128)(2,1)} %collective-permute-done.6.refs_1_, ...), custom_call_target="tpu_custom_call" | custom-call | flops 6543114240 | bytes 8000000 | tf_op jit(solution)/shard_map/attend/pallas_call | solution.py:111
  90.8 17.4 %attend.5 = (bf16[256,320]{1,0:T(8,128)(2,1)}, bf16[256,320]{1,0:T(8,128)(2,1)}, bf16[256,320]{1,0:T(8,128)(2,1)}, bf16[256,320]{1,0:T(8,128)(2,1)}, bf16[768,960]{1,0:T(8,128)(2,1)}) custom-call(s32[8]{0:T(128)} %get-tuple-element.143.lens, bf16[256,1280]{1,0:T(8,128)(2,1)} %copy-done.31, bf16[256,1280]{1,0:T(8,128)(2,1)} %copy-done.70, ...), custom_call_target="tpu_custom_call" | custom-call | flops 6543114240 | bytes 8000000 | tf_op jit(solution)/shard_map/attend/pallas_call | solution.py:111
  111.4 3.5 constant_dynamic-slice_fusion.9
  114.9 2.1 concatenate.67
  117.0 2.1 concatenate.68
  120.0 2.1 concatenate.69
  122.1 5.1 fusion.113
  131.2 120.8 %feed_sum.1 = (f32[768,1280]{1,0:T(8,128)}, f32[768,1280]{1,0:T(8,128)}, bf16[320,1280]{1,0:T(8,128)(2,1)}, bf16[3,2,80,512]{3,2,1,0:T(8,128)(2,1)}, bf16[2,2,2,2,80,512]{5,4,3,2,1,0:T(8,128)(2,1)}) custom-call(bf16[768,1280]{1,0:T(8,128)(2,1)} %add_convert_fusion.1.second_in, bf16[768,1280]{1,0:T(8,128)(2,1)} %bitcast_convert_fusion.low_in, ...), custom_call_target="tpu_custom_call" | custom-call | flops 60397977600 | bytes 60000000 | tf_op jit(solution)/shard_map/feed_sum/pallas_call | solution.py:631
  252.0 4.5 multiply_reduce_fusion
  257.6 4.3 bitcast_add_fusion
  262.0 2.8 fusion.78
  265.0 2.7 convolution_convert_fusion
  279.3 5.4 collective-permute-start.59
  287.6 5.7 %collective-permute-done.54 = f32[4,1280]{1,0:T(4,128)S(1)} collective-permute-done((f32[4,1280]{1,0:T(4,128)S(1)}, f32[4,1280]{1,0:T(4,128)S(1)}, u32[]{:S(2)}, u32[]{:S(2)}) %collective-permute-start.54) | collective-permute-done | bytes 20512 | tf_op jit(solution)/shard_map/ppermute | solution.py:671
  293.3 14.5 %collective-permute-start.20 = (bf16[256,320]{1,0:T(8,128)(2,1)S(1)}, bf16[256,320]{1,0:T(8,128)(2,1)S(1)}, u32[]{:S(2)}, u32[]{:S(2)}) collective-permute-start(bf16[256,320]{1,0:T(8,128)(2,1)S(1)} %get-tuple-element.100), channel_id=1, source_target_pairs={{0,3},{1,2},{2,1},{3,0},{4,7},{5,6},{6,5},{7,4},{8,11},{9,10},{10,... | collective-permute-start | bytes 491528 | tf_op jit(solution)/shard_map/ppermute | solution.py:671
  310.0 3.4 collective-permute-done.20.refs_3_
  314.2 20.8 %attend_back.3 = (bf16[256,960]{1,0:T(8,128)(2,1)}, bf16[256,960]{1,0:T(8,128)(2,1)}, bf16[256,960]{1,0:T(8,128)(2,1)}, bf16[256,960]{1,0:T(8,128)(2,1)}) custom-call(s32[8]{0:T(128)} %get-tuple-element.142.lens, bf16[256,320]{1,0:T(8,128)(2,1)} %get-tuple-element.111.refs_0_, bf16[256,320]{1,0:T(8,128)(2,1)} %copy-done.72, bf16[256,320]{1,0:T(8,128)(2,1)} %copy-done.73, ...), custom_call_target="tpu_custom_call" | custom-call | flops 7549747200 | bytes 6000000 | tf_op jit(solution)/shard_map/attend_back/pallas_call | solution.py:173
  335.0 2.8 fusion.48
  341.8 20.3 %attend_back.4 = (bf16[256,960]{1,0:T(8,128)(2,1)}, bf16[256,960]{1,0:T(8,128)(2,1)}, bf16[256,960]{1,0:T(8,128)(2,1)}, bf16[256,960]{1,0:T(8,128)(2,1)}) custom-call(s32[8]{0:T(128)} %get-tuple-element.144.lens, bf16[256,320]{1,0:T(8,128)(2,1)} %get-tuple-element.108.refs_0_, bf16[256,320]{1,0:T(8,128)(2,1)} %collective-permute-done.23.refs_1_, ...), custom_call_target="tpu_custom_call" | custom-call | flops 7549747200 | bytes 6000000 | tf_op jit(solution)/shard_map/attend_back/pallas_call | solution.py:173
  362.1 2.8 fusion.50
  366.8 20.3 %attend_back.5 = (bf16[256,960]{1,0:T(8,128)(2,1)}, bf16[256,960]{1,0:T(8,128)(2,1)}, bf16[256,960]{1,0:T(8,128)(2,1)}, bf16[256,960]{1,0:T(8,128)(2,1)}) custom-call(s32[8]{0:T(128)} %get-tuple-element.143.lens, bf16[256,320]{1,0:T(8,128)(2,1)} %get-tuple-element.104.refs_0_, bf16[256,320]{1,0:T(8,128)(2,1)} %collective-permute-done.28.refs_1_, ...), custom_call_target="tpu_custom_call" | custom-call | flops 7549747200 | bytes 6000000 | tf_op jit(solution)/shard_map/attend_back/pallas_call | solution.py:173
  387.1 3.3 fusion.52
  392.3 4.8 fusion.26
  397.2 4.6 fusion.18
  401.8 6.1 %add_convert_fusion = bf16[1280,960]{0,1:T(8,128)(2,1)} fusion(f32[1280,960]{0,1:T(8,128)S(1)} %fusion.18, f32[1280,960]{0,1:T(8,128)S(1)} %fusion.26, bf16[256,1280]{1,0:T(8,128)(2,1)} %collective-permute-done.14.refs_3_, bf16[256,1280]{1,0:T(8,128)(2,1)} %collective-permute-done.13.refs_2_, bf16[256,1280]{1,0:T(8,128)(2,1)S(1)} %copy-done.71, ...), kind=kOutput, calls=%fused_computation.1 | convolution fusion | flops 2538618880 | bytes 16875520 | tf_op jit(solution)/shard_map/dot_general | solution.py:793
  407.9 4.5 copy.35
  421.6 6.4 %collective-permute-done.56 = bf16[2,2,80,512]{3,2,1,0:T(8,128)(2,1)S(1)} collective-permute-done((bf16[2,2,80,512]{3,2,1,0:T(8,128)(2,1)S(1)}, bf16[2,2,80,512]{3,2,1,0:T(8,128)(2,1)S(1)}, u32[]{:S(2)}, u32[]{:S(2)}) %collective-permute-start.56) | collective-permute-done | bytes 327712 | tf_op jit(solution)/shard_map/ppermute | solution.py:671
  429.7 2.1 collective-permute-done.60
  432.8 16.8 %collective-permute-done.57 = bf16[80,2560]{1,0:T(8,128)(2,1)S(1)} collective-permute-done((bf16[80,2560]{1,0:T(8,128)(2,1)S(1)}, bf16[80,2560]{1,0:T(8,128)(2,1)S(1)}, u32[]{:S(2)}, u32[]{:S(2)}) %collective-permute-start.57) | collective-permute-done | bytes 409632 | tf_op jit(solution)/shard_map/ppermute | solution.py:671
  462.4 6.5 %collective-permute-done.22 = bf16[256,1280]{1,0:T(8,128)(2,1)S(1)} collective-permute-done((bf16[256,1280]{1,0:T(8,128)(2,1)S(1)}, bf16[256,1280]{1,0:T(8,128)(2,1)S(1)}, u32[]{:S(2)}, u32[]{:S(2)}) %collective-permute-start.22) | collective-permute-done | bytes 655392 | tf_op jit(solution)/shard_map/ppermute | solution.py:671
  469.9 13.0 %collective-permute-done.27 = bf16[256,1280]{1,0:T(8,128)(2,1)S(1)} collective-permute-done((bf16[256,1280]{1,0:T(8,128)(2,1)S(1)}, bf16[256,1280]{1,0:T(8,128)(2,1)S(1)}, u32[]{:S(2)}, u32[]{:S(2)}) %collective-permute-start.27) | collective-permute-done | bytes 655392 | tf_op jit(solution)/shard_map/ppermute | solution.py:671
  483.8 13.1 %collective-permute-done.32 = bf16[256,1280]{1,0:T(8,128)(2,1)S(1)} collective-permute-done((bf16[256,1280]{1,0:T(8,128)(2,1)S(1)}, bf16[256,1280]{1,0:T(8,128)(2,1)S(1)}, u32[]{:S(2)}, u32[]{:S(2)}) %collective-permute-start.32) | collective-permute-done | bytes 655392 | tf_op jit(solution)/shard_map/ppermute | solution.py:671
  510.5 3.6 collective-permute-done.36
  514.1 2.1 collective-permute-start.37
  516.2 5.1 fusion.14
  527.6 2.5 collective-permute-done.43
  533.7 10.4 %collective-permute-done.46 = bf16[2,2,80,640]{3,2,1,0:T(8,128)(2,1)S(1)} collective-permute-done((bf16[2,2,80,640]{3,2,1,0:T(8,128)(2,1)S(1)}, bf16[2,2,80,640]{3,2,1,0:T(8,128)(2,1)S(1)}, u32[]{:S(2)}, u32[]{:S(2)}) %collective-permute-start.46) | collective-permute-done | bytes 409632 | tf_op jit(solution)/shard_map/ppermute | solution.py:671
  545.9 10.7 %collective-permute-done.47 = bf16[2,80,640]{2,1,0:T(8,128)(2,1)S(1)} collective-permute-done((bf16[2,80,640]{2,1,0:T(8,128)(2,1)S(1)}, bf16[2,80,640]{2,1,0:T(8,128)(2,1)S(1)}, u32[]{:S(2)}, u32[]{:S(2)}) %collective-permute-start.47) | collective-permute-done | bytes 204832 | tf_op jit(solution)/shard_map/ppermute | solution.py:671
  557.6 3.0 collective-permute-done.48
  (399 shorter events, 112.6 us)
Async XLA Ops:
  6.5 16.6 %collective-permute-start.1 = (bf16[256,1280]{1,0:T(8,128)(2,1)S(1)}, bf16[256,1280]{1,0:T(8,128)(2,1)}, u32[]{:S(2)}, u32[]{:S(2)}) collective-permute-start(bf16[256,1280]{1,0:T(8,128)(2,1)S(1)} %get-tuple-element.112.refs_0_), channel_id=1, source_target_pairs={{0,2},{1,3},{2,0},{3,1},{4,6},{5,7},{6,4},{7,5},{8,10},{9,11},{10,... | collective-permute-start | bytes 1966088 | tf_op jit(solution)/shard_map/ppermute | solution.py:671
  8.5 31.2 %collective-permute-start = (bf16[256,1280]{1,0:T(8,128)(2,1)S(1)}, bf16[256,1280]{1,0:T(8,128)(2,1)}, u32[]{:S(2)}, u32[]{:S(2)}) collective-permute-start(bf16[256,1280]{1,0:T(8,128)(2,1)S(1)} %get-tuple-element.112.refs_0_), channel_id=1, source_target_pairs={{0,1},{1,0},{2,3},{3,2},{4,5},{5,4},{6,7},{7,6},{8,9},{9,8},{10,11... | collective-permute-start | bytes 1966088 | tf_op jit(solution)/shard_map/ppermute | solution.py:671
  9.5 27.6 %collective-permute-start.7 = (bf16[256,1280]{1,0:T(8,128)(2,1)}, bf16[256,1280]{1,0:T(8,128)(2,1)}, u32[]{:S(2)}, u32[]{:S(2)}) collective-permute-start(bf16[256,1280]{1,0:T(8,128)(2,1)} %get-tuple-element.114.refs_0_), channel_id=1, source_target_pairs={{0,2},{1,3},{2,0},{3,1},{4,6},{5,7},{6,4},{7,5},{8,10},{9,11},{10,... | collective-permute-start | bytes 1966088 | tf_op jit(solution)/shard_map/ppermute | solution.py:671
  9.5 60.2 %collective-permute-start.6 = (bf16[256,1280]{1,0:T(8,128)(2,1)}, bf16[256,1280]{1,0:T(8,128)(2,1)}, u32[]{:S(2)}, u32[]{:S(2)}) collective-permute-start(bf16[256,1280]{1,0:T(8,128)(2,1)} %get-tuple-element.114.refs_0_), channel_id=1, source_target_pairs={{0,1},{1,0},{2,3},{3,2},{4,5},{5,4},{6,7},{7,6},{8,9},{9,8},{10,11... | collective-permute-start | bytes 1966088 | tf_op jit(solution)/shard_map/ppermute | solution.py:671
  9.6 41.6 %collective-permute-start.13 = (bf16[256,1280]{1,0:T(8,128)(2,1)S(1)}, bf16[256,1280]{1,0:T(8,128)(2,1)}, u32[]{:S(2)}, u32[]{:S(2)}) collective-permute-start(bf16[256,1280]{1,0:T(8,128)(2,1)S(1)} %get-tuple-element.113.refs_0_), channel_id=1, source_target_pairs={{0,2},{1,3},{2,0},{3,1},{4,6},{5,7},{6,4},{7,5},{8,10},{9,11},{10,... | collective-permute-start | bytes 1966088 | tf_op jit(solution)/shard_map/ppermute | solution.py:671
  23.1 29.3 %collective-permute-start.2 = (bf16[256,1280]{1,0:T(8,128)(2,1)}, bf16[256,1280]{1,0:T(8,128)(2,1)}, u32[]{:S(2)}, u32[]{:S(2)}) collective-permute-start(bf16[256,1280]{1,0:T(8,128)(2,1)} %collective-permute-done.1.refs_2_), channel_id=1, source_target_pairs={{0,1},{1,0},{2,3},{3,2},{4,5},{5,4},{6,7},{7,6},{8,9},{9,8},{10,11... | collective-permute-start | bytes 1966088 | tf_op jit(solution)/shard_map/ppermute | solution.py:671
  37.1 34.1 %collective-permute-start.8 = (bf16[256,1280]{1,0:T(8,128)(2,1)}, bf16[256,1280]{1,0:T(8,128)(2,1)}, u32[]{:S(2)}, u32[]{:S(2)}) collective-permute-start(bf16[256,1280]{1,0:T(8,128)(2,1)} %collective-permute-done.7.refs_2_), channel_id=1, source_target_pairs={{0,1},{1,0},{2,3},{3,2},{4,5},{5,4},{6,7},{7,6},{8,9},{9,8},{10,11... | collective-permute-start | bytes 1966088 | tf_op jit(solution)/shard_map/ppermute | solution.py:671
  39.7 49.3 %collective-permute-start.12 = (bf16[256,1280]{1,0:T(8,128)(2,1)S(1)}, bf16[256,1280]{1,0:T(8,128)(2,1)S(1)}, u32[]{:S(2)}, u32[]{:S(2)}) collective-permute-start(bf16[256,1280]{1,0:T(8,128)(2,1)S(1)} %get-tuple-element.113.refs_0_), channel_id=1, source_target_pairs={{0,1},{1,0},{2,3},{3,2},{4,5},{5,4},{6,7},{7,6},{8,9},{9,8},{10,11... | collective-permute-start | bytes 1966088 | tf_op jit(solution)/shard_map/ppermute | solution.py:671
  51.2 39.4 %collective-permute-start.14 = (bf16[256,1280]{1,0:T(8,128)(2,1)}, bf16[256,1280]{1,0:T(8,128)(2,1)}, u32[]{:S(2)}, u32[]{:S(2)}) collective-permute-start(bf16[256,1280]{1,0:T(8,128)(2,1)} %collective-permute-done.13.refs_2_), channel_id=1, source_target_pairs={{0,1},{1,0},{2,3},{3,2},{4,5},{5,4},{6,7},{7,6},{8,9},{9,8},{10,11... | collective-permute-start | bytes 1966088 | tf_op jit(solution)/shard_map/ppermute | solution.py:671
  69.7 38.5 %collective-permute-start.3 = (bf16[256,320]{1,0:T(8,128)(2,1)}, bf16[256,320]{1,0:T(8,128)(2,1)S(1)}, u32[]{:S(2)}, u32[]{:S(2)}) collective-permute-start(bf16[256,320]{1,0:T(8,128)(2,1)} %get-tuple-element.47), channel_id=1, source_target_pairs={{0,1},{1,0},{2,3},{3,2},{4,5},{5,4},{6,7},{7,6},{8,9},{9,8},{10,11... | collective-permute-start | bytes 491528 | tf_op jit(solution)/shard_map/ppermute | solution.py:671
  69.7 38.8 %collective-permute-start.4 = (bf16[256,320]{1,0:T(8,128)(2,1)}, bf16[256,320]{1,0:T(8,128)(2,1)S(1)}, u32[]{:S(2)}, u32[]{:S(2)}) collective-permute-start(bf16[256,320]{1,0:T(8,128)(2,1)} %get-tuple-element.48), channel_id=1, source_target_pairs={{0,2},{1,3},{2,0},{3,1},{4,6},{5,7},{6,4},{7,5},{8,10},{9,11},{10,... | collective-permute-start | bytes 491528 | tf_op jit(solution)/shard_map/ppermute | solution.py:671
  71.3 37.6 %collective-permute-start.5 = (bf16[256,320]{1,0:T(8,128)(2,1)}, bf16[256,320]{1,0:T(8,128)(2,1)S(1)}, u32[]{:S(2)}, u32[]{:S(2)}) collective-permute-start(bf16[256,320]{1,0:T(8,128)(2,1)} %get-tuple-element.49), channel_id=1, source_target_pairs={{0,3},{1,2},{2,1},{3,0},{4,7},{5,6},{6,5},{7,4},{8,11},{9,10},{10,... | collective-permute-start | bytes 491528 | tf_op jit(solution)/shard_map/ppermute | solution.py:671
  89.0 21.0 %collective-permute-start.10 = (bf16[256,320]{1,0:T(8,128)(2,1)}, bf16[256,320]{1,0:T(8,128)(2,1)S(1)}, u32[]{:S(2)}, u32[]{:S(2)}) collective-permute-start(bf16[256,320]{1,0:T(8,128)(2,1)} %get-tuple-element.52), channel_id=1, source_target_pairs={{0,2},{1,3},{2,0},{3,1},{4,6},{5,7},{6,4},{7,5},{8,10},{9,11},{10,... | collective-permute-start | bytes 491528 | tf_op jit(solution)/shard_map/ppermute | solution.py:671
  90.6 26.4 %collective-permute-start.11 = (bf16[256,320]{1,0:T(8,128)(2,1)}, bf16[256,320]{1,0:T(8,128)(2,1)}, u32[]{:S(2)}, u32[]{:S(2)}) collective-permute-start(bf16[256,320]{1,0:T(8,128)(2,1)} %get-tuple-element.53), channel_id=1, source_target_pairs={{0,3},{1,2},{2,1},{3,0},{4,7},{5,6},{6,5},{7,4},{8,11},{9,10},{10,... | collective-permute-start | bytes 491528 | tf_op jit(solution)/shard_map/ppermute | solution.py:671
  108.2 8.7 %collective-permute-start.9 = (bf16[256,320]{1,0:T(8,128)(2,1)}, bf16[256,320]{1,0:T(8,128)(2,1)}, u32[]{:S(2)}, u32[]{:S(2)}) collective-permute-start(bf16[256,320]{1,0:T(8,128)(2,1)} %get-tuple-element.51), channel_id=1, source_target_pairs={{0,1},{1,0},{2,3},{3,2},{4,5},{5,4},{6,7},{7,6},{8,9},{9,8},{10,11... | collective-permute-start | bytes 491528 | tf_op jit(solution)/shard_map/ppermute | solution.py:671
  108.5 10.6 %collective-permute-start.15 = (bf16[256,320]{1,0:T(8,128)(2,1)}, bf16[256,320]{1,0:T(8,128)(2,1)}, u32[]{:S(2)}, u32[]{:S(2)}) collective-permute-start(bf16[256,320]{1,0:T(8,128)(2,1)} %get-tuple-element.55), channel_id=1, source_target_pairs={{0,1},{1,0},{2,3},{3,2},{4,5},{5,4},{6,7},{7,6},{8,9},{9,8},{10,11... | collective-permute-start | bytes 491528 | tf_op jit(solution)/shard_map/ppermute | solution.py:671
  108.8 10.2 %collective-permute-start.16 = (bf16[256,320]{1,0:T(8,128)(2,1)}, bf16[256,320]{1,0:T(8,128)(2,1)}, u32[]{:S(2)}, u32[]{:S(2)}) collective-permute-start(bf16[256,320]{1,0:T(8,128)(2,1)} %get-tuple-element.56), channel_id=1, source_target_pairs={{0,2},{1,3},{2,0},{3,1},{4,6},{5,7},{6,4},{7,5},{8,10},{9,11},{10,... | collective-permute-start | bytes 491528 | tf_op jit(solution)/shard_map/ppermute | solution.py:671
  110.7 9.3 %collective-permute-start.17 = (bf16[256,320]{1,0:T(8,128)(2,1)}, bf16[256,320]{1,0:T(8,128)(2,1)}, u32[]{:S(2)}, u32[]{:S(2)}) collective-permute-start(bf16[256,320]{1,0:T(8,128)(2,1)} %get-tuple-element.57), channel_id=1, source_target_pairs={{0,3},{1,2},{2,1},{3,0},{4,7},{5,6},{6,5},{7,4},{8,11},{9,10},{10,... | collective-permute-start | bytes 491528 | tf_op jit(solution)/shard_map/ppermute | solution.py:671
  270.3 39.3 %collective-permute-start.18 = (bf16[256,320]{1,0:T(8,128)(2,1)S(1)}, bf16[256,320]{1,0:T(8,128)(2,1)S(1)}, u32[]{:S(2)}, u32[]{:S(2)}) collective-permute-start(bf16[256,320]{1,0:T(8,128)(2,1)S(1)} %get-tuple-element.110), channel_id=1, source_target_pairs={{0,1},{1,0},{2,3},{3,2},{4,5},{5,4},{6,7},{7,6},{8,9},{9,8},{10,11... | collective-permute-start | bytes 491528 | tf_op jit(solution)/shard_map/ppermute | solution.py:671
  275.8 8.9 %collective-permute-start.53 = (f32[4,1280]{1,0:T(4,128)S(1)}, f32[4,1280]{1,0:T(4,128)S(1)}, u32[]{:S(2)}, u32[]{:S(2)}) collective-permute-start(f32[4,1280]{1,0:T(4,128)S(1)} %add.340), channel_id=1, source_target_pairs={{0,8},{4,12},{8,0},{12,4},{16,24},{20,28},{24,16},{28,20},{1,9},{5... | collective-permute-start | bytes 61448 | tf_op jit(solution)/shard_map/ppermute | solution.py:671
  279.3 139.8 %collective-permute-start.59 = (bf16[320,1280]{1,0:T(8,128)(2,1)S(1)}, bf16[320,1280]{1,0:T(8,128)(2,1)}, u32[]{:S(2)}, u32[]{:S(2)}) collective-permute-start(bf16[320,1280]{1,0:T(8,128)(2,1)S(1)} %copy-done.23), channel_id=1, source_target_pairs={{1,17},{3,19},{5,21},{7,23},{9,25},{11,27},{13,29},{15,31},{16,0},... | collective-permute-start | bytes 2457608 | tf_op jit(solution)/shard_map/ppermute | solution.py:740
  284.7 8.6 %collective-permute-start.54 = (f32[4,1280]{1,0:T(4,128)S(1)}, f32[4,1280]{1,0:T(4,128)S(1)}, u32[]{:S(2)}, u32[]{:S(2)}) collective-permute-start(f32[4,1280]{1,0:T(4,128)S(1)} %add.341), channel_id=1, source_target_pairs={{0,16},{4,20},{8,24},{12,28},{16,0},{20,4},{24,8},{28,12},{1,17},{... | collective-permute-start | bytes 61448 | tf_op jit(solution)/shard_map/ppermute | solution.py:671
  285.7 132.0 %collective-permute-start.55 = (bf16[2,2,2,80,512]{4,3,2,1,0:T(8,128)(2,1)}, bf16[2,2,2,80,512]{4,3,2,1,0:T(8,128)(2,1)}, u32[]{:S(2)}, u32[]{:S(2)}) collective-permute-start(bf16[2,2,2,80,512]{4,3,2,1,0:T(8,128)(2,1)} %dynamic-slice_bitcast_fusion.6), channel_id=1, source_target_pairs={{0,4},{4,0},{8,12},{12,8},{16,20},{20,16},{24,28},{28,24},{1,5},{5... | collective-permute-start | bytes 1966088 | tf_op jit(solution)/shard_map/ppermute | solution.py:671
  286.5 23.1 %collective-permute-start.19 = (bf16[256,320]{1,0:T(8,128)(2,1)S(1)}, bf16[256,320]{1,0:T(8,128)(2,1)S(1)}, u32[]{:S(2)}, u32[]{:S(2)}) collective-permute-start(bf16[256,320]{1,0:T(8,128)(2,1)S(1)} %get-tuple-element.109), channel_id=1, source_target_pairs={{0,2},{1,3},{2,0},{3,1},{4,6},{5,7},{6,4},{7,5},{8,10},{9,11},{10,... | collective-permute-start | bytes 491528 | tf_op jit(solution)/shard_map/ppermute | solution.py:671
  293.3 20.1 %collective-permute-start.20 = (bf16[256,320]{1,0:T(8,128)(2,1)S(1)}, bf16[256,320]{1,0:T(8,128)(2,1)S(1)}, u32[]{:S(2)}, u32[]{:S(2)}) collective-permute-start(bf16[256,320]{1,0:T(8,128)(2,1)S(1)} %get-tuple-element.100), channel_id=1, source_target_pairs={{0,3},{1,2},{2,1},{3,0},{4,7},{5,6},{6,5},{7,4},{8,11},{9,10},{10,... | collective-permute-start | bytes 491528 | tf_op jit(solution)/shard_map/ppermute | solution.py:671
  309.6 30.0 %collective-permute-start.23 = (bf16[256,320]{1,0:T(8,128)(2,1)}, bf16[256,320]{1,0:T(8,128)(2,1)}, u32[]{:S(2)}, u32[]{:S(2)}) collective-permute-start(bf16[256,320]{1,0:T(8,128)(2,1)} %get-tuple-element.107), channel_id=1, source_target_pairs={{0,1},{1,0},{2,3},{3,2},{4,5},{5,4},{6,7},{7,6},{8,9},{9,8},{10,11... | collective-permute-start | bytes 491528 | tf_op jit(solution)/shard_map/ppermute | solution.py:671
  309.6 30.4 %collective-permute-start.24 = (bf16[256,320]{1,0:T(8,128)(2,1)}, bf16[256,320]{1,0:T(8,128)(2,1)}, u32[]{:S(2)}, u32[]{:S(2)}) collective-permute-start(bf16[256,320]{1,0:T(8,128)(2,1)} %get-tuple-element.106), channel_id=1, source_target_pairs={{0,2},{1,3},{2,0},{3,1},{4,6},{5,7},{6,4},{7,5},{8,10},{9,11},{10,... | collective-permute-start | bytes 491528 | tf_op jit(solution)/shard_map/ppermute | solution.py:671
  313.4 27.3 %collective-permute-start.25 = (bf16[256,320]{1,0:T(8,128)(2,1)}, bf16[256,320]{1,0:T(8,128)(2,1)}, u32[]{:S(2)}, u32[]{:S(2)}) collective-permute-start(bf16[256,320]{1,0:T(8,128)(2,1)} %get-tuple-element.105), channel_id=1, source_target_pairs={{0,3},{1,2},{2,1},{3,0},{4,7},{5,6},{6,5},{7,4},{8,11},{9,10},{10,... | collective-permute-start | bytes 491528 | tf_op jit(solution)/shard_map/ppermute | solution.py:671
  339.6 27.1 %collective-permute-start.28 = (bf16[256,320]{1,0:T(8,128)(2,1)}, bf16[256,320]{1,0:T(8,128)(2,1)}, u32[]{:S(2)}, u32[]{:S(2)}) collective-permute-start(bf16[256,320]{1,0:T(8,128)(2,1)} %get-tuple-element.103), channel_id=1, source_target_pairs={{0,1},{1,0},{2,3},{3,2},{4,5},{5,4},{6,7},{7,6},{8,9},{9,8},{10,11... | collective-permute-start | bytes 491528 | tf_op jit(solution)/shard_map/ppermute | solution.py:671
  340.0 26.8 %collective-permute-start.29 = (bf16[256,320]{1,0:T(8,128)(2,1)S(1)}, bf16[256,320]{1,0:T(8,128)(2,1)}, u32[]{:S(2)}, u32[]{:S(2)}) collective-permute-start(bf16[256,320]{1,0:T(8,128)(2,1)S(1)} %get-tuple-element.102), channel_id=1, source_target_pairs={{0,2},{1,3},{2,0},{3,1},{4,6},{5,7},{6,4},{7,5},{8,10},{9,11},{10,... | collective-permute-start | bytes 491528 | tf_op jit(solution)/shard_map/ppermute | solution.py:671
  340.8 26.0 %collective-permute-start.30 = (bf16[256,320]{1,0:T(8,128)(2,1)S(1)}, bf16[256,320]{1,0:T(8,128)(2,1)}, u32[]{:S(2)}, u32[]{:S(2)}) collective-permute-start(bf16[256,320]{1,0:T(8,128)(2,1)S(1)} %get-tuple-element.101), channel_id=1, source_target_pairs={{0,3},{1,2},{2,1},{3,0},{4,7},{5,6},{6,5},{7,4},{8,11},{9,10},{10,... | collective-permute-start | bytes 491528 | tf_op jit(solution)/shard_map/ppermute | solution.py:671
  366.7 91.9 %collective-permute-start.44 = (bf16[1280,640]{1,0:T(8,128)(2,1)}, bf16[1280,640]{1,0:T(8,128)(2,1)}, u32[]{:S(2)}, u32[]{:S(2)}) collective-permute-start(bf16[1280,640]{1,0:T(8,128)(2,1)} %dynamic-slice_convert_fusion), channel_id=1, source_target_pairs={{0,1},{1,0},{2,3},{3,2},{4,5},{5,4},{6,7},{7,6},{8,9},{9,8},{10,11... | collective-permute-start | bytes 4915208 | tf_op jit(solution)/shard_map/ppermute | solution.py:671
  413.9 36.2 %collective-permute-start.38 = (bf16[2,2,160,960]{3,2,1,0:T(8,128)(2,1)S(1)}, bf16[2,2,160,960]{3,2,1,0:T(8,128)(2,1)S(1)}, u32[]{:S(2)}, u32[]{:S(2)}) collective-permute-start(bf16[2,2,160,960]{3,2,1,0:T(8,128)(2,1)S(1)} %dynamic-slice_bitcast_fusion.4), channel_id=1, source_target_pairs={{0,4},{4,0},{8,12},{12,8},{16,20},{20,16},{24,28},{28,24},{1,5},{5... | collective-permute-start | bytes 3686408 | tf_op jit(solution)/shard_map/ppermute | solution.py:671
  416.6 34.3 %collective-permute-start.21 = (bf16[2,256,1280]{2,1,0:T(8,128)(2,1)S(1)}, bf16[2,256,1280]{2,1,0:T(8,128)(2,1)S(1)}, u32[]{:S(2)}, u32[]{:S(2)}) collective-permute-start(bf16[2,256,1280]{2,1,0:T(8,128)(2,1)S(1)} %pad_maximum_fusion.5), channel_id=1, source_target_pairs={{0,1},{1,0},{2,3},{3,2},{4,5},{5,4},{6,7},{7,6},{8,9},{9,8},{10,11... | collective-permute-start | bytes 3932168 | tf_op jit(solution)/shard_map/ppermute | solution.py:671
  417.7 35.2 %collective-permute-start.26 = (bf16[2,256,1280]{2,1,0:T(8,128)(2,1)S(1)}, bf16[2,256,1280]{2,1,0:T(8,128)(2,1)S(1)}, u32[]{:S(2)}, u32[]{:S(2)}) collective-permute-start(bf16[2,256,1280]{2,1,0:T(8,128)(2,1)S(1)} %pad_maximum_fusion.6), channel_id=1, source_target_pairs={{0,1},{1,0},{2,3},{3,2},{4,5},{5,4},{6,7},{7,6},{8,9},{9,8},{10,11... | collective-permute-start | bytes 3932168 | tf_op jit(solution)/shard_map/ppermute | solution.py:671
  419.1 8.9 %collective-permute-start.56 = (bf16[2,2,80,512]{3,2,1,0:T(8,128)(2,1)S(1)}, bf16[2,2,80,512]{3,2,1,0:T(8,128)(2,1)S(1)}, u32[]{:S(2)}, u32[]{:S(2)}) collective-permute-start(bf16[2,2,80,512]{3,2,1,0:T(8,128)(2,1)S(1)} %dynamic-slice_bitcast_fusion.10), channel_id=1, source_target_pairs={{0,2},{1,3},{2,0},{3,1},{4,6},{5,7},{6,4},{7,5},{8,10},{9,11},{10,... | collective-permute-start | bytes 983048 | tf_op jit(solution)/shard_map/ppermute | solution.py:671
  431.8 17.8 %collective-permute-start.57 = (bf16[80,2560]{1,0:T(8,128)(2,1)S(1)}, bf16[80,2560]{1,0:T(8,128)(2,1)S(1)}, u32[]{:S(2)}, u32[]{:S(2)}) collective-permute-start(bf16[80,2560]{1,0:T(8,128)(2,1)S(1)} %dynamic-slice_bitcast_fusion.8), channel_id=1, source_target_pairs={{0,16},{4,20},{8,24},{12,28},{16,0},{20,4},{24,8},{28,12},{1,17},{... | collective-permute-start | bytes 1228808 | tf_op jit(solution)/shard_map/ppermute | solution.py:671
  449.6 5.2 collective-permute-start.31
  450.2 6.5 %collective-permute-start.58 = (bf16[40,2560]{1,0:T(8,128)(2,1)S(1)}, bf16[40,2560]{1,0:T(8,128)(2,1)S(1)}, u32[]{:S(2)}, u32[]{:S(2)}) collective-permute-start(bf16[40,2560]{1,0:T(8,128)(2,1)S(1)} %fusion.85), channel_id=1, source_target_pairs={{0,1},{1,0},{2,3},{3,2},{4,5},{5,4},{6,7},{7,6},{8,9},{9,8},{10,11... | collective-permute-start | bytes 614408 | tf_op jit(solution)/shard_map/ppermute | solution.py:671
  451.0 51.9 %collective-permute-start.39 = (bf16[2,160,960]{2,1,0:T(8,128)(2,1)S(1)}, bf16[2,160,960]{2,1,0:T(8,128)(2,1)S(1)}, u32[]{:S(2)}, u32[]{:S(2)}) collective-permute-start(bf16[2,160,960]{2,1,0:T(8,128)(2,1)S(1)} %dynamic-slice_bitcast_fusion.7), channel_id=1, source_target_pairs={{0,8},{4,12},{8,0},{12,4},{16,24},{20,28},{24,16},{28,20},{1,9},{5... | collective-permute-start | bytes 1843208 | tf_op jit(solution)/shard_map/ppermute | solution.py:671
  452.9 16.0 %collective-permute-start.22 = (bf16[256,1280]{1,0:T(8,128)(2,1)S(1)}, bf16[256,1280]{1,0:T(8,128)(2,1)S(1)}, u32[]{:S(2)}, u32[]{:S(2)}) collective-permute-start(bf16[256,1280]{1,0:T(8,128)(2,1)S(1)} %fusion.45), channel_id=1, source_target_pairs={{0,2},{1,3},{2,0},{3,1},{4,6},{5,7},{6,4},{7,5},{8,10},{9,11},{10,... | collective-permute-start | bytes 1966088 | tf_op jit(solution)/shard_map/ppermute | solution.py:671
  454.8 28.1 %collective-permute-start.27 = (bf16[256,1280]{1,0:T(8,128)(2,1)S(1)}, bf16[256,1280]{1,0:T(8,128)(2,1)S(1)}, u32[]{:S(2)}, u32[]{:S(2)}) collective-permute-start(bf16[256,1280]{1,0:T(8,128)(2,1)S(1)} %fusion.46), channel_id=1, source_target_pairs={{0,2},{1,3},{2,0},{3,1},{4,6},{5,7},{6,4},{7,5},{8,10},{9,11},{10,... | collective-permute-start | bytes 1966088 | tf_op jit(solution)/shard_map/ppermute | solution.py:671
  456.7 40.1 %collective-permute-start.32 = (bf16[256,1280]{1,0:T(8,128)(2,1)S(1)}, bf16[256,1280]{1,0:T(8,128)(2,1)S(1)}, u32[]{:S(2)}, u32[]{:S(2)}) collective-permute-start(bf16[256,1280]{1,0:T(8,128)(2,1)S(1)} %fusion.47), channel_id=1, source_target_pairs={{0,2},{1,3},{2,0},{3,1},{4,6},{5,7},{6,4},{7,5},{8,10},{9,11},{10,... | collective-permute-start | bytes 1966088 | tf_op jit(solution)/shard_map/ppermute | solution.py:671
  461.7 70.3 %collective-permute-start.45 = (bf16[2,2,2,80,640]{4,3,2,1,0:T(8,128)(2,1)}, bf16[2,2,2,80,640]{4,3,2,1,0:T(8,128)(2,1)}, u32[]{:S(2)}, u32[]{:S(2)}) collective-permute-start(bf16[2,2,2,80,640]{4,3,2,1,0:T(8,128)(2,1)} %dynamic-slice_bitcast_fusion.5), channel_id=1, source_target_pairs={{0,4},{4,0},{8,12},{12,8},{16,20},{20,16},{24,28},{28,24},{1,5},{5... | collective-permute-start | bytes 2457608 | tf_op jit(solution)/shard_map/ppermute | solution.py:671
  505.2 19.0 %collective-permute-start.40 = (bf16[160,960]{1,0:T(8,128)(2,1)}, bf16[160,960]{1,0:T(8,128)(2,1)}, u32[]{:S(2)}, u32[]{:S(2)}) collective-permute-start(bf16[160,960]{1,0:T(8,128)(2,1)} %dynamic-slice_bitcast_fusion.11), channel_id=1, source_target_pairs={{0,16},{4,20},{8,24},{12,28},{16,0},{20,4},{24,8},{28,12},{1,17},{... | collective-permute-start | bytes 921608 | tf_op jit(solution)/shard_map/ppermute | solution.py:671
  514.1 8.9 %collective-permute-start.37 = (f32[2,1280]{1,0:T(2,128)S(1)}, f32[2,1280]{1,0:T(2,128)S(1)}, u32[]{:S(2)}, u32[]{:S(2)}) collective-permute-start(f32[2,1280]{1,0:T(2,128)S(1)} %add.308), channel_id=1, source_target_pairs={{0,16},{4,20},{8,24},{12,28},{16,0},{20,4},{24,8},{28,12},{1,17},{... | collective-permute-start | bytes 30728 | tf_op jit(solution)/shard_map/ppermute | solution.py:671
  533.4 10.7 %collective-permute-start.46 = (bf16[2,2,80,640]{3,2,1,0:T(8,128)(2,1)S(1)}, bf16[2,2,80,640]{3,2,1,0:T(8,128)(2,1)S(1)}, u32[]{:S(2)}, u32[]{:S(2)}) collective-permute-start(bf16[2,2,80,640]{3,2,1,0:T(8,128)(2,1)S(1)} %dynamic-slice_bitcast_fusion.9), channel_id=1, source_target_pairs={{0,8},{4,12},{8,0},{12,4},{16,24},{20,28},{24,16},{28,20},{1,9},{5... | collective-permute-start | bytes 1228808 | tf_op jit(solution)/shard_map/ppermute | solution.py:671
  544.3 12.3 %collective-permute-start.47 = (bf16[2,80,640]{2,1,0:T(8,128)(2,1)S(1)}, bf16[2,80,640]{2,1,0:T(8,128)(2,1)S(1)}, u32[]{:S(2)}, u32[]{:S(2)}) collective-permute-start(bf16[2,80,640]{2,1,0:T(8,128)(2,1)S(1)} %dynamic-slice_bitcast_fusion.12), channel_id=1, source_target_pairs={{0,16},{4,20},{8,24},{12,28},{16,0},{20,4},{24,8},{28,12},{1,17},{... | collective-permute-start | bytes 614408 | tf_op jit(solution)/shard_map/ppermute | solution.py:671
  (100 other events, 602.9 us)

commit v3 on v2

--- a/solution.py
+++ b/solution.py
@@ -1,4 +1,5 @@
 import functools
+import itertools
 import math
 
 import jax
@@ -302,30 +303,31 @@
 TILE = 512
 SPAN = 256
 CHUNK = 256
-DOWN_ITEMS = ((0, 512, "xyz"), (512, 1024, "yzx"), (1024, 1280, "zxy"))
-UP_ORDERS = ("xyz", "yzx", "xyz", "zxy", "zxy")
-UP_WHOLE = 3
+DOWN_ITEMS = ((0, 512, "xyz"), (512, 1024, "yxz"), (1024, 1280, "zxy"))
+DOWN_CUT = 1024
+UP_ORDERS = ("zxy", "zxy", "yxz", "zxy", "yxz")
+UP_SLOT = (0, 1, 3, 2, 4)
 
 
 def add_pieces(total, view, got):
     lead = len(total.shape) - 2
-    tail = view[lead:] + (slice(None),) * (len(total.shape) - max(len(view), lead))
+    tail = tuple(view[lead:]) + (slice(None),) * (len(total.shape) - max(len(view), lead))
     free = [i for i in range(lead) if isinstance(view[i], slice)]
-    for n in range(2 ** len(free)):
-        pick = [(n >> i) & 1 for i in range(len(free))]
+    for pick in itertools.product(*[range(total.shape[i]) for i in free]):
         index = list(view[:lead])
-        for i, bit in zip(free, pick):
-            index[i] = bit
+        for i, n in zip(free, pick):
+            index[i] = n
         here = tuple(index) + tail
-        total[here] = (total[here].astype(F32) + got[tuple(pick)].astype(F32)).astype(BF)
+        add = got[pick] if pick else got[...]
+        total[here] = (total[here].astype(F32) + add.astype(F32)).astype(BF)
 
 
 def feed_sum_kernel(
     second_in, low_in, up, down,
-    back_out, result_out, down_out, up_out, up_rest,
+    back_out, result_out, down_ab, down_c, up_z, up_y,
     second, low, second_t, active, slope, down_part, up_part,
     wide_buf, tall_buf, flat_buf, thin_buf, stage,
-    ra1, ra2, ra3, rb1, rb2, rb3, rc1, rc2, rc3, ru1, ru2, ru3,
+    ra1, ra2, rb1, rb2, rc1, rc2, up_recv,
     load_sem, weight_sem, out_sem, end_sem, swap_send, swap_recv, sum_send, sum_recv,
     ready_second, ready_low,
 ):
@@ -417,17 +419,16 @@
             index[axis] = 1 - mine[axis] if (s == stage_no and other) else mine[axis]
         return (slice(None), index["z"], index["x"], index["y"])
 
-    down_recv = ((ra1, ra2, ra3), (rb1, rb2, rb3), (rc1, rc2, rc3))
-    up_recv = (ru1, ru2, ru3)
+    down_recv = ((ra1, ra2), (rb1, rb2), (rc1, rc2))
 
     def go_down(item, stage_no, fix_z=None):
         lo, hi, order = DOWN_ITEMS[item]
         src = down_part.at[down_view(order, stage_no, lo, hi, True, fix_z)]
         dst = down_recv[item][stage_no]
-        sem = item * 4 + stage_no
+        sem = item * 3 + stage_no
         if fix_z is not None:
             dst = dst.at[fix_z]
-            sem = item * 4 + (3 if fix_z else 0)
+            sem = item * 3 + (2 if fix_z else 0)
         copy = remote(src, dst, sum_send.at[sem], sum_recv.at[sem], near[order[stage_no]])
         flight.setdefault(("d", item, stage_no), []).append(copy)
         sent.append(copy)
@@ -437,25 +438,23 @@
         for copy in flight[("d", item, stage_no)]:
             copy.wait_recv()
         add_pieces(down_part, down_view(order, stage_no, lo, hi, False), down_recv[item][stage_no])
-        if stage_no < 2:
+        if stage_no < 1:
             go_down(item, stage_no + 1)
 
-    def go_up(j, stage_no):
+    def go_up(j):
         order = UP_ORDERS[j]
-        src = up_part.at[j].at[up_view(order, stage_no, True)]
-        sem = 12 + 3 * j + stage_no
+        slot = UP_SLOT[j]
         copy = remote(
-            src, up_recv[stage_no].at[j], sum_send.at[sem], sum_recv.at[sem], near[order[stage_no]]
+            up_part.at[slot].at[up_view(order, 0, True)], up_recv.at[slot],
+            sum_send.at[9 + j], sum_recv.at[9 + j], near[order[0]],
         )
-        flight[("u", j, stage_no)] = [copy]
+        flight[("u", j)] = copy
         sent.append(copy)
 
-    def end_up(j, stage_no):
-        flight[("u", j, stage_no)][0].wait_recv()
-        view = (j,) + up_view(UP_ORDERS[j], stage_no, False)
-        add_pieces(up_part, view, up_recv[stage_no].at[j])
-        if stage_no < 2 and j < UP_WHOLE:
-            go_up(j, stage_no + 1)
+    def end_up(j, _):
+        flight[("u", j)].wait_recv()
+        slot = UP_SLOT[j]
+        add_pieces(up_part, (slot,) + up_view(UP_ORDERS[j], 0, False), up_recv.at[slot])
 
     def down_rows(row):
         block = row // 320
@@ -505,7 +504,7 @@
     go_down(2, 0)
     for copy in swaps:
         copy.wait_send()
-        sent.remove(copy)
+        sent[:] = [other for other in sent if other is not copy]
     pl.semaphore_signal(ready_second, inc=1, device_id=sibling, device_id_type=MESH)
 
     for j in range(tiles):
@@ -526,25 +525,18 @@
             ).astype(BF)
             for s in range(4):
                 k = 4 * m + s
-                up_part[j, k // 8, (k // 4) % 2, (k // 2) % 2, k % 2] = grad[s * 80 : (s + 1) * 80]
-        go_up(j, 0)
-        if j == 3:
-            end_down(2, 0)
-        if j == 4:
-            end_down(0, 0)
-            end_down(1, 0)
+                up_part[UP_SLOT[j], k // 8, (k // 4) % 2, (k // 2) % 2, k % 2] = grad[s * 80 : (s + 1) * 80]
+        go_up(j)
+    end_down(0, 0)
     pl.semaphore_signal(ready_low, inc=1, device_id=sibling, device_id_type=MESH)
 
     events = {
-        0: [(end_down, 2, 1), (end_up, 0, 0)],
-        2: [(end_up, 1, 0), (end_down, 0, 1)],
-        4: [(end_down, 1, 1), (end_down, 2, 2)],
-        5: [(end_up, 2, 0), (end_up, 0, 1)],
-        6: [(end_up, 1, 1)],
-        8: [(end_up, 2, 1), (end_up, 3, 0)],
+        0: [(end_down, 1, 0)],
+        2: [(end_down, 2, 0)],
+        8: [(end_up, 0, 0)],
         9: [
-            (end_down, 0, 2), (end_down, 1, 2), (end_up, 0, 2), (end_up, 1, 2), (end_up, 2, 2),
-            (end_up, 4, 0),
+            (end_up, 2, 0), (end_down, 1, 1), (end_down, 2, 1), (end_up, 1, 0), (end_up, 3, 0),
+            (end_up, 4, 0), (end_down, 0, 1),
         ],
     }
     pending = []
@@ -590,14 +582,14 @@
         for event, item, stage_no in events.get(step, ()):
             event(item, stage_no)
     finish(*pending.pop())
+    views = (
+        (down_part.at[:, mine["x"], mine["y"], :, :DOWN_CUT], down_ab),
+        (down_part.at[mine["z"], mine["x"], :, :, DOWN_CUT:], down_c),
+        (up_part.at[:3, :, mine["z"]], up_z),
+        (up_part.at[3:, :, :, :, mine["y"]], up_y),
+    )
     ends = [
-        pltpu.make_async_copy(
-            down_part.at[mine["z"], mine["x"], mine["y"]], down_out, end_sem.at[0]
-        ),
-        pltpu.make_async_copy(
-            up_part.at[:UP_WHOLE, :, mine["z"], mine["x"], mine["y"]], up_out, end_sem.at[1]
-        ),
-        pltpu.make_async_copy(up_part.at[UP_WHOLE:, :, mine["z"]], up_rest, end_sem.at[2]),
+        pltpu.make_async_copy(src, dst, end_sem.at[i]) for i, (src, dst) in enumerate(views)
     ]
     for copy in ends:
         copy.start()
@@ -620,24 +612,20 @@
         recv += [
             pltpu.VMEM((2, 2, 320, hi - lo), BF),
             pltpu.VMEM((2, 320, hi - lo), BF),
-            pltpu.VMEM((320, hi - lo), BF),
         ]
-    recv += [
-        pltpu.VMEM((tiles, 2, 2, 2, 80, TILE), BF),
-        pltpu.VMEM((UP_WHOLE, 2, 2, 80, TILE), BF),
-        pltpu.VMEM((UP_WHOLE, 2, 80, TILE), BF),
-    ]
+    recv += [pltpu.VMEM((tiles, 2, 2, 2, 80, TILE), BF)]
     dma = pltpu.SemaphoreType.DMA
     return pl.pallas_call(
         feed_sum_kernel,
         in_specs=[anywhere] * 4,
-        out_specs=[anywhere] * 5,
+        out_specs=[anywhere] * 6,
         out_shape=[
             jax.ShapeDtypeStruct((rows, width), F32),
             jax.ShapeDtypeStruct((rows, width), F32),
-            jax.ShapeDtypeStruct((320, width), BF),
-            jax.ShapeDtypeStruct((UP_WHOLE, 2, 80, TILE), BF),
-            jax.ShapeDtypeStruct((tiles - UP_WHOLE, 2, 2, 2, 80, TILE), BF),
+            jax.ShapeDtypeStruct((2, 320, DOWN_CUT), BF),
+            jax.ShapeDtypeStruct((2, 320, width - DOWN_CUT), BF),
+            jax.ShapeDtypeStruct((3, 2, 2, 2, 80, TILE), BF),
+            jax.ShapeDtypeStruct((tiles - 3, 2, 2, 2, 80, TILE), BF),
         ],
         scratch_shapes=[
             pltpu.VMEM((two, width), BF),
@@ -655,7 +643,7 @@
         ]
         + recv
         + [
-            dma((2,)), dma((6,)), dma((2,)), dma((3,)), dma((12,)), dma((12,)), dma((27,)), dma((27,)),
+            dma((2,)), dma((6,)), dma((2,)), dma((4,)), dma((12,)), dma((12,)), dma((14,)), dma((14,)),
             pltpu.SemaphoreType.REGULAR, pltpu.SemaphoreType.REGULAR,
         ],
         compiler_params=pltpu.CompilerParams(
@@ -664,6 +652,529 @@
         cost_estimate=cost(2 * 6 * two * width * units, 6e7),
         name="feed_sum",
     )(second, low, up, down)
+
+
+QUERY_ITEMS = ((0, 512, "xzh"), (512, 960, "zxh"))
+
+
+def row_dot(left, right, exact_left):
+    wide = right if exact_left else left
+    high = wide.astype(BF)
+    low = (wide - high.astype(F32)).astype(BF)
+    pairs = ((left, high), (left, low)) if exact_left else ((high, right), (low, right))
+    return sum(lax.dot_general(a, b, NT, preferred_element_type=F32) for a, b in pairs)
+
+
+def attend_sum_kernel(
+    block, heads,
+    lens, g0, g1, g2, g3, kept, *refs
+):
+    firsts = refs[:12]
+    (
+        weight, up_z_in, up_y_in, out_in, down_ab_in, down_c_in, early_in, tokens_in, through_in, gain,
+        tokens_out, query_out, up_z_out, up_y_out, out_out, down_out, early_out, late_out,
+        grads, qkv_c, first, weights, back, moved, total, query_part,
+        up_z, up_y, out_part, down_ab, down_c, down_part, got_ab, got_c,
+        keep_back, got_near, got_far, got_over,
+        qa1, qa2, qa3, qb1, qb2, qb3, query_last, query_got,
+        uz1, uz2, uz3, up_z_last, up_z_got, uy1, uy2, uy3, up_y_last, up_y_got,
+        oc1, oc2, oc3, oc4, oc5, out_last, out_got, down_got, down_last, early, early_got, late, late_got, column_sum, norm_in,
+        load_sem, first_sem, turn_send, turn_recv, back_send, back_recv, sum_send, sum_recv, end_sem, norm_sem,
+    ) = refs[12:]
+    sources = (g0, g1, g2, g3)
+    cells = kept.shape[0]
+    rows = g0.shape[1]
+    wide = heads * HEAD_DIM
+    cell = lax.axis_index("cells")
+    place = lax.axis_index("chrom")
+    core = place % 2
+    mine = {"c": core, "y": place // 2, "x": cell % 2, "z": (cell // 2) % 2, "h": cell // 4}
+
+    def chrom_near(r):
+        return (place // 2 + r // 2) % 2 * 2 + (core + r % 2) % 2
+
+    near = {
+        "c": (cell, chrom_near(1)),
+        "y": (cell, chrom_near(2)),
+        "x": (cell + 1 - 2 * mine["x"], place),
+        "z": (cell + 2 - 4 * mine["z"], place),
+        "h": (cell + 4 - 8 * mine["h"], place),
+    }
+    far = (cell, chrom_near(3))
+    by_part = (None, near["c"], near["y"], far)
+
+    barrier = pltpu.get_barrier_semaphore()
+    for other in (*near.values(), far):
+        pl.semaphore_signal(barrier, inc=1, device_id=other, device_id_type=MESH)
+
+    def load(src, dst, sem):
+        copy = pltpu.make_async_copy(src, dst, sem)
+        copy.start()
+        return copy
+
+    def load_own(c):
+        return [
+            load(g0.at[c], grads.at[c, 0], load_sem.at[2 * c]),
+            load(kept.at[c], qkv_c.at[c % 2], load_sem.at[2 * c + 1]),
+        ]
+
+    own_loads = {c: load_own(c) for c in range(2)}
+    extra = [
+        load(down_ab_in, down_ab, load_sem.at[6]),
+        load(down_c_in, down_c, load_sem.at[11]),
+        load(up_z_in, up_z, load_sem.at[7]),
+        load(up_y_in, up_y, load_sem.at[8]),
+        load(out_in, out_part, load_sem.at[9]),
+        load(weight, weights, load_sem.at[10]),
+    ]
+
+    def load_first(c):
+        return [
+            load(
+                firsts[4 * c + r],
+                first.at[c % 2, r * rows : (r + 1) * rows],
+                first_sem.at[4 * c + r],
+            )
+            for r in range(4)
+        ]
+
+    first_loads = {c: load_first(c) for c in range(2)}
+    early_load = load(early_in, early.at[0], load_sem.at[12])
+    pl.semaphore_wait(barrier, 6)
+
+    def remote(src, dst, send, recv, device, start=True):
+        copy = pltpu.make_async_remote_copy(
+            src_ref=src, dst_ref=dst, send_sem=send, recv_sem=recv,
+            device_id=device, device_id_type=MESH,
+        )
+        if start:
+            copy.start()
+        return copy
+
+    sent = []
+
+    def turn(c):
+        line = []
+        for r in (2, 3, 1):
+            n = 3 * c + r - 1
+            line.append(
+                remote(sources[r].at[c], grads.at[c, r], turn_send.at[n], turn_recv.at[n], by_part[r])
+            )
+        sent.extend(line)
+        return line
+
+    turns = {0: turn(0)}
+
+    sems = iter(range(64))
+    items = {}
+
+    def item(name, part, dims, stages, recvs, cols=slice(None)):
+        items[name] = (part, dims, stages, recvs, cols, [next(sems) for _ in stages], {})
+
+    item("uz", up_z, "*hxy", "xyh", (uz1, uz2, uz3))
+    item("uy", up_y, "*hzx", "zxh", (uy1, uy2, uy3))
+    item("o", out_part, "chzxy", "czxyh", (oc1, oc2, oc3, oc4, oc5))
+    item("da", down_ab, "z", "z", (got_ab,))
+    item("dc", down_c, "y", "y", (got_c,))
+    for n, (lo, hi, stages) in enumerate(QUERY_ITEMS):
+        item("q%d" % n, query_part, "hzx", stages, ((qa1, qa2, qa3), (qb1, qb2, qb3))[n], slice(lo, hi))
+
+    def view(name, s, other):
+        _, dims, stages, _, cols, _, _ = items[name]
+        index = [slice(None)] * len(dims)
+        for t, axis in enumerate(stages[: s + 1]):
+            index[dims.index(axis)] = 1 - mine[axis] if (t == s and other) else mine[axis]
+        return tuple(index) + (slice(None), cols)
+
+    def go(name, s):
+        part, _, stages, recvs, _, ids, flight = items[name]
+        copy = remote(
+            part.at[view(name, s, True)], recvs[s],
+            sum_send.at[ids[s]], sum_recv.at[ids[s]], near[stages[s]],
+        )
+        flight[s] = copy
+        sent.append(copy)
+
+    def end(name, s):
+        part, _, stages, recvs, _, _, flight = items[name]
+        flight[s].wait_recv()
+        add_pieces(part, view(name, s, False), recvs[s])
+        if s + 1 < len(stages):
+            go(name, s + 1)
+
+    lasts = {
+        "uz": (up_z, up_z_last, up_z_got, next(sems)),
+        "uy": (up_y, up_y_last, up_y_got, next(sems)),
+        "o": (out_part, out_last, out_got, next(sems)),
+    }
+
+    def swap_last(name, _):
+        part, last, got, sem = lasts[name]
+        at = view(name, len(items[name][2]) - 1, False)
+        half = part.shape[-2] // 2
+        tiles = part.shape[0] if name != "o" else 1
+        for t in range(tiles):
+            here = (t,) + at[1:] if name != "o" else at
+            values = part[here]
+            for k in range(2):
+                last[k, t] = values[k * half : (k + 1) * half]
+        copy = remote(last.at[1 - core], got, sum_send.at[sem], sum_recv.at[sem], near["c"])
+        sent.append(copy)
+        items[name][6]["last"] = copy
+
+    down_sems = (next(sems), next(sems))
+
+    def down_far():
+        return remote(
+            down_part, down_got, sum_send.at[down_sems[0]], sum_recv.at[down_sems[0]], near["h"], False
+        )
+
+    def down_near():
+        return remote(
+            down_part.at[1 - core], down_last, sum_send.at[down_sems[1]], sum_recv.at[down_sems[1]],
+            near["c"], False,
+        )
+
+    def down_start(*_):
+        for k in range(2):
+            half = slice(k * 160, (k + 1) * 160)
+            down_part[k, :, :DOWN_CUT] = down_ab[mine["z"], half, :]
+            down_part[k, :, DOWN_CUT:] = down_c[mine["y"], half, :]
+
+        @pl.when(core != mine["h"])
+        def _():
+            down_far().start()
+
+    def down_add(*_):
+        @pl.when(core == mine["h"])
+        def _():
+            down_far().wait_recv()
+            for k in range(2):
+                down_part[k] = (down_part[k].astype(F32) + down_got[k].astype(F32)).astype(BF)
+            down_near().start()
+            down_last[...] = down_part[core]
+
+    def down_end(*_):
+        @pl.when(core != mine["h"])
+        def _():
+            down_far().wait_send()
+            down_near().wait_recv()
+
+        @pl.when(core == mine["h"])
+        def _():
+            down_near().wait_send()
+
+    vectors = {"early": (early, early_got, 26), "late": (late, late_got, 31)}
+
+    def vector_go(name, s):
+        stack, got, sem = vectors[name]
+        copy = remote(
+            stack.at[s], got.at[s], sum_send.at[sem + s], sum_recv.at[sem + s], near["cyxzh"[s]]
+        )
+        flights[name, s] = copy
+        sent.append(copy)
+
+    def vector_end(name, s):
+        stack, got, _ = vectors[name]
+        flights[name, s].wait_recv()
+        stack[s + 1] = stack[s] + got[s]
+        if s < 4:
+            vector_go(name, s + 1)
+
+    flights = {}
+
+    for copy in extra:
+        copy.wait()
+    go("da", 0)
+    go("dc", 0)
+    go("uz", 0)
+    go("uy", 0)
+    go("o", 0)
+    early_load.wait()
+    vector_go("early", 0)
+
+    near_copies, over_copies, norm_loads = {}, {}, {}
+
+    def back_sum(c, _):
+        near_copies[c][1].wait_recv()
+        mid = slice(512, 768)
+        first[c % 2, mid] = (first[c % 2, mid].astype(F32) + got_far[c].astype(F32)).astype(BF)
+        over_copies[c] = remote(
+            first.at[c % 2, mid], got_over.at[c], back_send.at[3 * c + 2], back_recv.at[3 * c + 2], near["y"]
+        )
+        sent.append(over_copies[c])
+        norm_loads[c] = [
+            load(tokens_in.at[c], norm_in, norm_sem.at[2 * c]),
+            load(through_in.at[c], got_far.at[c], norm_sem.at[2 * c + 1]),
+        ]
+
+    def back_end(c, _):
+        near_copies[c][0].wait_recv()
+        over_copies[c].wait_recv()
+        for copy in norm_loads[c]:
+            copy.wait()
+
+        def some(i, carry):
+            here = pl.ds(pl.multiple_of(i * 64, 64), 64)
+            values = norm_in[here, :].astype(F32)
+            center = values - jnp.mean(values, axis=1, keepdims=True)
+            inverse = lax.rsqrt(jnp.mean(center * center, axis=1, keepdims=True) + EPS)
+            normed = center * inverse
+            scaled = keep_back[c, here, :] + got_near[c, here, :].astype(F32)
+            scaled = (scaled + got_over[c, here, :].astype(F32)) * gain[...]
+            keep_back[c, here, :] = got_far[c, here, :].astype(F32) + inverse * (
+                scaled
+                - jnp.mean(scaled, axis=1, keepdims=True)
+                - normed * jnp.mean(scaled * normed, axis=1, keepdims=True)
+            )
+            return carry
+
+        lax.fori_loop(0, rows // 64, some, 0)
+        ends.append(load(keep_back.at[c], tokens_out.at[c], end_sem.at[c]))
+        if c + 2 < cells:
+            for copy in (*near_copies[c], over_copies[c]):
+                copy.wait_send()
+                sent[:] = [other for other in sent if other is not copy]
+            first_loads[c + 2] = load_first(c + 2)
+
+    ends = []
+    events = {
+        (0, 0): [(end, "o", 0), (vector_end, "early", 0)],
+        (0, 1): [(vector_end, "early", 1)],
+        (0, 2): [(end, "dc", 0), (vector_end, "early", 2)],
+        (0, 3): [(end, "uz", 0), (vector_end, "early", 3)],
+        (0, 4): [(end, "uy", 0), (end, "da", 0), (down_start, 0, 0), (vector_end, "early", 4)],
+        (0, 6): [(end, "uy", 1)],
+        (1, 0): [(end, "uz", 1), (back_sum, 0, 0)],
+        (1, 1): [(end, "o", 1)],
+        (1, 2): [(end, "uy", 2), (swap_last, "uy", 0), (down_add, 0, 0)],
+        (1, 3): [(end, "o", 2)],
+        (1, 4): [(end, "uz", 2), (swap_last, "uz", 0), (down_end, 0, 0)],
+        (1, 5): [(end, "o", 3)],
+        (1, 6): [(back_end, 0, 0)],
+        (2, 0): [(end, "o", 4), (swap_last, "o", 0), (back_sum, 1, 0)],
+        (2, 4): [(back_end, 1, 0)],
+    }
+
+    def run(key):
+        for event, a, b in events.get(key, ()):
+            event(a, b)
+
+    scale = LOG2E / math.sqrt(HEAD_DIM)
+    inv_root = 1.0 / math.sqrt(HEAD_DIM)
+    chunk = 256
+    per = rows // block
+    for c in range(cells):
+        own_loads[c][0].wait()
+        own_loads[c][1].wait()
+        for copy in turns[c]:
+            copy.wait_recv()
+        if c + 1 < cells:
+            turns[c + 1] = turn(c + 1)
+        ranks, columns = [], []
+        at = 0
+        for b in range(4 * per):
+            slot = lax.broadcasted_iota(jnp.int32, (1, block), 1)
+            ranks.append(jnp.where(slot < lens[c, b], slot + at, -1))
+            slot = lax.broadcasted_iota(jnp.int32, (block, 1), 0)
+            columns.append(jnp.where(slot < lens[c, b], slot + at, -1))
+            at = at + lens[c, b]
+        packed = jnp.zeros((wide, FILLED), F32)
+        for r in range(4):
+            rank = jnp.concatenate(ranks[r * per : (r + 1) * per], axis=1)
+            line = lax.broadcasted_iota(jnp.int32, (FILLED, rows), 0)
+            move = jnp.where(line == rank, 1.0, 0.0).astype(BF)
+            grad = grads[c, r].astype(F32).T.astype(BF)
+            packed = packed + lax.dot_general(grad, move, NT, preferred_element_type=F32)
+        query_t = qkv_c[c % 2, :, :wide].astype(F32).T.astype(BF)
+        key_t = qkv_c[c % 2, :, wide : 2 * wide].astype(F32).T.astype(BF)
+        for h in range(heads):
+            lo = h * HEAD_DIM
+            k = qkv_c[c % 2, :, wide + lo : wide + lo + HEAD_DIM]
+            v = qkv_c[c % 2, :, 2 * wide + lo : 2 * wide + lo + HEAD_DIM]
+            kt = key_t[lo : lo + HEAD_DIM, :]
+            dv = jnp.zeros((FILLED, HEAD_DIM), F32)
+            dk = jnp.zeros((FILLED, HEAD_DIM), F32)
+            for w in range(0, FILLED, chunk):
+                qt = query_t[lo : lo + HEAD_DIM, w : w + chunk]
+                s = jnp.dot(k, qt, preferred_element_type=F32)
+                top = jnp.max(s, axis=0, keepdims=True) * scale
+                e = jnp.exp2(s * scale - top)
+                inv = 1.0 / jnp.sum(e, axis=0, keepdims=True)
+                gt = (packed[lo : lo + HEAD_DIM, w : w + chunk] * inv).astype(BF)
+                dp = jnp.dot(v, gt, preferred_element_type=F32)
+                inner = jnp.sum(e * dp, axis=0, keepdims=True) * inv
+                ds = (e * (dp - inner)).astype(BF)
+                dv = dv + lax.dot_general(e.astype(BF), gt, NT, preferred_element_type=F32)
+                dk = dk + lax.dot_general(ds, qt, NT, preferred_element_type=F32)
+                dqt = jnp.dot(kt, ds, preferred_element_type=F32)
+                back[w : w + chunk, lo : lo + HEAD_DIM] = (dqt.T * inv_root).astype(BF)
+            back[:, wide + lo : wide + lo + HEAD_DIM] = (dk * inv_root).astype(BF)
+            back[:, 2 * wide + lo : 2 * wide + lo + HEAD_DIM] = dv.astype(BF)
+            run((c, h))
+        if c + 2 < cells:
+            own_loads[c + 2] = load_own(c + 2)
+        for r in range(4):
+            rank = jnp.concatenate(columns[r * per : (r + 1) * per], axis=0)
+            line = lax.broadcasted_iota(jnp.int32, (rows, FILLED), 1)
+            move = jnp.where(line == rank, 1.0, 0.0).astype(BF)
+            moved[r * rows : (r + 1) * rows, :] = jnp.dot(
+                move, back[...], preferred_element_type=F32
+            ).astype(BF)
+        for copy in first_loads[c]:
+            copy.wait()
+        ones = jnp.ones((8, 4 * rows), BF)
+        part = jnp.dot(ones, moved[...], preferred_element_type=F32)
+        column_sum[...] = part + column_sum[...] if c else part
+        for m in range(first.shape[2] // CHUNK):
+            cols = slice(m * CHUNK, (m + 1) * CHUNK)
+            part = jnp.dot(first[c % 2, :, cols].T, moved[...], preferred_element_type=F32)
+            if c:
+                part = part + total[cols, :]
+            if c < cells - 1:
+                total[cols, :] = part
+            else:
+                product = part * weights[cols, :].astype(F32)
+                late[0, :, cols] = row_dot(ones[:, : 3 * wide], product, True)
+                low = part.astype(BF)
+                for s in range(0, CHUNK, 32):
+                    row = m * CHUNK + s
+                    n = row // 160
+                    query_part[n // 4, (n // 2) % 2, n % 2, row % 160 : row % 160 + 32, :] = low[s : s + 32, :]
+        if c == cells - 1:
+            go("q0", 0)
+            go("q1", 0)
+            line = lax.broadcasted_iota(jnp.int32, late.shape[1:], 0)
+            late[0] = jnp.where(line == 0, late[0], row_dot(column_sum[...], weights[...], False))
+            vector_go("late", 0)
+        run((c, 5))
+        lines = []
+        for r in (3, 1, 2, 0):
+            part = lax.dot_general(
+                moved[r * rows : (r + 1) * rows, :], weights[...], NT, preferred_element_type=F32
+            )
+            if r == 0:
+                keep_back[c] = part
+                continue
+            spot = {1: slice(0, 256), 2: slice(512, 768), 3: slice(256, 512)}[r]
+            first[c % 2, spot] = part.astype(BF)
+            if r != 2:
+                n = 3 * c + (1 if r == 3 else 0)
+                copy = remote(
+                    first.at[c % 2, spot], (got_far if r == 3 else got_near).at[c],
+                    back_send.at[n], back_recv.at[n], near["c"],
+                )
+                lines.insert(0, copy)
+                sent.append(copy)
+        near_copies[c] = lines
+        run((c, 6))
+    back_sum(cells - 1, 0)
+    vector_end("late", 0)
+    end("q0", 0)
+    end("q1", 0)
+    vector_end("late", 1)
+    end("q1", 1)
+    end("q0", 1)
+    vector_end("late", 2)
+    back_end(cells - 1, 0)
+    vector_end("late", 3)
+    end("q0", 2)
+    end("q1", 2)
+    vector_end("late", 4)
+    values = query_part[mine["h"], mine["z"], mine["x"]]
+    for j in range(4):
+        query_last[j] = values[j * 40 : (j + 1) * 40]
+    last_query = []
+    for r in range(1, 4):
+        sem = next(sems)
+        copy = remote(
+            query_last.at[chrom_near(r)], query_got.at[r], sum_send.at[sem], sum_recv.at[sem], by_part[r]
+        )
+        last_query.append(copy)
+        sent.append(copy)
+    query_got[0] = query_last[place]
+    n = cells
+    for name, out in (("uz", up_z_out), ("uy", up_y_out), ("o", out_out)):
+        _, last, got, _ = lasts[name]
+        items[name][6]["last"].wait_recv()
+        ends.append(load(last.at[core], out.at[0], end_sem.at[n]))
+        ends.append(load(got, out.at[1], end_sem.at[n + 1]))
+        n += 2
+    ends.append(load(down_last, down_out, end_sem.at[n]))
+    ends.append(load(early.at[5], early_out, end_sem.at[n + 2]))
+    ends.append(load(late.at[5], late_out, end_sem.at[n + 3]))
+    for copy in last_query:
+        copy.wait_recv()
+    ends.append(load(query_got, query_out, end_sem.at[n + 1]))
+    for copy in ends:
+        copy.wait()
+    for copy in sent:
+        copy.wait_send()
+
+
+def attend_sum(
+    lens, grads, kept, firsts, weight, up_z, up_y, out_part, down_ab, down_c, early, tokens, through, gain, block
+):
+    cells, rows, wide = grads[0].shape
+    width = firsts[0].shape[1]
+    heads = wide // HEAD_DIM
+    seq = 4 * rows
+    anywhere = pl.BlockSpec(memory_space=pl.ANY)
+    dma = pltpu.SemaphoreType.DMA
+    vmem = lambda *shape: pltpu.VMEM(shape, BF)
+    qa, qb = [hi - lo for lo, hi, _ in QUERY_ITEMS]
+    return pl.pallas_call(
+        functools.partial(attend_sum_kernel, block, heads),
+        in_specs=[smem()] + [anywhere] * (5 + 12 + 9) + [pl.BlockSpec(memory_space=pltpu.VMEM)],
+        out_specs=[anywhere] * 8,
+        out_shape=[
+            jax.ShapeDtypeStruct((cells, rows, width), F32),
+            jax.ShapeDtypeStruct((4, 40, 3 * wide), BF),
+            jax.ShapeDtypeStruct((2, 3, 40, TILE), BF),
+            jax.ShapeDtypeStruct((2, 2, 40, TILE), BF),
+            jax.ShapeDtypeStruct((2, 1, 40, width // 2), BF),
+            jax.ShapeDtypeStruct((160, width), BF),
+            jax.ShapeDtypeStruct((8, width), F32),
+            jax.ShapeDtypeStruct((8, width), F32),
+        ],
+        scratch_shapes=[
+            vmem(cells, 4, rows, wide),
+            vmem(2, FILLED, 3 * wide),
+            vmem(2, seq, width),
+            vmem(width, 3 * wide),
+            vmem(FILLED, 3 * wide),
+            vmem(seq, 3 * wide),
+            pltpu.VMEM((width, 3 * wide), F32),
+            vmem(2, 2, 2, 160, 3 * wide),
+            vmem(*up_z.shape), vmem(*up_y.shape), vmem(*out_part.shape), vmem(*down_ab.shape), vmem(*down_c.shape),
+            vmem(2, 160, width), vmem(*down_ab.shape[1:]), vmem(*down_c.shape[1:]),
+            pltpu.VMEM((cells, rows, width), F32),
+            vmem(cells, rows, width), vmem(cells, rows, width), vmem(cells, rows, width),
+            vmem(2, 2, 160, qa), vmem(2, 160, qa), vmem(160, qa),
+            vmem(2, 2, 160, qb), vmem(2, 160, qb), vmem(160, qb),
+            vmem(4, 40, 3 * wide), vmem(4, 40, 3 * wide),
+            vmem(3, 2, 2, 80, TILE), vmem(3, 2, 80, TILE), vmem(3, 80, TILE),
+            vmem(2, 3, 40, TILE), vmem(3, 40, TILE),
+            vmem(2, 2, 2, 80, TILE), vmem(2, 2, 80, TILE), vmem(2, 80, TILE),
+            vmem(2, 2, 40, TILE), vmem(2, 40, TILE),
+            vmem(2, 2, 2, 2, 80, width // 2), vmem(2, 2, 2, 80, width // 2), vmem(2, 2, 80, width // 2),
+            vmem(2, 80, width // 2), vmem(80, width // 2),
+            vmem(2, 1, 40, width // 2), vmem(1, 40, width // 2),
+            vmem(2, 160, width), vmem(160, width),
+            pltpu.VMEM((6, 8, width), F32), pltpu.VMEM((5, 8, width), F32),
+            pltpu.VMEM((6, 8, width), F32), pltpu.VMEM((5, 8, width), F32),
+            pltpu.VMEM((8, 3 * wide), F32), vmem(rows, width),
+            dma((13,)), dma((12,)), dma((9,)), dma((9,)), dma((9,)), dma((9,)), dma((36,)), dma((36,)),
+            dma((16,)), dma((2 * cells,)),
+        ],
+        compiler_params=pltpu.CompilerParams(
+            vmem_limit_bytes=VMEM_TOP, collective_id=1, has_side_effects=True
+        ),
+        cost_estimate=cost(8e10, 6e7),
+        name="attend_sum",
+    )(
+        lens, *grads, kept, *firsts, weight, up_z, up_y, out_part, down_ab, down_c, early, tokens, through, gain
+    )
 
 
 def swap(x, axis, mask):
@@ -859,6 +1370,8 @@
         over = swap(mine, "chrom", 2)
         first_all.append([mine, swap(mine, "chrom", 1), over, swap(over, "chrom", 1)])
     for c in range(cells_here):
+        if c:
+            first_all[c], mixed_near[-1] = lax.optimization_barrier((first_all[c], mixed_near[-1]))
         mixed, qkv_c = attend(first_all[c], lens[c], qkv_weight, block)
         kept.append(qkv_c)
         mixed_near.append(
@@ -876,21 +1389,16 @@
     ).reshape(rows, width)
     down_low = result_back.astype(BF)
     low_bits = [("cells", b) for b in range(cell_bits - 1)]
-    if lax.axis_size("cells") == 8 and parts == 4:
-        second_back, result_part, down_grad, up_grad, up_rest = feed_forward_sum(
+    fused = lax.axis_size("cells") == 8 and parts == 4
+    if fused:
+        second_back, result_part, down_ab, down_c, up_z, up_y = feed_forward_sum(
             second_low, down_low, up_weight, down_weight
         )
-        result = middle + result_part
-        down_out = place_rows(down_grad)
-        up_rest = halve(halve(up_rest, 2, "cells", 0).astype(BF), 2, "chrom", 1).astype(BF)
-        up_grad = jnp.concatenate([up_grad, up_rest], axis=0)
-        up_grad = up_grad.transpose(1, 2, 0, 3).reshape(2, 80, -1)
-        up_out = place_columns(halve(up_grad, 0, "cells", 2))
     else:
         second_back, result_part, down_out, up_out = feed_forward_plain(
             second_low, down_low, up_weight, down_weight
         )
-        result = middle + result_part
+    result = middle + result_part
     result_cells = result.reshape(cells_here, seq_here, width)
     layer_out = result_cells.astype(BF)
 
@@ -903,65 +1411,106 @@
     )
     middle_back = result_back + middle_ln
     attend_low = middle_back.astype(BF)
-    mixed_back = back_through(attend_low, output_near).astype(BF)
     output_grad = contract(mixed_flat, attend_low).reshape(parts, wide, width)
     output_grad = jnp.concatenate(
         [lax.dynamic_index_in_dim(output_grad, place ^ j, 0, keepdims=False) for j in range(parts)],
         axis=0,
     )
-    half_width = width // 2
-    output_half = lax.dynamic_slice_in_dim(output_grad, core * half_width, half_width, 1) + swap(
-        lax.dynamic_slice_in_dim(output_grad, (1 - core) * half_width, half_width, 1).astype(BF),
-        "chrom",
-        1,
-    ).astype(F32)
-    output_out = scatter_columns_split(
-        output_half.astype(BF), low_bits + [("cells", cell_bits - 1), ("chrom", 1)]
-    )
-    early = sum_all(jnp.stack([cls_total, cls_square, second_gain_grad, second_shift_grad]))
-
-    mixed_back = mixed_back.reshape(cells_here, seq_here, width)
-    heads_back = []
-    for c in range(cells_here):
-        pieces = [mixed_back[c, :, r * wide : (r + 1) * wide] for r in range(parts)]
-        heads_back.append(
-            [pieces[0]] + [swap(pieces[r], "chrom", r) for r in range(1, parts)]
+    early = jnp.stack([cls_total, cls_square, second_gain_grad, second_shift_grad])
+
+    if fused:
+        grads_near = [
+            back_through(attend_low, output_near[r * wide : (r + 1) * wide])
+            .astype(BF)
+            .reshape(cells_here, seq_here, wide)
+            for r in range(parts)
+        ]
+        output_part = output_grad.astype(BF).reshape(2, 2, 2, 2, 80, 2, width // 2)
+        tokens_grad, qkv_got, up_z, up_y, out_two, down_grad, early, late = attend_sum(
+            lens,
+            grads_near,
+            jnp.stack(kept),
+            [piece for line in first_all for piece in line],
+            qkv_weight,
+            up_z,
+            up_y,
+            output_part.transpose(5, 0, 1, 2, 3, 4, 6),
+            down_ab,
+            down_c,
+            jnp.concatenate([early, jnp.zeros_like(early)], axis=0),
+            tokens,
+            attend_low.reshape(cells_here, seq_here, width),
+            first_gain[None, :],
+            block,
         )
-    qkv_grad = None
-    first_back = []
-    for c in range(cells_here):
-        qkv_back = attend_back(heads_back[c], lens[c], kept[c], block)
-        pieces = [back_through(g, qkv_weight) for g in qkv_back]
-        sent = swap(jnp.stack([pieces[1].astype(BF), pieces[3].astype(BF)]), "chrom", 1).astype(F32)
-        over = swap((pieces[2] + sent[1]).astype(BF), "chrom", 2)
-        first_back.append(pieces[0] + sent[0] + over.astype(F32))
-        part = contract(
-            jnp.concatenate(first_all[c], axis=0), jnp.concatenate(qkv_back, axis=0)
+        late = jnp.stack([(late[0] - first_shift * late[1]) / first_gain, late[1]])
+        down_out = down_grad.astype(F32)
+
+        def both_cores(two):
+            two = two.transpose(0, 2, 1, 3).reshape(2, two.shape[2], -1)
+            swapped = jnp.where(core == 0, two, two[::-1])
+            return jnp.concatenate([swapped[0], swapped[1]], axis=1).astype(F32)
+
+        up_two = jnp.stack([up_z[:, 0], up_z[:, 1], up_y[:, 0], up_z[:, 2], up_y[:, 1]], axis=1)
+        up_out = both_cores(up_two)
+        output_out = both_cores(out_two)
+        pieces = [
+            lax.dynamic_index_in_dim(qkv_got, place ^ j, 0, keepdims=False).astype(F32)
+            for j in range(parts)
+        ]
+    else:
+        half_width = width // 2
+        output_half = lax.dynamic_slice_in_dim(output_grad, core * half_width, half_width, 1) + swap(
+            lax.dynamic_slice_in_dim(output_grad, (1 - core) * half_width, half_width, 1).astype(BF),
+            "chrom",
+            1,
+        ).astype(F32)
+        output_out = scatter_columns_split(
+            output_half.astype(BF), low_bits + [("cells", cell_bits - 1), ("chrom", 1)]
         )
-        qkv_grad = part if qkv_grad is None else qkv_grad + part
-    first_back = jnp.concatenate(first_back, axis=0)
-
-    names = [("cells", b) for b in reversed(range(cell_bits))]
-    qkv_sum = scatter_rows(
-        qkv_grad.reshape((2,) * cell_bits + (-1, 3 * wide)),
-        [("cells", b) for b in range(cell_bits)],
-        names,
-    ).reshape(parts, -1, 3 * wide)
-    pieces = [lax.dynamic_index_in_dim(qkv_sum, near[0], 0, keepdims=False)]
-    for r in range(1, parts):
-        piece = lax.dynamic_index_in_dim(qkv_sum, near[r], 0, keepdims=False).astype(BF)
-        pieces.append(swap(piece, "chrom", r).astype(F32))
-    pieces = jnp.stack(pieces)
-    pieces = [lax.dynamic_index_in_dim(pieces, place ^ j, 0, keepdims=False) for j in range(parts)]
+        mixed_back = back_through(attend_low, output_near).astype(BF)
+        mixed_back = mixed_back.reshape(cells_here, seq_here, width)
+        heads_back = []
+        for c in range(cells_here):
+            pieces = [mixed_back[c, :, r * wide : (r + 1) * wide] for r in range(parts)]
+            heads_back.append(
+                [pieces[0]] + [swap(pieces[r], "chrom", r) for r in range(1, parts)]
+            )
+        qkv_grad = None
+        first_back = []
+        for c in range(cells_here):
+            qkv_back = attend_back(heads_back[c], lens[c], kept[c], block)
+            pieces = [back_through(g, qkv_weight) for g in qkv_back]
+            sent = swap(jnp.stack([pieces[1].astype(BF), pieces[3].astype(BF)]), "chrom", 1).astype(F32)
+            over = swap((pieces[2] + sent[1]).astype(BF), "chrom", 2)
+            first_back.append(pieces[0] + sent[0] + over.astype(F32))
+            part = contract(
+                jnp.concatenate(first_all[c], axis=0), jnp.concatenate(qkv_back, axis=0)
+            )
+            qkv_grad = part if qkv_grad is None else qkv_grad + part
+        first_back = jnp.concatenate(first_back, axis=0)
+
+        names = [("cells", b) for b in reversed(range(cell_bits))]
+        qkv_sum = scatter_rows(
+            qkv_grad.reshape((2,) * cell_bits + (-1, 3 * wide)),
+            [("cells", b) for b in range(cell_bits)],
+            names,
+        ).reshape(parts, -1, 3 * wide)
+        pieces = [lax.dynamic_index_in_dim(qkv_sum, near[0], 0, keepdims=False)]
+        for r in range(1, parts):
+            piece = lax.dynamic_index_in_dim(qkv_sum, near[r], 0, keepdims=False).astype(BF)
+            pieces.append(swap(piece, "chrom", r).astype(F32))
+        pieces = jnp.stack(pieces)
+        pieces = [lax.dynamic_index_in_dim(pieces, place ^ j, 0, keepdims=False) for j in range(parts)]
+        first_ln, first_gain_grad, first_shift_grad = norm_back(
+            first_back, first_norm, first_inv, first_gain
+        )
+        tokens_grad = (middle_back + first_ln).reshape(cells_here, seq_here, width)
+        early = sum_all(early)
+        late = sum_all(jnp.stack([first_gain_grad, first_shift_grad]))
     query_out, key_out, value_out = [
         jnp.concatenate([p[:, i * wide : (i + 1) * wide] for p in pieces], axis=1) for i in range(3)
     ]
-
-    first_ln, first_gain_grad, first_shift_grad = norm_back(
-        first_back, first_norm, first_inv, first_gain
-    )
-    tokens_grad = (middle_back + first_ln).reshape(cells_here, seq_here, width)
-    late = sum_all(jnp.stack([first_gain_grad, first_shift_grad]))
 
     count_cells = cells_here * lax.axis_size("cells")
     cls_mean = early[0] / count_cells

time: 575 us -> 492 us (0.86)
  waiting for transfers between devices: 128 us -> 29.2 us
  Pallas kernels: 234 us -> 332 us
  starting transfers between devices: 67.7 us -> 17.3 us
  matrix products: 45.9 us -> 14.7 us
  local copies, waits for them, and re-layouts: 43.2 us -> 52.2 us
  other arithmetic: 44.1 us -> 35.6 us
    pallas_call x3 -> x1, Pallas kernels: 61.5 us -> 181 us  [attend_sum(): pl.pallas_call(functools.partial(attend_sum_kernel, block, heads), in_spe...]
    ppermute x59 -> x18, waiting for transfers between devices: 126 us -> 29.2 us  [swap(): return lax.ppermute(x, axis, [(i, i ^ mask) for i in range(size)])]
    ppermute x59 -> x18, starting transfers between devices: 60.9 us -> 17.3 us  [swap(): return lax.ppermute(x, axis, [(i, i ^ mask) for i in range(size)])]
    pallas_call x1, Pallas kernels: 121 us -> 99.6 us  [feed_forward_sum(): pl.pallas_call(feed_sum_kernel, in_specs=[anywhere] * 4, out_specs=[anywh...]
    dot_general x13 -> x4, matrix products: 22.6 us -> 6.58 us  [back_through(): return lax.dot_general(grad, weight, NT, preferred_element_type=F32)]
    dot_general x4 -> x1, matrix products: 18.3 us -> 3.05 us  [contract(): return lax.dot_general(left, right, TN, preferred_element_type=F32)]
    add x16 -> x0, other arithmetic: 12 us -> none  [the longest x1 5.05 us: per_device(): tokens_grad = (middle_back + first_ln).reshape(cells_here, seq_here, width)]
    concatenate x3, local copies, waits for them, and re-layouts: 6.29 us -> 13.8 us  [per_device(): jnp.concatenate([mixed[0]] + [swap(mixed[r], 'chrom', r) for r in range(1...]
  transfers between devices with their start and end apart: 61 -> 18, of which waited for: 23 -> 8; matrix products, arithmetic and copies ran while one was open for 16% -> 7% of each run, Pallas kernels for 20% -> 7%
where the time goes in v3:
time: 492 us; the launch traced here: 483 us
  Pallas kernels  332 us (67%)
  local copies, waits for them, and re-layouts  52.2 us (11%)
  other arithmetic  35.6 us (7%)
  waiting for transfers between devices  29.2 us (6%)
  starting transfers between devices  17.3 us (4%)
  matrix products  14.7 us (3%)
    pallas_call x1, Pallas kernels, attend_sum(): pl.pallas_call(functools.partial(attend_sum_kernel, block, heads), in_spe...  181 us
    pallas_call x1, Pallas kernels, feed_forward_sum(): pl.pallas_call(feed_sum_kernel, in_specs=[anywhere] * 4, out_specs=[anywh...  99.6 us
    pallas_call x3, Pallas kernels, attend(): pl.pallas_call(functools.partial(attend_kernel, block, heads), in_specs=[...  51.4 us
    ppermute x18, waiting for transfers between devices, swap(): return lax.ppermute(x, axis, [(i, i ^ mask) for i in range(size)])  29.2 us
    ppermute x18, starting transfers between devices, swap(): return lax.ppermute(x, axis, [(i, i ^ mask) for i in range(size)])  17.3 us
    concatenate x3, local copies, waits for them, and re-layouts, per_device(): jnp.concatenate([mixed[0]] + [swap(mixed[r], 'chrom', r) for r in range(1...  13.8 us
  transfers between devices with their start and end apart: 18, of which 8 were waited for; matrix products, arithmetic and copies ran while one was open for 7% of the time, Pallas kernels for 7%

profile of v3, /device:TPU:1, one launch (start us, length us, event | category | flops | bytes accessed | tf_op | source)
XLA Modules:
  0.0 483.0 jit_solution(1579619414220036304)
XLA Ops:
  0.7 2.0 convert_reduce_fusion
  2.7 2.2 fusion.2
  5.8 1.3 fusion.27
  7.1 2.1 collective-permute-start.4
  10.3 1.6 collective-permute-start.10
  12.0 2.7 constant_dynamic-slice_fusion.10
  14.6 4.0 constant_dynamic-slice_fusion.8
  19.0 2.2 multiply_multiply_fusion
  21.2 2.7 collective-permute-done.4.refs_2_
  24.0 2.1 collective-permute-start.5
  26.1 2.5 pad_maximum_fusion.2.refs_4_.refs_12_
  29.1 8.9 %collective-permute-done.1.refs_2_.refs_6_ = bf16[256,1280]{1,0:T(8,128)(2,1)} collective-permute-done((bf16[256,1280]{1,0:T(8,128)(2,1)}, bf16[256,1280]{1,0:T(8,128)(2,1)}, u32[]{:S(2)}, u32[]{:S(2)}) %collective-permute-start.1) | collective-permute-done | bytes 655392 | tf_op jit(solution)/shard_map/ppermute | solution.py:1182
  38.0 2.1 collective-permute-start.2
  40.1 17.2 %attend.3 = (bf16[256,320]{1,0:T(8,128)(2,1)}, bf16[256,320]{1,0:T(8,128)(2,1)}, bf16[256,320]{1,0:T(8,128)(2,1)}, bf16[256,320]{1,0:T(8,128)(2,1)}, bf16[768,960]{1,0:T(8,128)(2,1)}) custom-call(s32[8]{0:T(128)} %get-tuple-element.140.lens, bf16[256,1280]{1,0:T(8,128)(2,1)} %get-tuple-element.112.refs_0_, bf16[256,1280]{1,0:T(8,128)(2,1)} %collective-permute-done.3.refs_1_, ...), custom_call_target="tpu_custom_call" | custom-call | flops 6543114240 | bytes 8000000 | tf_op jit(solution)/shard_map/attend/pallas_call | solution.py:112
  57.3 1.8 collective-permute-start.7
  59.5 1.5 bitcast_convert_fusion.low_in
  61.4 2.9 collective-permute-done.7
  64.4 1.5 collective-permute-start.11
  65.9 3.0 collective-permute-done.8
  68.8 2.1 concatenate.45
  70.9 17.1 %attend.4 = (bf16[256,320]{1,0:T(8,128)(2,1)}, bf16[256,320]{1,0:T(8,128)(2,1)}, bf16[256,320]{1,0:T(8,128)(2,1)}, bf16[256,320]{1,0:T(8,128)(2,1)}, bf16[768,960]{1,0:T(8,128)(2,1)}) custom-call(s32[8]{0:T(128)} %get-tuple-element.142.lens, bf16[256,1280]{1,0:T(8,128)(2,1)} %get-tuple-element.58.refs_0_.refs_4_, ...), custom_call_target="tpu_custom_call" | custom-call | flops 6543114240 | bytes 8000000 | tf_op jit(solution)/shard_map/attend/pallas_call | solution.py:112
  88.2 1.4 collective-permute-start.13
  90.2 1.8 constant_dynamic-slice_fusion.7
  92.6 1.9 collective-permute-done.13
  94.5 4.8 collective-permute-done.14
  99.2 9.9 %concatenate.46 = bf16[256,1280]{1,0:T(8,128)(2,1)} concatenate(bf16[256,320]{1,0:T(8,128)(2,1)S(1)} %copy-done.25, bf16[256,320]{1,0:T(8,128)(2,1)S(1)} %collective-permute-done.12, bf16[256,320]{1,0:T(8,128)(2,1)S(1)} %collective-permute-done.13, bf16[256,320]{1,0:T(8,128)(2,1)S(1)} %collective-permute-done.14), dimensions={1} | concatenate | bytes 1310720 | tf_op jit(solution)/shard_map/concatenate | solution.py:1378
  109.1 17.0 %attend.5 = (bf16[256,320]{1,0:T(8,128)(2,1)}, bf16[256,320]{1,0:T(8,128)(2,1)}, bf16[256,320]{1,0:T(8,128)(2,1)}, bf16[256,320]{1,0:T(8,128)(2,1)}, bf16[768,960]{1,0:T(8,128)(2,1)}) custom-call(s32[8]{0:T(128)} %get-tuple-element.141.lens, bf16[256,1280]{1,0:T(8,128)(2,1)} %get-tuple-element.67.refs_0_.refs_8_, ...), custom_call_target="tpu_custom_call" | custom-call | flops 6543114240 | bytes 8000000 | tf_op jit(solution)/shard_map/attend/pallas_call | solution.py:112
  126.2 1.4 collective-permute-start.16
  128.3 3.9 pad_maximum_fusion.kept
  132.4 4.9 %collective-permute-done.17 = bf16[256,320]{1,0:T(8,128)(2,1)S(1)} collective-permute-done((bf16[256,320]{1,0:T(8,128)(2,1)}, bf16[256,320]{1,0:T(8,128)(2,1)S(1)}, u32[]{:S(2)}, u32[]{:S(2)}) %collective-permute-start.17) | collective-permute-done | bytes 163872 | tf_op jit(solution)/shard_map/ppermute | solution.py:1182
  137.9 1.8 concatenate.47
  139.8 5.1 %fusion.33 = (f32[768]{0:T(1024)S(1)}, f32[768,1280]{1,0:T(8,128)S(1)}) fusion(bf16[320,1280]{1,0:T(8,128)(2,1)} %get-tuple-element.110, bf16[320,1280]{1,0:T(8,128)(2,1)} %get-tuple-element.111, bf16[320,1280]{1,0:T(8,128)(2,1)} %get-tuple-element.109, bf16[320,1280]{1,0:T(8,128)(2,1)} %get-tuple-element.108, bf16[256,1280]{1,0:T(8,128)(2,1)S(1)} %concatenate.47, ...), kind=kOutput, calls=%fused_computation.112 | convolution fusion | flops 2538536192 | bytes 11144192 | tf_op jit(solution)/shard_map/dot_general | solution.py:1382
  145.5 1.3 copy-done
  146.7 2.0 add_convert_fusion.second_in
  148.7 99.6 %feed_sum.1 = (f32[768,1280]{1,0:T(8,128)}, f32[768,1280]{1,0:T(8,128)}, bf16[2,320,1024]{2,1,0:T(8,128)(2,1)}, bf16[2,320,256]{2,1,0:T(8,128)(2,1)}, bf16[3,2,2...) custom-call(bf16[768,1280]{1,0:T(8,128)(2,1)} %add_convert_fusion.second_in, ...), custom_call_target="tpu_custom_call" | custom-call | flops 60397977600 | bytes 60000000 | tf_op jit(solution)/shard_map/feed_sum/pallas_call | solution.py:618
  248.3 4.7 multiply_reduce_fusion
  253.9 4.3 fusion
  258.3 3.0 fusion.18
  261.4 1.7 convolution_convert_fusion
  263.0 1.7 convolution_convert_fusion.1
  264.7 1.6 convolution_convert_fusion.2
  266.3 1.6 convolution_convert_fusion.3
  268.6 3.3 convert_element_type.95
  272.0 4.2 copy.49
  281.1 181.4 %attend_sum.1 = (f32[3,256,1280]{2,1,0:T(8,128)}, bf16[4,40,960]{2,1,0:T(8,128)(2,1)}, bf16[2,3,40,512]{3,2,1,0:T(8,128)(2,1)}, bf16[2,2,40,512]{3,2,1,0:T(8,128...) custom-call(s32[3,8]{1,0:T(4,128)} %copy-done.40, ...), custom_call_target="tpu_custom_call" | custom-call | flops 80000000000 | bytes 60000000 | tf_op jit(solution)/shard_map/attend_sum/pallas_call | solution.py:1126
  464.5 3.6 convert_element_type.89
  474.7 1.3 dynamic-slice_divide_fusion
  478.4 4.3 copy.52
  (165 shorter events, 24.4 us)
Async XLA Ops:
  0.6 4.3 copy-start.4
  0.7 4.3 copy-start.34
  0.7 4.3 copy-start.38
  5.0 6.9 %copy-start.33 = (s32[3,8]{1,0:T(4,128)S(1)}, s32[3,8]{1,0:T(4,128)}, u32[]{:S(2)}) copy-start(s32[3,8]{1,0:T(4,128)} %param.17) | copy-start | bytes 292
  7.1 11.7 %copy-start.41 = (f32[4]{0:T(128)S(1)}, f32[4]{0:T(128)}, u32[]{:S(2)}) copy-start(f32[4]{0:T(128)} %param.19) | copy-start | bytes 52
  7.1 11.7 %copy-start.42 = (s32[3]{0:T(128)S(1)}, s32[3]{0:T(128)}, u32[]{:S(2)}) copy-start(s32[3]{0:T(128)} %param.18) | copy-start | bytes 40
  7.1 16.8 %collective-permute-start.4 = (bf16[256,1280]{1,0:T(8,128)(2,1)}, bf16[256,1280]{1,0:T(8,128)(2,1)}, u32[]{:S(2)}, u32[]{:S(2)}) collective-permute-start(bf16[256,1280]{1,0:T(8,128)(2,1)} %get-tuple-element.112.refs_0_), channel_id=1, source_target_pairs={{0,2},{1,3},{2,0},{3,1},{4,6},{5,7},{6,4},{7,5},{8,10},{9,11},{10,... | collective-permute-start | bytes 1966088 | tf_op jit(solution)/shard_map/ppermute | solution.py:1182
  9.2 30.9 %collective-permute-start.3 = (bf16[256,1280]{1,0:T(8,128)(2,1)}, bf16[256,1280]{1,0:T(8,128)(2,1)}, u32[]{:S(2)}, u32[]{:S(2)}) collective-permute-start(bf16[256,1280]{1,0:T(8,128)(2,1)} %get-tuple-element.112.refs_0_), channel_id=1, source_target_pairs={{0,1},{1,0},{2,3},{3,2},{4,5},{5,4},{6,7},{7,6},{8,9},{9,8},{10,11... | collective-permute-start | bytes 1966088 | tf_op jit(solution)/shard_map/ppermute | solution.py:1182
  10.1 27.9 %collective-permute-start.1 = (bf16[256,1280]{1,0:T(8,128)(2,1)}, bf16[256,1280]{1,0:T(8,128)(2,1)}, u32[]{:S(2)}, u32[]{:S(2)}) collective-permute-start(bf16[256,1280]{1,0:T(8,128)(2,1)} %get-tuple-element.58.refs_0_.refs_4_), channel_id=1, source_target_pairs={{0,2},{1,3},{2,0},{3,1},{4,6},{5,7},{6,4},{7,5},{8,10},{9,11},{10,... | collective-permute-start | bytes 1966088 | tf_op jit(solution)/shard_map/ppermute | solution.py:1182
  10.2 60.8 %collective-permute-start = (bf16[256,1280]{1,0:T(8,128)(2,1)}, bf16[256,1280]{1,0:T(8,128)(2,1)}, u32[]{:S(2)}, u32[]{:S(2)}) collective-permute-start(bf16[256,1280]{1,0:T(8,128)(2,1)} %get-tuple-element.58.refs_0_.refs_4_), channel_id=1, source_target_pairs={{0,1},{1,0},{2,3},{3,2},{4,5},{5,4},{6,7},{7,6},{8,9},{9,8},{10,11... | collective-permute-start | bytes 1966088 | tf_op jit(solution)/shard_map/ppermute | solution.py:1182
  10.3 48.8 %collective-permute-start.10 = (bf16[256,1280]{1,0:T(8,128)(2,1)}, bf16[256,1280]{1,0:T(8,128)(2,1)}, u32[]{:S(2)}, u32[]{:S(2)}) collective-permute-start(bf16[256,1280]{1,0:T(8,128)(2,1)} %get-tuple-element.67.refs_0_.refs_8_), channel_id=1, source_target_pairs={{0,2},{1,3},{2,0},{3,1},{4,6},{5,7},{6,4},{7,5},{8,10},{9,11},{10,... | collective-permute-start | bytes 1966088 | tf_op jit(solution)/shard_map/ppermute | solution.py:1182
  18.7 7.4 %copy-start.7 = (bf16[1280,320]{1,0:T(8,128)(2,1)S(1)}, bf16[1280,320]{1,0:T(8,128)(2,1)}, u32[]{:S(2)}) copy-start(bf16[1280,320]{1,0:T(8,128)(2,1)} %constant_dynamic-slice_fusion.10) | copy-start | bytes 2457604
  18.7 7.4 %copy-start.8 = (bf16[1280,320]{1,0:T(8,128)(2,1)S(1)}, bf16[1280,320]{1,0:T(8,128)(2,1)}, u32[]{:S(2)}) copy-start(bf16[1280,320]{1,0:T(8,128)(2,1)} %get-tuple-element.149) | copy-start | bytes 2457604
  18.7 7.4 %copy-start.9 = (bf16[1280,320]{1,0:T(8,128)(2,1)S(1)}, bf16[1280,320]{1,0:T(8,128)(2,1)}, u32[]{:S(2)}) copy-start(bf16[1280,320]{1,0:T(8,128)(2,1)} %get-tuple-element.150) | copy-start | bytes 2457604
  21.2 38.3 %copy-start.2 = (f32[3,256,1280]{2,1,0:T(8,128)}, f32[3,256,1280]{2,1,0:T(8,128)S(1)}, u32[]{:S(2)}) copy-start(f32[3,256,1280]{2,1,0:T(8,128)S(1)} %multiply_multiply_fusion) | copy-start | bytes 11796484
  24.0 16.1 %collective-permute-start.5 = (bf16[256,1280]{1,0:T(8,128)(2,1)}, bf16[256,1280]{1,0:T(8,128)(2,1)}, u32[]{:S(2)}, u32[]{:S(2)}) collective-permute-start(bf16[256,1280]{1,0:T(8,128)(2,1)} %collective-permute-done.4.refs_2_), channel_id=1, source_target_pairs={{0,1},{1,0},{2,3},{3,2},{4,5},{5,4},{6,7},{7,6},{8,9},{9,8},{10,11... | collective-permute-start | bytes 1966088 | tf_op jit(solution)/shard_map/ppermute | solution.py:1182
  38.0 32.9 %collective-permute-start.2 = (bf16[256,1280]{1,0:T(8,128)(2,1)}, bf16[256,1280]{1,0:T(8,128)(2,1)}, u32[]{:S(2)}, u32[]{:S(2)}) collective-permute-start(bf16[256,1280]{1,0:T(8,128)(2,1)} %collective-permute-done.1.refs_2_.refs_6_), channel_id=1, source_target_pairs={{0,1},{1,0},{2,3},{3,2},{4,5},{5,4},{6,7},{7,6},{8,9},{9,8},{10,11... | collective-permute-start | bytes 1966088 | tf_op jit(solution)/shard_map/ppermute | solution.py:1182
  57.3 11.6 %copy-start.26 = (bf16[256,320]{1,0:T(8,128)(2,1)S(1)}, bf16[256,320]{1,0:T(8,128)(2,1)}, u32[]{:S(2)}) copy-start(bf16[256,320]{1,0:T(8,128)(2,1)} %get-tuple-element.53) | copy-start | bytes 491524
  57.3 3.7 collective-permute-start.6
  57.3 7.1 %collective-permute-start.7 = (bf16[256,320]{1,0:T(8,128)(2,1)}, bf16[256,320]{1,0:T(8,128)(2,1)}, u32[]{:S(2)}, u32[]{:S(2)}) collective-permute-start(bf16[256,320]{1,0:T(8,128)(2,1)} %get-tuple-element.55), channel_id=1, source_target_pairs={{0,2},{1,3},{2,0},{3,1},{4,6},{5,7},{6,4},{7,5},{8,10},{9,11},{10,... | collective-permute-start | bytes 491528 | tf_op jit(solution)/shard_map/ppermute | solution.py:1182
  59.1 9.7 %collective-permute-start.8 = (bf16[256,320]{1,0:T(8,128)(2,1)}, bf16[256,320]{1,0:T(8,128)(2,1)}, u32[]{:S(2)}, u32[]{:S(2)}) collective-permute-start(bf16[256,320]{1,0:T(8,128)(2,1)} %get-tuple-element.56), channel_id=1, source_target_pairs={{0,3},{1,2},{2,1},{3,0},{4,7},{5,6},{6,5},{7,4},{8,11},{9,10},{10,... | collective-permute-start | bytes 491528 | tf_op jit(solution)/shard_map/ppermute | solution.py:1182
  61.0 48.1 %collective-permute-start.9 = (bf16[256,1280]{1,0:T(8,128)(2,1)}, bf16[256,1280]{1,0:T(8,128)(2,1)}, u32[]{:S(2)}, u32[]{:S(2)}) collective-permute-start(bf16[256,1280]{1,0:T(8,128)(2,1)} %get-tuple-element.67.refs_0_.refs_8_), channel_id=1, source_target_pairs={{0,1},{1,0},{2,3},{3,2},{4,5},{5,4},{6,7},{7,6},{8,9},{9,8},{10,11... | collective-permute-start | bytes 1966088 | tf_op jit(solution)/shard_map/ppermute | solution.py:1182
  64.4 44.8 %collective-permute-start.11 = (bf16[256,1280]{1,0:T(8,128)(2,1)}, bf16[256,1280]{1,0:T(8,128)(2,1)}, u32[]{:S(2)}, u32[]{:S(2)}) collective-permute-start(bf16[256,1280]{1,0:T(8,128)(2,1)} %collective-permute-done.10.refs_2_.refs_10_), channel_id=1, source_target_pairs={{0,1},{1,0},{2,3},{3,2},{4,5},{5,4},{6,7},{7,6},{8,9},{9,8},{10,11... | collective-permute-start | bytes 1966088 | tf_op jit(solution)/shard_map/ppermute | solution.py:1182
  70.9 19.3 %copy-start.10 = (bf16[1280,1280]{1,0:T(8,128)(2,1)S(1)}, bf16[1280,1280]{1,0:T(8,128)(2,1)}, u32[]{:S(2)}) copy-start(bf16[1280,1280]{1,0:T(8,128)(2,1)} %param.25) | copy-start | bytes 9830404
  88.1 11.2 %copy-start.25 = (bf16[256,320]{1,0:T(8,128)(2,1)S(1)}, bf16[256,320]{1,0:T(8,128)(2,1)}, u32[]{:S(2)}) copy-start(bf16[256,320]{1,0:T(8,128)(2,1)} %get-tuple-element.62) | copy-start | bytes 491524
  88.1 4.5 collective-permute-start.12
  88.2 6.3 %collective-permute-start.13 = (bf16[256,320]{1,0:T(8,128)(2,1)}, bf16[256,320]{1,0:T(8,128)(2,1)S(1)}, u32[]{:S(2)}, u32[]{:S(2)}) collective-permute-start(bf16[256,320]{1,0:T(8,128)(2,1)} %get-tuple-element.64), channel_id=1, source_target_pairs={{0,2},{1,3},{2,0},{3,1},{4,6},{5,7},{6,4},{7,5},{8,10},{9,11},{10,... | collective-permute-start | bytes 491528 | tf_op jit(solution)/shard_map/ppermute | solution.py:1182
  89.6 9.6 %collective-permute-start.14 = (bf16[256,320]{1,0:T(8,128)(2,1)}, bf16[256,320]{1,0:T(8,128)(2,1)S(1)}, u32[]{:S(2)}, u32[]{:S(2)}) collective-permute-start(bf16[256,320]{1,0:T(8,128)(2,1)} %get-tuple-element.65), channel_id=1, source_target_pairs={{0,3},{1,2},{2,1},{3,0},{4,7},{5,6},{6,5},{7,4},{8,11},{9,10},{10,... | collective-permute-start | bytes 491528 | tf_op jit(solution)/shard_map/ppermute | solution.py:1182
  109.1 19.2 %copy-start.12 = (bf16[768,960]{1,0:T(8,128)(2,1)S(1)}, bf16[768,960]{1,0:T(8,128)(2,1)}, u32[]{:S(2)}) copy-start(bf16[768,960]{1,0:T(8,128)(2,1)} %get-tuple-element.77) | copy-start | bytes 4423684
  126.2 6.1 %collective-permute-start.15 = (bf16[256,320]{1,0:T(8,128)(2,1)}, bf16[256,320]{1,0:T(8,128)(2,1)S(1)}, u32[]{:S(2)}, u32[]{:S(2)}) collective-permute-start(bf16[256,320]{1,0:T(8,128)(2,1)} %get-tuple-element.72), channel_id=1, source_target_pairs={{0,1},{1,0},{2,3},{3,2},{4,5},{5,4},{6,7},{7,6},{8,9},{9,8},{10,11... | collective-permute-start | bytes 491528 | tf_op jit(solution)/shard_map/ppermute | solution.py:1182
  126.2 6.2 %collective-permute-start.16 = (bf16[256,320]{1,0:T(8,128)(2,1)}, bf16[256,320]{1,0:T(8,128)(2,1)S(1)}, u32[]{:S(2)}, u32[]{:S(2)}) collective-permute-start(bf16[256,320]{1,0:T(8,128)(2,1)} %get-tuple-element.73), channel_id=1, source_target_pairs={{0,2},{1,3},{2,0},{3,1},{4,6},{5,7},{6,4},{7,5},{8,10},{9,11},{10,... | collective-permute-start | bytes 491528 | tf_op jit(solution)/shard_map/ppermute | solution.py:1182
  127.6 9.6 %collective-permute-start.17 = (bf16[256,320]{1,0:T(8,128)(2,1)}, bf16[256,320]{1,0:T(8,128)(2,1)S(1)}, u32[]{:S(2)}, u32[]{:S(2)}) collective-permute-start(bf16[256,320]{1,0:T(8,128)(2,1)} %get-tuple-element.74), channel_id=1, source_target_pairs={{0,3},{1,2},{2,1},{3,0},{4,7},{5,6},{6,5},{7,4},{8,11},{9,10},{10,... | collective-permute-start | bytes 491528 | tf_op jit(solution)/shard_map/ppermute | solution.py:1182
  128.3 11.4 %copy-start.5 = (bf16[3,256,1280]{2,1,0:T(8,128)(2,1)S(1)}, bf16[3,256,1280]{2,1,0:T(8,128)(2,1)}, u32[]{:S(2)}) copy-start(bf16[3,256,1280]{2,1,0:T(8,128)(2,1)} %refs_19_.1) | copy-start | bytes 5898244
  132.3 5.0 %copy-start.27 = (bf16[256,320]{1,0:T(8,128)(2,1)}, bf16[256,320]{1,0:T(8,128)(2,1)S(1)}, u32[]{:S(2)}) copy-start(bf16[256,320]{1,0:T(8,128)(2,1)S(1)} %collective-permute-done.15) | copy-start | bytes 491524
  132.4 4.9 %copy-start.28 = (bf16[256,320]{1,0:T(8,128)(2,1)}, bf16[256,320]{1,0:T(8,128)(2,1)S(1)}, u32[]{:S(2)}) copy-start(bf16[256,320]{1,0:T(8,128)(2,1)S(1)} %collective-permute-done.16) | copy-start | bytes 491524
  248.3 4.7 copy-start.1
  248.3 5.6 %copy-start.3 = (f32[3,256,1280]{2,1,0:T(8,128)S(1)}, f32[3,256,1280]{2,1,0:T(8,128)}, u32[]{:S(2)}) copy-start(f32[3,256,1280]{2,1,0:T(8,128)} %copy-done.2) | copy-start | bytes 11796484
  253.9 4.3 copy-start.17
  253.9 4.3 copy-start.18
  258.2 8.1 %copy-start.11 = (bf16[768,1280]{1,0:T(8,128)(2,1)}, bf16[768,1280]{1,0:T(8,128)(2,1)S(1)}, u32[]{:S(2)}) copy-start(bf16[768,1280]{1,0:T(8,128)(2,1)S(1)} %get-tuple-element.102) | copy-start | bytes 5898244
  258.2 9.7 %copy-start.6 = (f32[768,1280]{1,0:T(8,128)}, f32[768,1280]{1,0:T(8,128)S(1)}, u32[]{:S(2)}) copy-start(f32[768,1280]{1,0:T(8,128)S(1)} %get-tuple-element.103) | copy-start | bytes 11796484
  271.9 4.2 copy-start.19
  271.9 5.3 %copy-start.20 = (bf16[768,320]{0,1:T(8,128)(2,1)S(1)}, bf16[768,320]{0,1:T(8,128)(2,1)}, u32[]{:S(2)}) copy-start(bf16[768,320]{0,1:T(8,128)(2,1)} %convolution_convert_fusion.1) | copy-start | bytes 1474564
  272.0 6.4 %copy-start.21 = (bf16[768,320]{0,1:T(8,128)(2,1)S(1)}, bf16[768,320]{0,1:T(8,128)(2,1)}, u32[]{:S(2)}) copy-start(bf16[768,320]{0,1:T(8,128)(2,1)} %convolution_convert_fusion.2) | copy-start | bytes 1474564
  272.0 7.4 %copy-start.22 = (bf16[768,320]{0,1:T(8,128)(2,1)S(1)}, bf16[768,320]{0,1:T(8,128)(2,1)}, u32[]{:S(2)}) copy-start(bf16[768,320]{0,1:T(8,128)(2,1)} %convolution_convert_fusion.3) | copy-start | bytes 1474564
  462.6 5.5 %copy-start.37 = (f32[8,1280]{1,0:T(8,128)S(1)}, f32[8,1280]{1,0:T(8,128)}, u32[]{:S(2)}) copy-start(f32[8,1280]{1,0:T(8,128)} %get-tuple-element.88) | copy-start | bytes 122884
  462.6 5.6 %copy-start.30 = (bf16[2,2,40,512]{3,2,1,0:T(8,128)(2,1)S(1)}, bf16[2,2,40,512]{3,2,1,0:T(8,128)(2,1)}, u32[]{:S(2)}) copy-start(bf16[2,2,40,512]{3,2,1,0:T(8,128)(2,1)} %get-tuple-element.90) | copy-start | bytes 491524
  468.1 5.9 %copy-start.36 = (f32[1280]{0:T(1024)}, f32[1280]{0:T(1024)S(1)}, u32[]{:S(2)}) copy-start(f32[1280]{0:T(1024)S(1)} %get-tuple-element.177) | copy-start | bytes 15364
  (13 other events, 30.4 us)

commit v4 on v3

--- a/solution.py
+++ b/solution.py
@@ -654,6 +654,302 @@
     )(second, low, up, down)
 
 
+def one_hot_rows(lens, c, block, part, rows, along):
+    per = rows // block
+    at = 0
+    ranks = []
+    for b in range((part + 1) * per):
+        if b >= part * per:
+            slot = lax.broadcasted_iota(jnp.int32, (1, block) if along else (block, 1), along)
+            ranks.append(jnp.where(slot < lens[c, b], slot + at, -1))
+        at = at + lens[c, b]
+    rank = jnp.concatenate(ranks, axis=along)
+    line = lax.broadcasted_iota(jnp.int32, (FILLED, rows) if along else (rows, FILLED), 1 - along)
+    return jnp.where(line == rank, 1.0, 0.0).astype(BF)
+
+
+def normed_rows(values, gain, shift):
+    center = values - jnp.mean(values, axis=1, keepdims=True)
+    inverse = lax.rsqrt(jnp.mean(center * center, axis=1, keepdims=True) + EPS)
+    return center * inverse * gain + shift
+
+
+def attend_gather_kernel(
+    block, heads,
+    lens, tokens_in, weight, output_in, norms,
+    first_out, kept_out, mixed_out, middle_out, second_out,
+    tok, first, weights, outputs, qkv, packed, mixed, mixed_got, middle, second,
+    load_sem, send_sem, recv_sem, turn_send, turn_recv, out_sem,
+):
+    cells, rows, width = tok.shape
+    wide = heads * HEAD_DIM
+    cell = lax.axis_index("cells")
+    place = lax.axis_index("chrom")
+    core = place % 2
+
+    def chrom_near(r):
+        return (cell, (place // 2 + r // 2) % 2 * 2 + (core + r % 2) % 2)
+
+    barrier = pltpu.get_barrier_semaphore()
+    for r in range(1, 4):
+        pl.semaphore_signal(barrier, inc=1, device_id=chrom_near(r), device_id_type=MESH)
+
+    def load(src, dst, sem):
+        copy = pltpu.make_async_copy(src, dst, sem)
+        copy.start()
+        return copy
+
+    loads = [
+        load(tokens_in.at[0], tok.at[0], load_sem.at[0]),
+        load(tokens_in.at[1], tok.at[1], load_sem.at[1]),
+        load(tokens_in.at[2], tok.at[2], load_sem.at[2]),
+        load(weight, weights, load_sem.at[3]),
+        load(output_in, outputs, load_sem.at[4]),
+    ]
+    sent, writes = [], []
+
+    def remote(src, dst, send, recv, r):
+        copy = pltpu.make_async_remote_copy(
+            src_ref=src, dst_ref=dst, send_sem=send, recv_sem=recv,
+            device_id=chrom_near(r), device_id_type=MESH,
+        )
+        copy.start()
+        sent.append(copy)
+        return copy
+
+    def part_rows(r):
+        return slice(r * rows, (r + 1) * rows)
+
+    near, over, across = {}, {}, {}
+
+    def send_over(c):
+        over[c] = remote(
+            first.at[c, part_rows(0)], first.at[c, part_rows(2)], send_sem.at[3 * c], recv_sem.at[3 * c], 2
+        )
+
+    for c in range(cells):
+        loads[c].wait()
+
+        def some(i, carry, c=c):
+            here = pl.ds(pl.multiple_of(i * 64, 64), 64)
+            first[c, here, :] = normed_rows(tok[c, here, :].astype(F32), norms[0:1, :], norms[1:2, :]).astype(BF)
+            return carry
+
+        lax.fori_loop(0, rows // 64, some, 0)
+        if c == 0:
+            pl.semaphore_wait(barrier, 3)
+            send_over(0)
+        near[c] = remote(
+            first.at[c, part_rows(0)], first.at[c, part_rows(1)],
+            send_sem.at[3 * c + 1], recv_sem.at[3 * c + 1], 1,
+        )
+    loads[3].wait()
+
+    def project(c, r):
+        qkv[c, part_rows(r), :] = jnp.dot(
+            first[c, part_rows(r), :], weights[...], preferred_element_type=F32
+        ).astype(BF)
+
+    for c in range(cells):
+        project(c, 0)
+    for c in range(cells):
+        near[c].wait_recv()
+        project(c, 1)
+    loads[4].wait()
+
+    turns = {}
+
+    def finish(c):
+        for copy in turns[c]:
+            copy.wait_recv()
+        writes.append(load(mixed_got.at[c], mixed_out.at[c], out_sem.at[5 * c]))
+        total = tok[c].astype(F32)
+        for r in range(4):
+            total = total + jnp.dot(
+                mixed_got[c, r], outputs[r * wide : (r + 1) * wide, :], preferred_element_type=F32
+            )
+        middle[c] = total
+
+        def some(i, carry):
+            here = pl.ds(pl.multiple_of(i * 64, 64), 64)
+            second[c, here, :] = normed_rows(middle[c, here, :], norms[2:3, :], norms[3:4, :]).astype(BF)
+            return carry
+
+        lax.fori_loop(0, rows // 64, some, 0)
+        writes.append(load(middle.at[c], middle_out.at[c], out_sem.at[5 * c + 1]))
+        writes.append(load(second.at[c], second_out.at[c], out_sem.at[5 * c + 2]))
+
+    scale = LOG2E / math.sqrt(HEAD_DIM)
+    ones = jnp.ones((FILLED, HEAD_DIM), BF)
+    for c in range(cells):
+        over[c].wait_recv()
+        across[c] = remote(
+            first.at[c, part_rows(2)], first.at[c, part_rows(3)],
+            send_sem.at[3 * c + 2], recv_sem.at[3 * c + 2], 1,
+        )
+        if c + 1 < cells:
+            send_over(c + 1)
+        project(c, 2)
+        across[c].wait_recv()
+        project(c, 3)
+        writes.append(load(first.at[c], first_out.at[c], out_sem.at[5 * c + 3]))
+        total = None
+        for r in range(4):
+            part = jnp.dot(
+                one_hot_rows(lens, c, block, r, rows, 1), qkv[c, part_rows(r), :], preferred_element_type=F32
+            )
+            total = part if total is None else total + part
+        packed[c] = total.astype(BF)
+        writes.append(load(packed.at[c], kept_out.at[c], out_sem.at[5 * c + 4]))
+        turns[c] = []
+        for r in (2, 3, 1, 0):
+            for h in range(heads):
+                lo = h * HEAD_DIM
+                q = qkv[c, part_rows(r), lo : lo + HEAD_DIM]
+                k = packed[c, :, wide + lo : wide + lo + HEAD_DIM]
+                v = packed[c, :, 2 * wide + lo : 2 * wide + lo + HEAD_DIM]
+                s = lax.dot_general(q, k, NT, preferred_element_type=F32)
+                top = jnp.max(s, axis=1, keepdims=True) * scale
+                e = jnp.exp2(s * scale - top).astype(BF)
+                o = jnp.dot(e, jnp.concatenate([v, ones], axis=1), preferred_element_type=F32)
+                o = (o[:, :HEAD_DIM] / o[:, HEAD_DIM:]).astype(BF)
+                if r:
+                    mixed[c, r, :, lo : lo + HEAD_DIM] = o
+                else:
+                    mixed_got[c, 0, :, lo : lo + HEAD_DIM] = o
+            if r:
+                n = 3 * c + r - 1
+                turns[c].append(
+                    remote(mixed.at[c, r], mixed_got.at[c, r], turn_send.at[n], turn_recv.at[n], r)
+                )
+        if c:
+            finish(c - 1)
+    finish(cells - 1)
+    for copy in writes:
+        copy.wait()
+    for copy in sent:
+        copy.wait_send()
+
+
+def attend_gather(lens, tokens, weight, output, norms, block):
+    cells, rows, width = tokens.shape
+    wide = weight.shape[1] // 3
+    heads = wide // HEAD_DIM
+    anywhere = pl.BlockSpec(memory_space=pl.ANY)
+    local = pl.BlockSpec(memory_space=pltpu.VMEM)
+    dma = pltpu.SemaphoreType.DMA
+    shapes = [
+        jax.ShapeDtypeStruct((cells, 4 * rows, width), BF),
+        jax.ShapeDtypeStruct((cells, FILLED, 3 * wide), BF),
+        jax.ShapeDtypeStruct((cells, 4, rows, wide), BF),
+        jax.ShapeDtypeStruct((cells, rows, width), F32),
+        jax.ShapeDtypeStruct((cells, rows, width), BF),
+    ]
+    return pl.pallas_call(
+        functools.partial(attend_gather_kernel, block, heads),
+        in_specs=[smem()] + [anywhere] * 3 + [local],
+        out_specs=[anywhere] * 5,
+        out_shape=shapes,
+        scratch_shapes=[
+            pltpu.VMEM((cells, rows, width), BF),
+            pltpu.VMEM((cells, 4 * rows, width), BF),
+            pltpu.VMEM((width, 3 * wide), BF),
+            pltpu.VMEM((width, width), BF),
+            pltpu.VMEM((cells, 4 * rows, 3 * wide), BF),
+            pltpu.VMEM((cells, FILLED, 3 * wide), BF),
+            pltpu.VMEM((cells, 4, rows, wide), BF),
+            pltpu.VMEM((cells, 4, rows, wide), BF),
+            pltpu.VMEM((cells, rows, width), F32),
+            pltpu.VMEM((cells, rows, width), BF),
+            dma((5,)), dma((9,)), dma((9,)), dma((9,)), dma((9,)), dma((5 * cells,)),
+        ],
+        compiler_params=pltpu.CompilerParams(
+            vmem_limit_bytes=VMEM_MAX, collective_id=2, has_side_effects=True
+        ),
+        cost_estimate=cost(6e10, 6e7),
+        name="attend_gather",
+    )(lens, tokens, weight, output, norms)
+
+
+def middle_kernel(
+    middle, back, part, cotangent, scale, mixed, output, gain,
+    layer_out, low_out, g0, g1, g2, g3, output_part, sums, total,
+):
+    step = pl.program_id(0)
+    rows = middle.shape[1]
+    wide = mixed.shape[3]
+    half = middle.shape[2] // 2
+    place = lax.axis_index("chrom")
+
+    @pl.when(step == 0)
+    def _():
+        sums[...] = jnp.zeros_like(sums)
+        total[...] = jnp.zeros_like(total)
+
+    def some(i, carry):
+        here = pl.ds(pl.multiple_of(i * 64, 64), 64)
+        values = middle[0, here, :]
+        layer_out[0, here, :] = (values + part[0, here, :]).astype(BF)
+        center = values - jnp.mean(values, axis=1, keepdims=True)
+        inverse = lax.rsqrt(jnp.mean(center * center, axis=1, keepdims=True) + EPS)
+        normed = center * inverse
+        grad = back[0, here, :]
+        sums[2:3, :] += jnp.sum(grad * normed, axis=0, keepdims=True)
+        sums[3:4, :] += jnp.sum(grad, axis=0, keepdims=True)
+        scaled = grad * gain[...]
+        through = inverse * (
+            scaled
+            - jnp.mean(scaled, axis=1, keepdims=True)
+            - normed * jnp.mean(scaled * normed, axis=1, keepdims=True)
+        )
+        low_out[0, here, :] = (cotangent[0, here, :].astype(F32) * scale[0, here, :] + through).astype(BF)
+        return carry
+
+    lax.fori_loop(0, rows // 64, some, 0)
+    head = jnp.where(place == 0, middle[0, :1, :] + part[0, :1, :], 0.0)
+    sums[0:1, :] += head
+    sums[1:2, :] += head * head
+    for r, out in enumerate((g0, g1, g2, g3)):
+        out[0] = lax.dot_general(
+            low_out[0], output[r * wide : (r + 1) * wide, :], NT, preferred_element_type=F32
+        ).astype(BF)
+        total[r] += lax.dot_general(mixed[0, r], low_out[0], TN, preferred_element_type=F32)
+
+    @pl.when(step == pl.num_programs(0) - 1)
+    def _():
+        for j in range(4):
+            r = (place // 2 + j // 2) % 2 * 2 + (place % 2 + j % 2) % 2
+            values = total[r].astype(BF)
+            for s in range(4):
+                k = 4 * j + s
+                at = (k // 8, (k // 4) % 2, (k // 2) % 2, k % 2)
+                for c in range(2):
+                    output_part[(c,) + at] = values[s * 80 : (s + 1) * 80, c * half : (c + 1) * half]
+
+
+def middle_step(middle, back, part, cotangent, scale, mixed, output, gain):
+    cells, rows, width = middle.shape
+    wide = mixed.shape[3]
+    one = lambda *shape: pl.BlockSpec((1,) + shape, lambda c: (c,) + (0,) * len(shape))
+    parted = (2, 2, 2, 2, 2, 80, width // 2)
+    return pl.pallas_call(
+        middle_kernel,
+        grid=(cells,),
+        in_specs=[
+            one(rows, width), one(rows, width), one(rows, width), one(rows, width), one(rows, 1),
+            one(4, rows, wide), whole(output.shape), whole(gain.shape),
+        ],
+        out_specs=[one(rows, width), one(rows, width)] + [one(rows, wide)] * 4 + [whole(parted), whole((8, width))],
+        out_shape=[jax.ShapeDtypeStruct(middle.shape, BF)] * 2
+        + [jax.ShapeDtypeStruct((cells, rows, wide), BF)] * 4
+        + [jax.ShapeDtypeStruct(parted, BF), jax.ShapeDtypeStruct((8, width), F32)],
+        scratch_shapes=[pltpu.VMEM((4, wide, width), F32)],
+        compiler_params=pltpu.CompilerParams(vmem_limit_bytes=VMEM_MAX),
+        cost_estimate=cost(8 * cells * rows * width * wide * 2, 3e7),
+        name="middle_step",
+    )(middle, back, part, cotangent, scale, mixed, output, gain)
+
+
 QUERY_ITEMS = ((0, 512, "xzh"), (512, 960, "zxh"))
 
 
@@ -667,9 +963,8 @@
 
 def attend_sum_kernel(
     block, heads,
-    lens, g0, g1, g2, g3, kept, *refs
+    lens, g0, g1, g2, g3, kept, first_in, *refs
 ):
-    firsts = refs[:12]
     (
         weight, up_z_in, up_y_in, out_in, down_ab_in, down_c_in, early_in, tokens_in, through_in, gain,
         tokens_out, query_out, up_z_out, up_y_out, out_out, down_out, early_out, late_out,
@@ -680,7 +975,7 @@
         uz1, uz2, uz3, up_z_last, up_z_got, uy1, uy2, uy3, up_y_last, up_y_got,
         oc1, oc2, oc3, oc4, oc5, out_last, out_got, down_got, down_last, early, early_got, late, late_got, column_sum, norm_in,
         load_sem, first_sem, turn_send, turn_recv, back_send, back_recv, sum_send, sum_recv, end_sem, norm_sem,
-    ) = refs[12:]
+    ) = refs
     sources = (g0, g1, g2, g3)
     cells = kept.shape[0]
     rows = g0.shape[1]
@@ -729,14 +1024,7 @@
     ]
 
     def load_first(c):
-        return [
-            load(
-                firsts[4 * c + r],
-                first.at[c % 2, r * rows : (r + 1) * rows],
-                first_sem.at[4 * c + r],
-            )
-            for r in range(4)
-        ]
+        return [load(first_in.at[c], first.at[c % 2], first_sem.at[c])]
 
     first_loads = {c: load_first(c) for c in range(2)}
     early_load = load(early_in, early.at[0], load_sem.at[12])
@@ -773,7 +1061,7 @@
 
     item("uz", up_z, "*hxy", "xyh", (uz1, uz2, uz3))
     item("uy", up_y, "*hzx", "zxh", (uy1, uy2, uy3))
-    item("o", out_part, "chzxy", "czxyh", (oc1, oc2, oc3, oc4, oc5))
+    item("o", out_part, "chzxy", "cyxzh", (oc1, oc2, oc3, oc4, oc5))
     item("da", down_ab, "z", "z", (got_ab,))
     item("dc", down_c, "y", "y", (got_c,))
     for n, (lo, hi, stages) in enumerate(QUERY_ITEMS):
@@ -885,8 +1173,6 @@
 
     for copy in extra:
         copy.wait()
-    go("da", 0)
-    go("dc", 0)
     go("uz", 0)
     go("uy", 0)
     go("o", 0)
@@ -921,7 +1207,7 @@
             inverse = lax.rsqrt(jnp.mean(center * center, axis=1, keepdims=True) + EPS)
             normed = center * inverse
             scaled = keep_back[c, here, :] + got_near[c, here, :].astype(F32)
-            scaled = (scaled + got_over[c, here, :].astype(F32)) * gain[...]
+            scaled = (scaled + got_over[c, here, :].astype(F32)) * gain[0:1, :]
             keep_back[c, here, :] = got_far[c, here, :].astype(F32) + inverse * (
                 scaled
                 - jnp.mean(scaled, axis=1, keepdims=True)
@@ -940,20 +1226,19 @@
     ends = []
     events = {
         (0, 0): [(end, "o", 0), (vector_end, "early", 0)],
-        (0, 1): [(vector_end, "early", 1)],
-        (0, 2): [(end, "dc", 0), (vector_end, "early", 2)],
-        (0, 3): [(end, "uz", 0), (vector_end, "early", 3)],
-        (0, 4): [(end, "uy", 0), (end, "da", 0), (down_start, 0, 0), (vector_end, "early", 4)],
-        (0, 6): [(end, "uy", 1)],
-        (1, 0): [(end, "uz", 1), (back_sum, 0, 0)],
-        (1, 1): [(end, "o", 1)],
-        (1, 2): [(end, "uy", 2), (swap_last, "uy", 0), (down_add, 0, 0)],
-        (1, 3): [(end, "o", 2)],
-        (1, 4): [(end, "uz", 2), (swap_last, "uz", 0), (down_end, 0, 0)],
-        (1, 5): [(end, "o", 3)],
-        (1, 6): [(back_end, 0, 0)],
-        (2, 0): [(end, "o", 4), (swap_last, "o", 0), (back_sum, 1, 0)],
-        (2, 4): [(back_end, 1, 0)],
+        (0, 2): [(end, "uy", 0)],
+        (0, 3): [(end, "uz", 0), (end, "dc", 0), (vector_end, "early", 1)],
+        (0, 5): [(end, "da", 0), (down_start, 0, 0), (end, "uy", 1), (vector_end, "early", 2)],
+        (1, 0): [(vector_end, "early", 3)],
+        (1, 1): [(back_sum, 0, 0)],
+        (1, 3): [(vector_end, "early", 4)],
+        (1, 4): [(end, "uy", 2), (swap_last, "uy", 0), (end, "uz", 1)],
+        (1, 5): [(end, "o", 1)],
+        (2, 0): [(down_add, 0, 0), (back_end, 0, 0), (back_sum, 1, 0)],
+        (2, 1): [(end, "uz", 2), (swap_last, "uz", 0), (end, "o", 2), (down_end, 0, 0)],
+        (2, 4): [(end, "o", 3)],
+        (2, 5): [(back_end, 1, 0)],
+        (2, 6): [(vector_end, "late", 0), (end, "o", 4), (swap_last, "o", 0)],
     }
 
     def run(key):
@@ -963,27 +1248,19 @@
     scale = LOG2E / math.sqrt(HEAD_DIM)
     inv_root = 1.0 / math.sqrt(HEAD_DIM)
     chunk = 256
-    per = rows // block
     for c in range(cells):
         own_loads[c][0].wait()
         own_loads[c][1].wait()
         for copy in turns[c]:
             copy.wait_recv()
+        if c == 0:
+            go("da", 0)
+            go("dc", 0)
         if c + 1 < cells:
             turns[c + 1] = turn(c + 1)
-        ranks, columns = [], []
-        at = 0
-        for b in range(4 * per):
-            slot = lax.broadcasted_iota(jnp.int32, (1, block), 1)
-            ranks.append(jnp.where(slot < lens[c, b], slot + at, -1))
-            slot = lax.broadcasted_iota(jnp.int32, (block, 1), 0)
-            columns.append(jnp.where(slot < lens[c, b], slot + at, -1))
-            at = at + lens[c, b]
         packed = jnp.zeros((wide, FILLED), F32)
         for r in range(4):
-            rank = jnp.concatenate(ranks[r * per : (r + 1) * per], axis=1)
-            line = lax.broadcasted_iota(jnp.int32, (FILLED, rows), 0)
-            move = jnp.where(line == rank, 1.0, 0.0).astype(BF)
+            move = one_hot_rows(lens, c, block, r, rows, 1)
             grad = grads[c, r].astype(F32).T.astype(BF)
             packed = packed + lax.dot_general(grad, move, NT, preferred_element_type=F32)
         query_t = qkv_c[c % 2, :, :wide].astype(F32).T.astype(BF)
@@ -1015,9 +1292,7 @@
         if c + 2 < cells:
             own_loads[c + 2] = load_own(c + 2)
         for r in range(4):
-            rank = jnp.concatenate(columns[r * per : (r + 1) * per], axis=0)
-            line = lax.broadcasted_iota(jnp.int32, (rows, FILLED), 1)
-            move = jnp.where(line == rank, 1.0, 0.0).astype(BF)
+            move = one_hot_rows(lens, c, block, r, rows, 0)
             moved[r * rows : (r + 1) * rows, :] = jnp.dot(
                 move, back[...], preferred_element_type=F32
             ).astype(BF)
@@ -1068,19 +1343,18 @@
                 sent.append(copy)
         near_copies[c] = lines
         run((c, 6))
+    vector_end("late", 1)
     back_sum(cells - 1, 0)
-    vector_end("late", 0)
+    vector_end("late", 2)
+    end("q1", 0)
+    vector_end("late", 3)
     end("q0", 0)
-    end("q1", 0)
-    vector_end("late", 1)
+    vector_end("late", 4)
     end("q1", 1)
+    back_end(cells - 1, 0)
     end("q0", 1)
-    vector_end("late", 2)
-    back_end(cells - 1, 0)
-    vector_end("late", 3)
+    end("q1", 2)
     end("q0", 2)
-    end("q1", 2)
-    vector_end("late", 4)
     values = query_part[mine["h"], mine["z"], mine["x"]]
     for j in range(4):
         query_last[j] = values[j * 40 : (j + 1) * 40]
@@ -1113,10 +1387,10 @@
 
 
 def attend_sum(
-    lens, grads, kept, firsts, weight, up_z, up_y, out_part, down_ab, down_c, early, tokens, through, gain, block
+    lens, grads, kept, first, weight, up_z, up_y, out_part, down_ab, down_c, early, tokens, through, gain, block
 ):
     cells, rows, wide = grads[0].shape
-    width = firsts[0].shape[1]
+    width = first.shape[2]
     heads = wide // HEAD_DIM
     seq = 4 * rows
     anywhere = pl.BlockSpec(memory_space=pl.ANY)
@@ -1125,7 +1399,7 @@
     qa, qb = [hi - lo for lo, hi, _ in QUERY_ITEMS]
     return pl.pallas_call(
         functools.partial(attend_sum_kernel, block, heads),
-        in_specs=[smem()] + [anywhere] * (5 + 12 + 9) + [pl.BlockSpec(memory_space=pltpu.VMEM)],
+        in_specs=[smem()] + [anywhere] * 15 + [pl.BlockSpec(memory_space=pltpu.VMEM)],
         out_specs=[anywhere] * 8,
         out_shape=[
             jax.ShapeDtypeStruct((cells, rows, width), F32),
@@ -1164,7 +1438,7 @@
             pltpu.VMEM((6, 8, width), F32), pltpu.VMEM((5, 8, width), F32),
             pltpu.VMEM((6, 8, width), F32), pltpu.VMEM((5, 8, width), F32),
             pltpu.VMEM((8, 3 * wide), F32), vmem(rows, width),
-            dma((13,)), dma((12,)), dma((9,)), dma((9,)), dma((9,)), dma((9,)), dma((36,)), dma((36,)),
+            dma((13,)), dma((3,)), dma((9,)), dma((9,)), dma((9,)), dma((9,)), dma((36,)), dma((36,)),
             dma((16,)), dma((2 * cells,)),
         ],
         compiler_params=pltpu.CompilerParams(
@@ -1173,7 +1447,7 @@
         cost_estimate=cost(8e10, 6e7),
         name="attend_sum",
     )(
-        lens, *grads, kept, *firsts, weight, up_z, up_y, out_part, down_ab, down_c, early, tokens, through, gain
+        lens, *grads, kept, first, weight, up_z, up_y, out_part, down_ab, down_c, early, tokens, through, gain
     )
 
 
@@ -1361,27 +1635,38 @@
         [lax.dynamic_slice_in_dim(output_weight, n * wide, wide, 0) for n in near], axis=0
     )
 
-    flat = tokens.reshape(rows, width).astype(F32)
-    first_out, first_norm, first_inv = norm_rows(flat, first_gain, first_shift)
-    first_low = first_out.astype(BF).reshape(cells_here, seq_here, width)
-    first_all, mixed_near, kept = [], [], []
-    for c in range(cells_here):
-        mine = first_low[c]
-        over = swap(mine, "chrom", 2)
-        first_all.append([mine, swap(mine, "chrom", 1), over, swap(over, "chrom", 1)])
-    for c in range(cells_here):
-        if c:
-            first_all[c], mixed_near[-1] = lax.optimization_barrier((first_all[c], mixed_near[-1]))
-        mixed, qkv_c = attend(first_all[c], lens[c], qkv_weight, block)
-        kept.append(qkv_c)
-        mixed_near.append(
-            jnp.concatenate([mixed[0]] + [swap(mixed[r], "chrom", r) for r in range(1, parts)], axis=1)
-        )
-    mixed_flat = jnp.concatenate(mixed_near, axis=0)
-
-    middle = flat + jnp.dot(mixed_flat, output_near, preferred_element_type=F32)
-    second_out, second_norm, second_inv = norm_rows(middle, second_gain, second_shift)
-    second_low = second_out.astype(BF)
+    fused = lax.axis_size("cells") == 8 and parts == 4
+    if fused:
+        norms = jnp.stack([first_gain, first_shift, second_gain, second_shift])
+        first_all, kept, mixed_near, middle, second_low = attend_gather(
+            lens,
+            tokens,
+            qkv_weight,
+            output_near,
+            norms,
+            block,
+        )
+        second_low = second_low.reshape(rows, width)
+    else:
+        flat = tokens.reshape(rows, width).astype(F32)
+        first_out, first_norm, first_inv = norm_rows(flat, first_gain, first_shift)
+        first_low = first_out.astype(BF).reshape(cells_here, seq_here, width)
+        first_all, mixed_near, kept = [], [], []
+        for c in range(cells_here):
+            mine = first_low[c]
+            over = swap(mine, "chrom", 2)
+            first_all.append([mine, swap(mine, "chrom", 1), over, swap(over, "chrom", 1)])
+        for c in range(cells_here):
+            mixed, qkv_c = attend(first_all[c], lens[c], qkv_weight, block)
+            kept.append(qkv_c)
+            mixed_near.append(
+                jnp.concatenate([mixed[0]] + [swap(mixed[r], "chrom", r) for r in range(1, parts)], axis=1)
+            )
+        mixed_flat = jnp.concatenate(mixed_near, axis=0)
+
+        middle = flat + jnp.dot(mixed_flat, output_near, preferred_element_type=F32)
+        second_out, second_norm, second_inv = norm_rows(middle, second_gain, second_shift)
+        second_low = second_out.astype(BF)
     result_back = (
         cotangent.astype(F32)
         * cell_scale[:, None, None]
@@ -1389,7 +1674,6 @@
     ).reshape(rows, width)
     down_low = result_back.astype(BF)
     low_bits = [("cells", b) for b in range(cell_bits - 1)]
-    fused = lax.axis_size("cells") == 8 and parts == 4
     if fused:
         second_back, result_part, down_ab, down_c, up_z, up_y = feed_forward_sum(
             second_low, down_low, up_weight, down_weight
@@ -1398,49 +1682,57 @@
         second_back, result_part, down_out, up_out = feed_forward_plain(
             second_low, down_low, up_weight, down_weight
         )
-    result = middle + result_part
-    result_cells = result.reshape(cells_here, seq_here, width)
-    layer_out = result_cells.astype(BF)
-
-    cls_rows = jnp.where(place == 0, result_cells[:, 0, :], 0.0)
-    cls_total = jnp.sum(cls_rows, axis=0)
-    cls_square = jnp.sum(cls_rows * cls_rows, axis=0)
-
-    middle_ln, second_gain_grad, second_shift_grad = norm_back(
-        second_back, second_norm, second_inv, second_gain
-    )
-    middle_back = result_back + middle_ln
-    attend_low = middle_back.astype(BF)
-    output_grad = contract(mixed_flat, attend_low).reshape(parts, wide, width)
-    output_grad = jnp.concatenate(
-        [lax.dynamic_index_in_dim(output_grad, place ^ j, 0, keepdims=False) for j in range(parts)],
-        axis=0,
-    )
-    early = jnp.stack([cls_total, cls_square, second_gain_grad, second_shift_grad])
-
     if fused:
-        grads_near = [
-            back_through(attend_low, output_near[r * wide : (r + 1) * wide])
-            .astype(BF)
-            .reshape(cells_here, seq_here, wide)
-            for r in range(parts)
-        ]
-        output_part = output_grad.astype(BF).reshape(2, 2, 2, 2, 80, 2, width // 2)
+        cells_shape = (cells_here, seq_here, width)
+        layer_out, attend_low, *rest = middle_step(
+            middle,
+            second_back.reshape(cells_shape),
+            result_part.reshape(cells_shape),
+            cotangent,
+            cell_scale[:, None, None] * local_valid.astype(F32)[:, :, None],
+            mixed_near,
+            output_near,
+            second_gain.reshape(1, width),
+        )
+        grads_near, output_part, early = rest[:4], rest[4], rest[5]
+    else:
+        result = middle + result_part
+        result_cells = result.reshape(cells_here, seq_here, width)
+        layer_out = result_cells.astype(BF)
+
+        cls_rows = jnp.where(place == 0, result_cells[:, 0, :], 0.0)
+        cls_total = jnp.sum(cls_rows, axis=0)
+        cls_square = jnp.sum(cls_rows * cls_rows, axis=0)
+
+        middle_ln, second_gain_grad, second_shift_grad = norm_back(
+            second_back, second_norm, second_inv, second_gain
+        )
+        middle_back = result_back + middle_ln
+        attend_low = middle_back.astype(BF)
+        output_grad = contract(mixed_flat, attend_low).reshape(parts, wide, width)
+        output_grad = jnp.concatenate(
+            [lax.dynamic_index_in_dim(output_grad, place ^ j, 0, keepdims=False) for j in range(parts)],
+            axis=0,
+        )
+        early = jnp.stack([cls_total, cls_square, second_gain_grad, second_shift_grad])
+
+
+    if fused:
         tokens_grad, qkv_got, up_z, up_y, out_two, down_grad, early, late = attend_sum(
             lens,
             grads_near,
-            jnp.stack(kept),
-            [piece for line in first_all for piece in line],
+            kept,
+            first_all,
             qkv_weight,
             up_z,
             up_y,
-            output_part.transpose(5, 0, 1, 2, 3, 4, 6),
+            output_part,
             down_ab,
             down_c,
-            jnp.concatenate([early, jnp.zeros_like(early)], axis=0),
+            early,
             tokens,
-            attend_low.reshape(cells_here, seq_here, width),
-            first_gain[None, :],
+            attend_low,
+            norms,
             block,
         )
         late = jnp.stack([(late[0] - first_shift * late[1]) / first_gain, late[1]])

time: 492 us -> 411 us (0.84); the launches traced: 483 us -> 407 us
  Pallas kernels: 332 us -> 372 us
  local copies, waits for them, and re-layouts: 52.2 us -> 20.3 us
  waiting for transfers between devices: 29.2 us -> 0 us
  other arithmetic: 35.6 us -> 13.5 us
  starting transfers between devices: 17.3 us -> 0 us
  matrix products: 14.7 us -> 0 us
    pallas_call x3 -> x2, Pallas kernels: 51.4 us -> 101 us  [the longest x1 80.9 us: attend_gather(): pl.pallas_call(functools.partial(attend_gather_kernel, block, heads), in_...]
    ppermute x18 -> x0, waiting for transfers between devices: 29.2 us -> none  [swap(): return lax.ppermute(x, axis, [(i, i ^ mask) for i in range(size)])]
    ppermute x18 -> x0, starting transfers between devices: 17.3 us -> none  [swap(): return lax.ppermute(x, axis, [(i, i ^ mask) for i in range(size)])]
    dot_general x6 -> x0, matrix products: 14.7 us -> none  [the longest x4 6.58 us: back_through(): return lax.dot_general(grad, weight, NT, preferred_element_type=F32)]
    concatenate x4 -> x0, local copies, waits for them, and re-layouts: 14.4 us -> none  [the longest x3 13.8 us: per_device(): jnp.concatenate([mixed[0]] + [swap(mixed[r], 'chrom', r) for r in range(1...]
    convert_element_type x6 -> x0, local copies, waits for them, and re-layouts: 11.7 us -> none  [the longest x2 7.49 us: per_device(): output_part = output_grad.astype(BF).reshape(2, 2, 2, 2, 80, 2, width // 2)]
    convert_element_type x4 -> x0, other arithmetic: 10.7 us -> none  [the longest x1 4.27 us: per_device(): attend_low = middle_back.astype(BF)]
    reduce_sum x5 -> x0, other arithmetic: 9.45 us -> none  [the longest x1 4.66 us: norm_back(): jnp.sum(grad_out * normed, axis=0)]
  transfers between devices with their start and end apart: 18 -> 0, of which waited for: 8 -> 0; matrix products, arithmetic and copies ran while one was open for 7% -> 0% of each run, Pallas kernels for 7% -> 0%
where the time goes in v4:
time: 411 us; the launch traced here: 407 us
  Pallas kernels  372 us (91%)
  local copies, waits for them, and re-layouts  20.3 us (5%)
  other arithmetic  13.5 us (3%)
    pallas_call x1, Pallas kernels, attend_sum(): pl.pallas_call(functools.partial(attend_sum_kernel, block, heads), in_spe...  172 us
    pallas_call x1, Pallas kernels, feed_forward_sum(): pl.pallas_call(feed_sum_kernel, in_specs=[anywhere] * 4, out_specs=[anywh...  99.4 us
    pallas_call x1, Pallas kernels, attend_gather(): pl.pallas_call(functools.partial(attend_gather_kernel, block, heads), in_...  80.9 us
    pallas_call x1, Pallas kernels, middle_step(): pl.pallas_call(middle_kernel, grid=(cells,), in_specs=[one(rows, width),...  19.6 us

profile of v4, /device:TPU:1, one launch (start us, length us, event | category | flops | bytes accessed | tf_op | source)
XLA Modules:
  0.0 407.1 jit_solution(4256746785583040461)
XLA Ops:
  0.7 2.1 constant_dynamic-slice_fusion.7
  2.8 0.0 copy-start.4
  2.8 1.9 pad_maximum_fusion.output_in.output
  4.7 0.1 constant_dynamic-slice_fusion.14
  4.7 0.7 pad_add_fusion.lens
  5.4 2.8 constant_dynamic-slice_fusion.8
  8.2 1.7 constant_dynamic-slice_fusion.10
  9.9 0.0 copy-start.9
  9.9 0.0 copy-start.8
  9.9 0.0 copy-start.7
  9.9 2.6 pad_maximum_fusion.1.weight.refs_0_
  12.5 0.0 copy-start.5
  12.6 0.6 pad_maximum_fusion.2.norms.refs_9_
  13.3 80.9 %attend_gather.1 = (bf16[3,1024,1280]{2,1,0:T(8,128)(2,1)}, bf16[3,768,960]{2,1,0:T(8,128)(2,1)}, bf16[3,4,256,320]{3,2,1,0:T(8,128)(2,1)}, f32[3,256,1280]{2,1,0:T(8,128)}, bf16[3,256,1280]{2,1,0:T(8,128)(2,1)}) custom-call(s32[3,8]{1,0:T(4,128)} %pad_add_fusion.lens, bf16[3,256,1280]{2,1,0:T(8,128)(2,1)} %refs_7_.1, ...), custom_call_target="tpu_custom_call" | custom-call | flops 60000002048 | bytes 60000000 | tf_op jit(solution)/shard_map/attend_gather/pallas_call | solution.py:848
  94.2 0.1 dynamic-slice.3
  94.3 0.2 select_reduce_fusion
  94.5 0.1 broadcast_bitcast_fusion
  94.6 0.1 select_bitcast_fusion
  94.7 1.8 multiply_convert_fusion
  96.4 99.4 %feed_sum.1 = (f32[768,1280]{1,0:T(8,128)}, f32[768,1280]{1,0:T(8,128)}, bf16[2,320,1024]{2,1,0:T(8,128)(2,1)}, bf16[2,320,256]{2,1,0:T(8,128)(2,1)}, bf16[3,2,2...) custom-call(bf16[768,1280]{1,0:T(8,128)(2,1)} %bitcast.50, bf16[768,1280]{1,0:T(8,128)(2,1)} %bitcast.46, ...), custom_call_target="tpu_custom_call" | custom-call | flops 60397977600 | bytes 60000000 | tf_op jit(solution)/shard_map/feed_sum/pallas_call | solution.py:618
  195.8 0.9 copy.31.scale
  196.7 19.6 %middle_step.1 = (bf16[3,256,1280]{2,1,0:T(8,128)(2,1)}, bf16[3,256,1280]{2,1,0:T(8,128)(2,1)}, bf16[3,256,320]{2,1,0:T(8,128)(2,1)}, bf16[3,256,320]{2,1,0:T(8,...) custom-call(f32[3,256,1280]{2,1,0:T(8,128)} %get-tuple-element.41.mi, ...), custom_call_target="tpu_custom_call" | custom-call | flops 5033164800 | bytes 30000000 | tf_op jit(solution)/shard_map/middle_step/pallas_call | solution.py:935
  216.4 172.2 %attend_sum.1 = (f32[3,256,1280]{2,1,0:T(8,128)}, bf16[4,40,960]{2,1,0:T(8,128)(2,1)}, bf16[2,3,40,512]{3,2,1,0:T(8,128)(2,1)}, bf16[2,2,40,512]{3,2,1,0:T(8,128...) custom-call(s32[3,8]{1,0:T(4,128)} %pad_add_fusion.lens, ...), custom_call_target="tpu_custom_call" | custom-call | flops 80000000000 | bytes 60000000 | tf_op jit(solution)/shard_map/attend_sum/pallas_call | solution.py:1400
  388.6 1.0 multiply_reduce_fusion
  389.6 0.0 copy-start.6
  389.6 0.6 multiply_subtract_fusion
  390.2 0.9 fusion.5
  391.1 0.9 slice.99
  392.1 0.9 slice.101
  393.0 0.1 maximum_bitcast_fusion
  393.1 0.1 reverse_select_fusion
  393.2 0.9 maximum_convert_fusion
  394.2 0.7 maximum_convert_fusion.1
  394.9 0.1 bitcast_convert_fusion
  394.9 0.1 fusion.6
  395.0 0.1 fusion.7
  395.1 0.1 fusion.8
  395.2 0.1 fusion.9
  395.3 0.8 concatenate.29
  396.1 0.8 concatenate.28
  396.9 0.8 concatenate.27
  397.6 0.9 slice_reduce_fusion.1
  398.5 1.3 dynamic-slice_divide_fusion
  399.9 0.9 convert_element_type.59
  400.8 0.6 fusion.2
  401.4 0.6 fusion.3
  402.0 0.6 fusion.1
  402.5 4.3 %copy.38 = f32[3,256,1280]{2,1,0:T(8,128)} copy(f32[3,256,1280]{2,1,0:T(8,128)} %get-tuple-element.124) | data formatting | bytes 7864320
  (31 shorter events, 0.2 us)
Async XLA Ops:
  2.8 1.9 copy-start.4
  9.9 2.7 copy-start.9
  9.9 2.7 copy-start.8
  9.9 2.7 copy-start.7
  9.9 2.7 copy-start.10
  12.5 81.7 %copy-start.5 = (f32[1,1280]{1,0:T(1,128)}, f32[1,1280]{1,0:T(1,128)S(1)}, u32[]{:S(2)}) copy-start(f32[1,1280]{1,0:T(1,128)S(1)} %stack.21.gain) | copy-start | bytes 15364
  13.3 81.1 %copy-start.11 = (f32[4]{0:T(128)S(1)}, f32[4]{0:T(128)}, u32[]{:S(2)}) copy-start(f32[4]{0:T(128)} %param.19) | copy-start | bytes 52
  13.3 81.1 %copy-start.12 = (s32[3]{0:T(128)S(1)}, s32[3]{0:T(128)}, u32[]{:S(2)}) copy-start(s32[3]{0:T(128)} %param.18) | copy-start | bytes 40
  13.3 81.4 %copy-start = (bf16[3,256,1280]{2,1,0:T(8,128)(2,1)S(1)}, bf16[3,256,1280]{2,1,0:T(8,128)(2,1)}, u32[]{:S(2)}) copy-start(bf16[3,256,1280]{2,1,0:T(8,128)(2,1)} %cotangent.1) | copy-start | bytes 5898244
  388.6 5.6 %copy-start.3 = (bf16[2,1,40,640]{3,2,1,0:T(8,128)(2,1)S(1)}, bf16[2,1,40,640]{3,2,1,0:T(8,128)(2,1)}, u32[]{:S(2)}) copy-start(bf16[2,1,40,640]{3,2,1,0:T(8,128)(2,1)} %get-tuple-element.63) | copy-start | bytes 307204
  388.6 6.3 %copy-start.2 = (bf16[4,40,960]{2,1,0:T(8,128)(2,1)S(1)}, bf16[4,40,960]{2,1,0:T(8,128)(2,1)}, u32[]{:S(2)}) copy-start(bf16[4,40,960]{2,1,0:T(8,128)(2,1)} %get-tuple-element.62) | copy-start | bytes 921604
  389.6 5.4 %copy-start.6 = (f32[1280]{0:T(1024)}, f32[1280]{0:T(1024)S(1)}, u32[]{:S(2)}) copy-start(f32[1280]{0:T(1024)S(1)} %get-tuple-element.135) | copy-start | bytes 15364
  393.1 6.7 %copy-start.1 = (bf16[160,1280]{1,0:T(8,128)(2,1)S(1)}, bf16[160,1280]{1,0:T(8,128)(2,1)}, u32[]{:S(2)}) copy-start(bf16[160,1280]{1,0:T(8,128)(2,1)} %get-tuple-element.67) | copy-start | bytes 1228804

commit v5 on v4

--- a/solution.py
+++ b/solution.py
@@ -871,9 +871,12 @@
     )(lens, tokens, weight, output, norms)
 
 
+MIDDLE_CUT = 1
+
+
 def middle_kernel(
     middle, back, part, cotangent, scale, mixed, output, gain,
-    layer_out, low_out, g0, g1, g2, g3, output_part, sums, total,
+    layer_out, low_out, g0, g1, g2, g3, output_part, sums, low_all, mixed_all,
 ):
     step = pl.program_id(0)
     rows = middle.shape[1]
@@ -884,7 +887,6 @@
     @pl.when(step == 0)
     def _():
         sums[...] = jnp.zeros_like(sums)
-        total[...] = jnp.zeros_like(total)
 
     def some(i, carry):
         here = pl.ds(pl.multiple_of(i * 64, 64), 64)
@@ -906,20 +908,25 @@
         return carry
 
     lax.fori_loop(0, rows // 64, some, 0)
-    head = jnp.where(place == 0, middle[0, :1, :] + part[0, :1, :], 0.0)
+    spot = pl.ds(pl.multiple_of(step * rows, rows), rows)
+    starts = jnp.logical_and(place == 0, step % MIDDLE_CUT == 0)
+    head = jnp.where(starts, middle[0, :1, :] + part[0, :1, :], 0.0)
     sums[0:1, :] += head
     sums[1:2, :] += head * head
     for r, out in enumerate((g0, g1, g2, g3)):
         out[0] = lax.dot_general(
             low_out[0], output[r * wide : (r + 1) * wide, :], NT, preferred_element_type=F32
         ).astype(BF)
-        total[r] += lax.dot_general(mixed[0, r], low_out[0], TN, preferred_element_type=F32)
+        mixed_all[r, spot, :] = mixed[0, r]
+    low_all[spot, :] = low_out[0]
 
     @pl.when(step == pl.num_programs(0) - 1)
     def _():
         for j in range(4):
             r = (place // 2 + j // 2) % 2 * 2 + (place % 2 + j % 2) % 2
-            values = total[r].astype(BF)
+            values = lax.dot_general(
+                mixed_all[r], low_all[...], TN, preferred_element_type=F32
+            ).astype(BF)
             for s in range(4):
                 k = 4 * j + s
                 at = (k // 8, (k // 4) % 2, (k // 2) % 2, k % 2)
@@ -930,20 +937,26 @@
 def middle_step(middle, back, part, cotangent, scale, mixed, output, gain):
     cells, rows, width = middle.shape
     wide = mixed.shape[3]
-    one = lambda *shape: pl.BlockSpec((1,) + shape, lambda c: (c,) + (0,) * len(shape))
+    cut = MIDDLE_CUT
+    some = rows // cut
+
+    def one(last):
+        return pl.BlockSpec((1, some, last), lambda s: (s // cut, s % cut, 0))
+
+    heads = pl.BlockSpec((1, 4, some, wide), lambda s: (s // cut, 0, s % cut, 0))
     parted = (2, 2, 2, 2, 2, 80, width // 2)
     return pl.pallas_call(
         middle_kernel,
-        grid=(cells,),
-        in_specs=[
-            one(rows, width), one(rows, width), one(rows, width), one(rows, width), one(rows, 1),
-            one(4, rows, wide), whole(output.shape), whole(gain.shape),
-        ],
-        out_specs=[one(rows, width), one(rows, width)] + [one(rows, wide)] * 4 + [whole(parted), whole((8, width))],
+        grid=(cells * cut,),
+        in_specs=[one(width)] * 4 + [one(1), heads, whole(output.shape), whole(gain.shape)],
+        out_specs=[one(width)] * 2 + [one(wide)] * 4 + [whole(parted), whole((8, width))],
         out_shape=[jax.ShapeDtypeStruct(middle.shape, BF)] * 2
         + [jax.ShapeDtypeStruct((cells, rows, wide), BF)] * 4
         + [jax.ShapeDtypeStruct(parted, BF), jax.ShapeDtypeStruct((8, width), F32)],
-        scratch_shapes=[pltpu.VMEM((4, wide, width), F32)],
+        scratch_shapes=[
+            pltpu.VMEM((cells * rows, width), BF),
+            pltpu.VMEM((4, cells * rows, wide), BF),
+        ],
         compiler_params=pltpu.CompilerParams(vmem_limit_bytes=VMEM_MAX),
         cost_estimate=cost(8 * cells * rows * width * wide * 2, 3e7),
         name="middle_step",
@@ -1060,8 +1073,8 @@
         items[name] = (part, dims, stages, recvs, cols, [next(sems) for _ in stages], {})
 
     item("uz", up_z, "*hxy", "xyh", (uz1, uz2, uz3))
-    item("uy", up_y, "*hzx", "zxh", (uy1, uy2, uy3))
-    item("o", out_part, "chzxy", "cyxzh", (oc1, oc2, oc3, oc4, oc5))
+    item("uy", up_y, "*hzx", "xzh", (uy1, uy2, uy3))
+    item("o", out_part, "chzxy", "cxyzh", (oc1, oc2, oc3, oc4, oc5))
     item("da", down_ab, "z", "z", (got_ab,))
     item("dc", down_c, "y", "y", (got_c,))
     for n, (lo, hi, stages) in enumerate(QUERY_ITEMS):
@@ -1226,19 +1239,16 @@
     ends = []
     events = {
         (0, 0): [(end, "o", 0), (vector_end, "early", 0)],
-        (0, 2): [(end, "uy", 0)],
-        (0, 3): [(end, "uz", 0), (end, "dc", 0), (vector_end, "early", 1)],
-        (0, 5): [(end, "da", 0), (down_start, 0, 0), (end, "uy", 1), (vector_end, "early", 2)],
-        (1, 0): [(vector_end, "early", 3)],
-        (1, 1): [(back_sum, 0, 0)],
-        (1, 3): [(vector_end, "early", 4)],
-        (1, 4): [(end, "uy", 2), (swap_last, "uy", 0), (end, "uz", 1)],
-        (1, 5): [(end, "o", 1)],
-        (2, 0): [(down_add, 0, 0), (back_end, 0, 0), (back_sum, 1, 0)],
-        (2, 1): [(end, "uz", 2), (swap_last, "uz", 0), (end, "o", 2), (down_end, 0, 0)],
-        (2, 4): [(end, "o", 3)],
+        (0, 3): [(end, "dc", 0), (vector_end, "early", 1)],
+        (0, 4): [(end, "da", 0), (down_start, 0, 0)],
+        (0, 6): [(end, "uy", 0), (vector_end, "early", 2)],
+        (1, 1): [(back_sum, 0, 0), (vector_end, "early", 3)],
+        (1, 3): [(end, "uz", 0), (end, "uy", 1), (down_add, 0, 0)],
+        (1, 5): [(end, "o", 1), (end, "uy", 2), (swap_last, "uy", 0), (vector_end, "early", 4)],
+        (2, 1): [(back_end, 0, 0), (back_sum, 1, 0), (down_end, 0, 0)],
+        (2, 4): [(end, "uz", 1), (end, "o", 2)],
         (2, 5): [(back_end, 1, 0)],
-        (2, 6): [(vector_end, "late", 0), (end, "o", 4), (swap_last, "o", 0)],
+        (2, 6): [(back_sum, 2, 0), (vector_end, "late", 0), (end, "o", 3)],
     }
 
     def run(key):
@@ -1344,17 +1354,20 @@
         near_copies[c] = lines
         run((c, 6))
     vector_end("late", 1)
-    back_sum(cells - 1, 0)
+    end("uz", 2)
+    swap_last("uz", 0)
+    end("q1", 0)
+    end("q0", 0)
     vector_end("late", 2)
-    end("q1", 0)
-    vector_end("late", 3)
-    end("q0", 0)
-    vector_end("late", 4)
+    end("o", 4)
+    swap_last("o", 0)
     end("q1", 1)
     back_end(cells - 1, 0)
     end("q0", 1)
+    vector_end("late", 3)
     end("q1", 2)
     end("q0", 2)
+    vector_end("late", 4)
     values = query_part[mine["h"], mine["z"], mine["x"]]
     for j in range(4):
         query_last[j] = values[j * 40 : (j + 1) * 40]

time: 411 us -> 412 us (level)
  no operation moved by 1% of the time
where the time goes in v5:
time: 412 us; the launch traced here: 408 us
  Pallas kernels  373 us (91%)
  local copies, waits for them, and re-layouts  20.3 us (5%)
  other arithmetic  13.5 us (3%)
    pallas_call x1, Pallas kernels, attend_sum(): pl.pallas_call(functools.partial(attend_sum_kernel, block, heads), in_spe...  174 us
    pallas_call x1, Pallas kernels, feed_forward_sum(): pl.pallas_call(feed_sum_kernel, in_specs=[anywhere] * 4, out_specs=[anywh...  99.4 us
    pallas_call x1, Pallas kernels, attend_gather(): pl.pallas_call(functools.partial(attend_gather_kernel, block, heads), in_...  80.9 us
    pallas_call x1, Pallas kernels, middle_step(): pl.pallas_call(middle_kernel, grid=(cells * cut,), in_specs=[one(width)]...  19.1 us

profile of v5, /device:TPU:1, one launch (start us, length us, event | category | flops | bytes accessed | tf_op | source)
XLA Modules:
  0.0 408.1 jit_solution(7547325784708302994)
XLA Ops:
  0.7 2.1 constant_dynamic-slice_fusion.7
  2.8 0.0 copy-start.4
  2.8 1.9 pad_maximum_fusion.output_in.output
  4.7 0.1 constant_dynamic-slice_fusion.14
  4.7 0.7 pad_add_fusion.lens
  5.4 2.8 constant_dynamic-slice_fusion.8
  8.2 1.7 constant_dynamic-slice_fusion.10
  9.9 0.0 copy-start.9
  9.9 0.0 copy-start.8
  9.9 0.0 copy-start.7
  9.9 0.0 copy-start.10
  9.9 2.6 pad_maximum_fusion.1.weight.refs_0_
  12.6 0.6 pad_maximum_fusion.2.norms.refs_9_
  13.3 80.9 %attend_gather.1 = (bf16[3,1024,1280]{2,1,0:T(8,128)(2,1)}, bf16[3,768,960]{2,1,0:T(8,128)(2,1)}, bf16[3,4,256,320]{3,2,1,0:T(8,128)(2,1)}, f32[3,256,1280]{2,1,0:T(8,128)}, bf16[3,256,1280]{2,1,0:T(8,128)(2,1)}) custom-call(s32[3,8]{1,0:T(4,128)} %pad_add_fusion.lens, bf16[3,256,1280]{2,1,0:T(8,128)(2,1)} %refs_7_.1, ...), custom_call_target="tpu_custom_call" | custom-call | flops 60000002048 | bytes 60000000 | tf_op jit(solution)/shard_map/attend_gather/pallas_call | solution.py:848
  94.2 0.1 dynamic-slice.3
  94.3 0.2 select_reduce_fusion
  94.5 0.1 broadcast_bitcast_fusion
  94.6 0.1 select_bitcast_fusion
  94.7 1.8 multiply_convert_fusion
  96.4 99.4 %feed_sum.1 = (f32[768,1280]{1,0:T(8,128)}, f32[768,1280]{1,0:T(8,128)}, bf16[2,320,1024]{2,1,0:T(8,128)(2,1)}, bf16[2,320,256]{2,1,0:T(8,128)(2,1)}, bf16[3,2,2...) custom-call(bf16[768,1280]{1,0:T(8,128)(2,1)} %bitcast.50, bf16[768,1280]{1,0:T(8,128)(2,1)} %bitcast.46, ...), custom_call_target="tpu_custom_call" | custom-call | flops 60397977600 | bytes 60000000 | tf_op jit(solution)/shard_map/feed_sum/pallas_call | solution.py:618
  195.8 0.9 copy.31.scale
  196.7 19.1 %middle_step.1 = (bf16[3,256,1280]{2,1,0:T(8,128)(2,1)}, bf16[3,256,1280]{2,1,0:T(8,128)(2,1)}, bf16[3,256,320]{2,1,0:T(8,128)(2,1)}, bf16[3,256,320]{2,1,0:T(8,...) custom-call(f32[3,256,1280]{2,1,0:T(8,128)} %get-tuple-element.41.mi, ...), custom_call_target="tpu_custom_call" | custom-call | flops 5033164800 | bytes 30000000 | tf_op jit(solution)/shard_map/middle_step/pallas_call | solution.py:948
  215.9 173.7 %attend_sum.1 = (f32[3,256,1280]{2,1,0:T(8,128)}, bf16[4,40,960]{2,1,0:T(8,128)(2,1)}, bf16[2,3,40,512]{3,2,1,0:T(8,128)(2,1)}, bf16[2,2,40,512]{3,2,1,0:T(8,128...) custom-call(s32[3,8]{1,0:T(4,128)} %pad_add_fusion.lens, ...), custom_call_target="tpu_custom_call" | custom-call | flops 80000000000 | bytes 60000000 | tf_op jit(solution)/shard_map/attend_sum/pallas_call | solution.py:1413
  389.6 1.0 multiply_reduce_fusion
  390.6 0.0 copy-start.6
  390.6 0.6 multiply_subtract_fusion
  391.2 0.9 fusion.5
  392.1 0.9 slice.99
  393.1 0.9 slice.101
  394.0 0.1 maximum_bitcast_fusion
  394.1 0.1 reverse_select_fusion
  394.2 0.9 maximum_convert_fusion
  395.2 0.7 maximum_convert_fusion.1
  395.9 0.1 bitcast_convert_fusion
  396.0 0.1 fusion.6
  396.0 0.1 fusion.7
  396.1 0.1 fusion.8
  396.2 0.1 fusion.9
  396.3 0.8 concatenate.29
  397.1 0.8 concatenate.28
  397.9 0.8 concatenate.27
  398.6 0.9 slice_reduce_fusion.1
  399.5 1.3 dynamic-slice_divide_fusion
  400.9 0.9 convert_element_type.59
  401.8 0.6 fusion.2
  402.4 0.6 fusion.3
  403.0 0.6 fusion.1
  403.6 4.3 %copy.38 = f32[3,256,1280]{2,1,0:T(8,128)} copy(f32[3,256,1280]{2,1,0:T(8,128)} %get-tuple-element.124) | data formatting | bytes 7864320
  (31 shorter events, 0.2 us)
Async XLA Ops:
  2.8 1.9 copy-start.4
  9.9 2.7 copy-start.9
  9.9 2.7 copy-start.8
  9.9 2.7 copy-start.7
  9.9 2.7 copy-start.10
  12.5 81.7 %copy-start.5 = (f32[1,1280]{1,0:T(1,128)}, f32[1,1280]{1,0:T(1,128)S(1)}, u32[]{:S(2)}) copy-start(f32[1,1280]{1,0:T(1,128)S(1)} %stack.21.gain) | copy-start | bytes 15364
  13.3 81.1 %copy-start.11 = (f32[4]{0:T(128)S(1)}, f32[4]{0:T(128)}, u32[]{:S(2)}) copy-start(f32[4]{0:T(128)} %param.19) | copy-start | bytes 52
  13.3 81.1 %copy-start.12 = (s32[3]{0:T(128)S(1)}, s32[3]{0:T(128)}, u32[]{:S(2)}) copy-start(s32[3]{0:T(128)} %param.18) | copy-start | bytes 40
  13.3 81.4 %copy-start = (bf16[3,256,1280]{2,1,0:T(8,128)(2,1)S(1)}, bf16[3,256,1280]{2,1,0:T(8,128)(2,1)}, u32[]{:S(2)}) copy-start(bf16[3,256,1280]{2,1,0:T(8,128)(2,1)} %cotangent.1) | copy-start | bytes 5898244
  389.6 5.6 %copy-start.3 = (bf16[2,1,40,640]{3,2,1,0:T(8,128)(2,1)S(1)}, bf16[2,1,40,640]{3,2,1,0:T(8,128)(2,1)}, u32[]{:S(2)}) copy-start(bf16[2,1,40,640]{3,2,1,0:T(8,128)(2,1)} %get-tuple-element.63) | copy-start | bytes 307204
  389.6 6.3 %copy-start.2 = (bf16[4,40,960]{2,1,0:T(8,128)(2,1)S(1)}, bf16[4,40,960]{2,1,0:T(8,128)(2,1)}, u32[]{:S(2)}) copy-start(bf16[4,40,960]{2,1,0:T(8,128)(2,1)} %get-tuple-element.62) | copy-start | bytes 921604
  390.6 5.4 %copy-start.6 = (f32[1280]{0:T(1024)}, f32[1280]{0:T(1024)S(1)}, u32[]{:S(2)}) copy-start(f32[1280]{0:T(1024)S(1)} %get-tuple-element.135) | copy-start | bytes 15364
  394.1 6.7 %copy-start.1 = (bf16[160,1280]{1,0:T(8,128)(2,1)S(1)}, bf16[160,1280]{1,0:T(8,128)(2,1)}, u32[]{:S(2)}) copy-start(bf16[160,1280]{1,0:T(8,128)(2,1)} %get-tuple-element.67) | copy-start | bytes 1228804
